TPU v7x, 512 devices: a whole 4x4x16 slice. The times are simulated.
512 devices in a mesh: seq: 32 (over y, z_hi, core), ch: 16 (over x, z_lo).
Axes of the slice: x: 4, y: 4, z: 16 (z_hi: 4, z_lo: 4; z = z_hi * 4 + z_lo), core: 2. Of those that a mesh axis runs over, the one named last changes fastest.
Arguments:
- tokens: bfloat16 [4096, 8192], P('seq', 'ch'), may hold values from -6 to 6
- gate_weight: bfloat16 [8192, 4096], P('seq', 'ch'), may hold values from -0.0625 to 0.0625
- value_weight: bfloat16 [8192, 4096], P('seq', 'ch'), may hold values from -0.0625 to 0.0625
- out_weight: bfloat16 [4096, 8192], P('ch'), may hold values from -0.125 to 0.125
- filter_spectrum: float32 [2, 4096, 4096], P(None, 'seq', 'ch'), may hold values from -6 to 6
Outputs:
- mixed: bfloat16 [4096, 8192], P('seq', 'ch')
All inputs are finite; a program needn't handle non-finite values.
Results may differ from a plain program's by a relative error of at most 0.005.
Values may be sent and summed in bfloat16 or wider, within the bound.
No kernel may reach another device: no remote copies, remote signals or barrier semaphores. Data moves between devices by JAX's collectives and lax.ppermute only.
A program may use at most 64 MiB of HBM per device.

v0:
```python
import math

import jax
import jax.numpy as jnp
from jax import lax
from jax.sharding import PartitionSpec as P


def partner(block, axis, apart):
    count = lax.axis_size(axis)
    route = []
    for low in range(count):
        high = low | 1 << apart
        if high != low and high < count:
            route += [(low, high), (high, low)]
    return lax.ppermute(block, axis, route)


def reverse_bits(count):
    total_bits = count.bit_length() - 1
    positions = jnp.arange(count, dtype=jnp.int32)
    reversed_codes = jnp.zeros((count,), jnp.int32)
    for bit_level in range(total_bits):
        reversed_codes = reversed_codes | (positions >> bit_level & 1) << total_bits - 1 - bit_level
    return reversed_codes


def phase_table(row_codes, col_codes, modulus, direction):
    product = row_codes[:, None] * col_codes[None, :] % modulus
    angle = direction * 2.0 * math.pi * product.astype(jnp.float32) / modulus
    return (jnp.cos(angle), jnp.sin(angle))


def matmul_high(left, right):
    return jnp.dot(left, right, precision=lax.Precision.HIGHEST, preferred_element_type=jnp.float32)


def add_rows(whole, piece):
    return jnp.dot(whole, piece, preferred_element_type=jnp.float32)


def local(tokens, gate_weight, value_weight, out_weight, filter_spectrum):
    whole = lax.all_gather(tokens, "ch", axis=1, tiled=True)

    def add_one(piece):
        return add_rows(whole, piece)

    gate = add_one(lax.all_gather(gate_weight, "seq", axis=0, tiled=True))
    value = add_one(lax.all_gather(value_weight, "seq", axis=0, tiled=True))
    seq_count = lax.axis_size("seq")
    seq_bits = seq_count.bit_length() - 1
    seq_rank = lax.axis_index("seq")
    block_rows = value.shape[0]
    total_len = block_rows * seq_count
    local_codes = jnp.arange(block_rows, dtype=jnp.int32)
    local_pos = local_codes[:, None]
    fwd_real, fwd_imag = phase_table(reverse_bits(block_rows), local_codes, block_rows, -1.0)
    real_part = value
    imag_part = jnp.zeros_like(value)
    for bit_level in range(seq_bits - 1, -1, -1):
        other_real, other_imag = partner((real_part, imag_part), "seq", bit_level)
        upper = seq_rank >> bit_level & 1 == 1
        span = block_rows * (1 << bit_level)
        offset = seq_rank % (1 << bit_level) * block_rows + local_pos
        angle = -2.0 * math.pi * offset.astype(jnp.float32) / (2 * span)
        cosine = jnp.cos(angle)
        sine = jnp.sin(angle)
        diff_real = other_real - real_part
        diff_imag = other_imag - imag_part
        turned_real = diff_real * cosine - diff_imag * sine
        turned_imag = diff_real * sine + diff_imag * cosine
        real_part = jnp.where(upper, turned_real, real_part + other_real)
        imag_part = jnp.where(upper, turned_imag, imag_part + other_imag)
    spec_real = matmul_high(fwd_real, real_part) - matmul_high(fwd_imag, imag_part)
    spec_imag = matmul_high(fwd_real, imag_part) + matmul_high(fwd_imag, real_part)
    resp_real = filter_spectrum[0]
    resp_imag = filter_spectrum[1]
    prod_real = spec_real * resp_real - spec_imag * resp_imag
    prod_imag = spec_real * resp_imag + spec_imag * resp_real
    back_real = jnp.transpose(fwd_real)
    back_imag = -jnp.transpose(fwd_imag)
    real_part = matmul_high(back_real, prod_real) - matmul_high(back_imag, prod_imag)
    imag_part = matmul_high(back_real, prod_imag) + matmul_high(back_imag, prod_real)
    for bit_level in range(seq_bits):
        upper = seq_rank >> bit_level & 1 == 1
        span = block_rows * (1 << bit_level)
        offset = seq_rank % (1 << bit_level) * block_rows + local_pos
        angle = 2.0 * math.pi * offset.astype(jnp.float32) / (2 * span)
        cosine = jnp.cos(angle)
        sine = jnp.sin(angle)
        turned_real = real_part * cosine - imag_part * sine
        turned_imag = real_part * sine + imag_part * cosine
        send_real = jnp.where(upper, turned_real, real_part)
        send_imag = jnp.where(upper, turned_imag, imag_part)
        other_real, other_imag = partner((send_real, send_imag), "seq", bit_level)
        real_part = jnp.where(upper, other_real - turned_real, real_part + other_real)
        imag_part = jnp.where(upper, other_imag - turned_imag, imag_part + other_imag)
    conv = real_part / total_len
    hidden = (jax.nn.silu(gate) * conv).astype(jnp.bfloat16)
    partial_sum = jnp.dot(hidden, out_weight, preferred_element_type=jnp.float32)
    return lax.psum_scatter(partial_sum, "ch", scatter_dimension=1, tiled=True).astype(jnp.bfloat16)


def solution(mesh):
    return jax.shard_map(
        local,
        mesh=mesh,
        in_specs=(
            P("seq", "ch"),
            P("seq", "ch"),
            P("seq", "ch"),
            P("ch", None),
            P(None, "seq", "ch"),
        ),
        out_specs=P("seq", "ch"),
        check_vma=False,
    )
```

profile of v0, /device:TPU:1, one launch (start us, length us, event | category | flops | bytes accessed | tf_op | source)
XLA Modules:
  0.0 524.2 jit_solution(13221064942445483509)
XLA Ops:
  6.5 0.7 all-gather.4.cloned.1.call-update
  7.3 0.7 all-gather.8.cloned.1.call-update
  8.1 0.7 all-gather.6.cloned.1.call-update
  8.8 5.8 %collective-permute-start.1 = (f32[128,256]{1,0:T(8,128)S(1)}, f32[128,256]{1,0:T(8,128)S(1)}, u32[]{:S(2)}, u32[]{:S(2)}) collective-permute-start(f32[128,256]{1,0:T(8,128)S(1)} %broadcast_in_dim.2), channel_id=1, source_target_pairs={{0,256},{256,0},{16,272},{272,16},{32,288},{288,32},{48,304},{304,... | collective-permute-start | bytes 393224 | tf_op jit(solution)/shard_map/ppermute | solution.py:16
  14.6 83.2 %all-gather.4.cloned.1.call-done = bf16[128,8192]{1,0:T(8,128)(2,1)} async-done(((bf16[128,512]{1,0:T(8,128)(2,1)}), bf16[128,8192]{1,0:T(8,128)(2,1)}) %all-gather.4.cloned.1.call-update) | async-done | bytes 2097168 | tf_op jit(solution)/shard_map/all_gather | solution.py:43
  97.8 107.8 %all-gather.8.cloned.1.call-done = bf16[8192,256]{1,0:T(8,128)(2,1)} async-done(((bf16[256,256]{1,0:T(8,128)(2,1)}), bf16[8192,256]{1,0:T(8,128)(2,1)}) %all-gather.8.cloned.1.call-update) | async-done | bytes 4194320 | tf_op jit(solution)/shard_map/all_gather | solution.py:49
  205.6 3.5 fusion.118
  209.2 3.8 collective-permute-start
  213.0 4.4 collective-permute-done
  217.4 0.1 add_select_fusion.15
  217.5 2.0 collective-permute-start.3
  219.6 3.3 collective-permute-start.2
  222.9 0.4 collective-permute-done.3
  223.3 4.1 collective-permute-done.2
  227.3 0.1 add_select_fusion.13
  227.5 6.5 %collective-permute-start.5 = (f32[128,256]{1,0:T(8,128)S(1)}, f32[128,256]{1,0:T(8,128)S(1)}, u32[]{:S(2)}, u32[]{:S(2)}) collective-permute-start(f32[128,256]{1,0:T(8,128)S(1)} %get-tuple-element.20), channel_id=1, source_target_pairs={{0,64},{64,0},{16,80},{80,16},{32,96},{96,32},{48,112},{112,48},{1... | collective-permute-start | bytes 393224 | tf_op jit(solution)/shard_map/ppermute | solution.py:16
  233.9 7.5 %collective-permute-start.4 = (f32[128,256]{1,0:T(8,128)S(1)}, f32[128,256]{1,0:T(8,128)S(1)}, u32[]{:S(2)}, u32[]{:S(2)}) collective-permute-start(f32[128,256]{1,0:T(8,128)S(1)} %get-tuple-element.21), channel_id=1, source_target_pairs={{0,64},{64,0},{16,80},{80,16},{32,96},{96,32},{48,112},{112,48},{1... | collective-permute-start | bytes 393224 | tf_op jit(solution)/shard_map/ppermute | solution.py:16
  241.5 12.6 %collective-permute-done.5 = f32[128,256]{1,0:T(8,128)S(1)} collective-permute-done((f32[128,256]{1,0:T(8,128)S(1)}, f32[128,256]{1,0:T(8,128)S(1)}, u32[]{:S(2)}, u32[]{:S(2)}) %collective-permute-start.5) | collective-permute-done | bytes 131104 | tf_op jit(solution)/shard_map/ppermute | solution.py:16
  254.1 4.6 collective-permute-done.4
  258.7 0.1 add_select_fusion.11
  258.8 13.4 %collective-permute-start.7 = (f32[128,256]{1,0:T(8,128)S(1)}, f32[128,256]{1,0:T(8,128)S(1)}, u32[]{:S(2)}, u32[]{:S(2)}) collective-permute-start(f32[128,256]{1,0:T(8,128)S(1)} %get-tuple-element.18), channel_id=1, source_target_pairs={{0,32},{32,0},{16,48},{48,16},{64,96},{96,64},{80,112},{112,80},{1... | collective-permute-start | bytes 393224 | tf_op jit(solution)/shard_map/ppermute | solution.py:16
  272.2 1.9 collective-permute-start.6
  274.3 24.4 %collective-permute-done.7 = f32[128,256]{1,0:T(8,128)S(1)} collective-permute-done((f32[128,256]{1,0:T(8,128)S(1)}, f32[128,256]{1,0:T(8,128)S(1)}, u32[]{:S(2)}, u32[]{:S(2)}) %collective-permute-start.7) | collective-permute-done | bytes 131104 | tf_op jit(solution)/shard_map/ppermute | solution.py:16
  298.6 25.6 %collective-permute-done.6 = f32[128,256]{1,0:T(8,128)S(1)} collective-permute-done((f32[128,256]{1,0:T(8,128)S(1)}, f32[128,256]{1,0:T(8,128)S(1)}, u32[]{:S(2)}, u32[]{:S(2)}) %collective-permute-start.6) | collective-permute-done | bytes 131104 | tf_op jit(solution)/shard_map/ppermute | solution.py:16
  324.3 0.1 add_select_fusion.9
  324.4 2.2 collective-permute-start.9
  326.6 2.1 collective-permute-start.8
  328.8 1.0 collective-permute-done.8
  329.8 0.1 add_select_fusion.7
  329.9 0.6 fusion.40
  330.5 0.6 fusion.38
  331.1 0.6 convolution_add_fusion.1
  331.6 0.6 fusion.1
  332.2 0.6 fusion.32
  332.8 0.6 fusion.34
  333.4 0.5 convolution_subtract_fusion
  334.0 0.5 fusion.7
  334.5 2.1 collective-permute-start.11
  336.6 2.2 collective-permute-start.10
  338.9 1.0 collective-permute-done.10
  339.9 0.1 fusion.8
  340.0 0.1 fusion.5
  340.1 1.9 collective-permute-start.13
  342.1 7.3 %collective-permute-start.12 = (f32[128,256]{1,0:T(8,128)S(1)}, f32[128,256]{1,0:T(8,128)S(1)}, u32[]{:S(2)}, u32[]{:S(2)}) collective-permute-start(f32[128,256]{1,0:T(8,128)S(1)} %get-tuple-element.11), channel_id=1, source_target_pairs={{0,32},{32,0},{16,48},{48,16},{64,96},{96,64},{80,112},{112,80},{1... | collective-permute-start | bytes 393224 | tf_op jit(solution)/shard_map/ppermute | solution.py:16
  349.4 4.2 collective-permute-done.13
  353.5 2.8 collective-permute-done.12
  356.4 0.1 fusion.6
  356.5 0.1 fusion.3
  356.6 7.4 %collective-permute-start.15 = (f32[128,256]{1,0:T(8,128)S(1)}, f32[128,256]{1,0:T(8,128)S(1)}, u32[]{:S(2)}, u32[]{:S(2)}) collective-permute-start(f32[128,256]{1,0:T(8,128)S(1)} %fusion.3), channel_id=1, source_target_pairs={{0,64},{64,0},{16,80},{80,16},{32,96},{96,32},{48,112},{112,48},{1... | collective-permute-start | bytes 393224 | tf_op jit(solution)/shard_map/ppermute | solution.py:16
  364.0 6.6 %collective-permute-start.14 = (f32[128,256]{1,0:T(8,128)S(1)}, f32[128,256]{1,0:T(8,128)S(1)}, u32[]{:S(2)}, u32[]{:S(2)}) collective-permute-start(f32[128,256]{1,0:T(8,128)S(1)} %get-tuple-element.8), channel_id=1, source_target_pairs={{0,64},{64,0},{16,80},{80,16},{32,96},{96,32},{48,112},{112,48},{1... | collective-permute-start | bytes 393224 | tf_op jit(solution)/shard_map/ppermute | solution.py:16
  370.7 1.8 collective-permute-done.15
  372.4 8.2 %collective-permute-done.14 = f32[128,256]{1,0:T(8,128)S(1)} collective-permute-done((f32[128,256]{1,0:T(8,128)S(1)}, f32[128,256]{1,0:T(8,128)S(1)}, u32[]{:S(2)}, u32[]{:S(2)}) %collective-permute-start.14) | collective-permute-done | bytes 131104 | tf_op jit(solution)/shard_map/ppermute | solution.py:16
  380.6 0.1 fusion.4
  380.7 0.1 fusion.2
  380.9 7.3 %collective-permute-start.17 = (f32[128,256]{1,0:T(8,128)S(1)}, f32[128,256]{1,0:T(8,128)S(1)}, u32[]{:S(2)}, u32[]{:S(2)}) collective-permute-start(f32[128,256]{1,0:T(8,128)S(1)} %fusion.2), channel_id=1, source_target_pairs={{0,128},{128,0},{16,144},{144,16},{32,160},{160,32},{48,176},{176,... | collective-permute-start | bytes 393224 | tf_op jit(solution)/shard_map/ppermute | solution.py:16
  388.1 1.9 collective-permute-start.16
  390.1 0.4 collective-permute-done.17
  390.5 4.4 collective-permute-done.16
  394.9 0.1 broadcast_select_fusion
  395.0 7.6 %collective-permute-start.18 = (f32[128,256]{1,0:T(8,128)S(1)}, f32[128,256]{1,0:T(8,128)S(1)}, u32[]{:S(2)}, u32[]{:S(2)}) collective-permute-start(f32[128,256]{1,0:T(8,128)S(1)} %broadcast_select_fusion), channel_id=1, source_target_pairs={{0,256},{256,0},{16,272},{272,16},{32,288},{288,32},{48,304},{304,... | collective-permute-start | bytes 393224 | tf_op jit(solution)/shard_map/ppermute | solution.py:16
  402.7 2.3 collective-permute-done.18
  405.0 7.9 %fusion.18 = f32[128,8192]{1,0:T(8,128)} fusion(bf16[256,8192]{1,0:T(8,128)(2,1)} %param.8, f32[128,256]{1,0:T(8,128)S(1)} %collective-permute-done.18, pred[]{:T(512)S(6)} %eq.33, f32[128,256]{1,0:T(8,128)S(1)} %get-tuple-element.7, f32[128,256]{1,0:T(8,128)S(1)} %collective-permute-done.17, f32[128,256]{1,0:T(8,128)S(1)} %get-tuple-element.6, ...), kind=kOutput, calls=%fused_computation.59 | convolution fusion | flops 1074561024 | bytes 15337474 | tf_op jit(solution)/shard_map/dot_general | solution.py:100
  412.9 103.1 %reduce-scatter.2.cloned.1.call-done = f32[128,512]{1,0:T(8,128)} async-done(((f32[128,8192]{1,0:T(8,128)}), f32[128,512]{1,0:T(8,128)}) %reduce-scatter.2.cloned.1.call-update) | async-done | bytes 262160 | tf_op jit(solution)/shard_map/reduce_scatter | solution.py:101
  516.1 1.6 convert_element_type.136
  (25 shorter events, 0.6 us)
Async XLA Ops:
  6.5 91.3 %all-gather.4.cloned.1.call-start = ((), (), s32[]{:S(2)}) async-start(), calls=%async_computation.1 | async-start | bytes 2228224 | tf_op jit(solution)/shard_map/all_gather | solution.py:43
  7.3 198.4 %all-gather.8.cloned.1.call-start = ((), (), s32[]{:S(2)}) async-start(), calls=%async_computation.3 | async-start | bytes 4325376 | tf_op jit(solution)/shard_map/all_gather | solution.py:49
  8.0 394.7 %all-gather.6.cloned.1.call-start = ((), (), s32[]{:S(2)}) async-start(), calls=%async_computation.2 | async-start | bytes 4325376 | tf_op jit(solution)/shard_map/all_gather | solution.py:48
  8.7 507.3 %reduce-scatter.2.cloned.1.call-start = ((), (), s32[]{:S(2)}) async-start(), calls=%async_computation.4 | async-start | bytes 4456448 | tf_op jit(solution)/shard_map/reduce_scatter | solution.py:101
  8.8 322.8 %copy-start.1 = (f32[2,128,256]{2,1,0:T(8,128)S(1)}, f32[2,128,256]{2,1,0:T(8,128)}, u32[]{:S(2)}) copy-start(f32[2,128,256]{2,1,0:T(8,128)} %param.9) | copy-start | bytes 786436
  8.8 204.2 %collective-permute-start.1 = (f32[128,256]{1,0:T(8,128)S(1)}, f32[128,256]{1,0:T(8,128)S(1)}, u32[]{:S(2)}, u32[]{:S(2)}) collective-permute-start(f32[128,256]{1,0:T(8,128)S(1)} %broadcast_in_dim.2), channel_id=1, source_target_pairs={{0,256},{256,0},{16,272},{272,16},{32,288},{288,32},{48,304},{304,... | collective-permute-start | bytes 393224 | tf_op jit(solution)/shard_map/ppermute | solution.py:16
  209.2 8.3 %collective-permute-start = (f32[128,256]{1,0:T(8,128)S(1)}, f32[128,256]{1,0:T(8,128)S(1)}, u32[]{:S(2)}, u32[]{:S(2)}) collective-permute-start(f32[128,256]{1,0:T(8,128)S(1)} %fusion.118), channel_id=1, source_target_pairs={{0,256},{256,0},{16,272},{272,16},{32,288},{288,32},{48,304},{304,... | collective-permute-start | bytes 393224 | tf_op jit(solution)/shard_map/ppermute | solution.py:16
  217.5 5.7 %collective-permute-start.3 = (f32[128,256]{1,0:T(8,128)S(1)}, f32[128,256]{1,0:T(8,128)S(1)}, u32[]{:S(2)}, u32[]{:S(2)}) collective-permute-start(f32[128,256]{1,0:T(8,128)S(1)} %get-tuple-element.24), channel_id=1, source_target_pairs={{0,128},{128,0},{16,144},{144,16},{32,160},{160,32},{48,176},{176,... | collective-permute-start | bytes 393224 | tf_op jit(solution)/shard_map/ppermute | solution.py:16
  219.6 7.8 %collective-permute-start.2 = (f32[128,256]{1,0:T(8,128)S(1)}, f32[128,256]{1,0:T(8,128)S(1)}, u32[]{:S(2)}, u32[]{:S(2)}) collective-permute-start(f32[128,256]{1,0:T(8,128)S(1)} %get-tuple-element.25), channel_id=1, source_target_pairs={{0,128},{128,0},{16,144},{144,16},{32,160},{160,32},{48,176},{176,... | collective-permute-start | bytes 393224 | tf_op jit(solution)/shard_map/ppermute | solution.py:16
  227.5 26.6 %collective-permute-start.5 = (f32[128,256]{1,0:T(8,128)S(1)}, f32[128,256]{1,0:T(8,128)S(1)}, u32[]{:S(2)}, u32[]{:S(2)}) collective-permute-start(f32[128,256]{1,0:T(8,128)S(1)} %get-tuple-element.20), channel_id=1, source_target_pairs={{0,64},{64,0},{16,80},{80,16},{32,96},{96,32},{48,112},{112,48},{1... | collective-permute-start | bytes 393224 | tf_op jit(solution)/shard_map/ppermute | solution.py:16
  233.9 24.8 %collective-permute-start.4 = (f32[128,256]{1,0:T(8,128)S(1)}, f32[128,256]{1,0:T(8,128)S(1)}, u32[]{:S(2)}, u32[]{:S(2)}) collective-permute-start(f32[128,256]{1,0:T(8,128)S(1)} %get-tuple-element.21), channel_id=1, source_target_pairs={{0,64},{64,0},{16,80},{80,16},{32,96},{96,32},{48,112},{112,48},{1... | collective-permute-start | bytes 393224 | tf_op jit(solution)/shard_map/ppermute | solution.py:16
  258.8 39.8 %collective-permute-start.7 = (f32[128,256]{1,0:T(8,128)S(1)}, f32[128,256]{1,0:T(8,128)S(1)}, u32[]{:S(2)}, u32[]{:S(2)}) collective-permute-start(f32[128,256]{1,0:T(8,128)S(1)} %get-tuple-element.18), channel_id=1, source_target_pairs={{0,32},{32,0},{16,48},{48,16},{64,96},{96,64},{80,112},{112,80},{1... | collective-permute-start | bytes 393224 | tf_op jit(solution)/shard_map/ppermute | solution.py:16
  272.2 52.0 %collective-permute-start.6 = (f32[128,256]{1,0:T(8,128)S(1)}, f32[128,256]{1,0:T(8,128)S(1)}, u32[]{:S(2)}, u32[]{:S(2)}) collective-permute-start(f32[128,256]{1,0:T(8,128)S(1)} %get-tuple-element.19), channel_id=1, source_target_pairs={{0,32},{32,0},{16,48},{48,16},{64,96},{96,64},{80,112},{112,80},{1... | collective-permute-start | bytes 393224 | tf_op jit(solution)/shard_map/ppermute | solution.py:16
  324.4 4.4 collective-permute-start.9
  326.6 3.2 collective-permute-start.8
  329.9 75.1 %copy-start = (bf16[128,8192]{1,0:T(8,128)(2,1)S(1)}, bf16[128,8192]{1,0:T(8,128)(2,1)}, u32[]{:S(2)}) copy-start(bf16[128,8192]{1,0:T(8,128)(2,1)} %all-gather.4.cloned.1.call-done) | copy-start | bytes 6291460
  334.5 4.4 collective-permute-start.11
  336.6 3.2 collective-permute-start.10
  340.1 13.4 %collective-permute-start.13 = (f32[128,256]{1,0:T(8,128)S(1)}, f32[128,256]{1,0:T(8,128)S(1)}, u32[]{:S(2)}, u32[]{:S(2)}) collective-permute-start(f32[128,256]{1,0:T(8,128)S(1)} %fusion.5), channel_id=1, source_target_pairs={{0,32},{32,0},{16,48},{48,16},{64,96},{96,64},{80,112},{112,80},{1... | collective-permute-start | bytes 393224 | tf_op jit(solution)/shard_map/ppermute | solution.py:16
  342.1 14.3 %collective-permute-start.12 = (f32[128,256]{1,0:T(8,128)S(1)}, f32[128,256]{1,0:T(8,128)S(1)}, u32[]{:S(2)}, u32[]{:S(2)}) collective-permute-start(f32[128,256]{1,0:T(8,128)S(1)} %get-tuple-element.11), channel_id=1, source_target_pairs={{0,32},{32,0},{16,48},{48,16},{64,96},{96,64},{80,112},{112,80},{1... | collective-permute-start | bytes 393224 | tf_op jit(solution)/shard_map/ppermute | solution.py:16
  356.6 15.8 %collective-permute-start.15 = (f32[128,256]{1,0:T(8,128)S(1)}, f32[128,256]{1,0:T(8,128)S(1)}, u32[]{:S(2)}, u32[]{:S(2)}) collective-permute-start(f32[128,256]{1,0:T(8,128)S(1)} %fusion.3), channel_id=1, source_target_pairs={{0,64},{64,0},{16,80},{80,16},{32,96},{96,32},{48,112},{112,48},{1... | collective-permute-start | bytes 393224 | tf_op jit(solution)/shard_map/ppermute | solution.py:16
  364.0 16.5 %collective-permute-start.14 = (f32[128,256]{1,0:T(8,128)S(1)}, f32[128,256]{1,0:T(8,128)S(1)}, u32[]{:S(2)}, u32[]{:S(2)}) collective-permute-start(f32[128,256]{1,0:T(8,128)S(1)} %get-tuple-element.8), channel_id=1, source_target_pairs={{0,64},{64,0},{16,80},{80,16},{32,96},{96,32},{48,112},{112,48},{1... | collective-permute-start | bytes 393224 | tf_op jit(solution)/shard_map/ppermute | solution.py:16
  380.9 9.6 %collective-permute-start.17 = (f32[128,256]{1,0:T(8,128)S(1)}, f32[128,256]{1,0:T(8,128)S(1)}, u32[]{:S(2)}, u32[]{:S(2)}) collective-permute-start(f32[128,256]{1,0:T(8,128)S(1)} %fusion.2), channel_id=1, source_target_pairs={{0,128},{128,0},{16,144},{144,16},{32,160},{160,32},{48,176},{176,... | collective-permute-start | bytes 393224 | tf_op jit(solution)/shard_map/ppermute | solution.py:16
  388.1 6.7 %collective-permute-start.16 = (f32[128,256]{1,0:T(8,128)S(1)}, f32[128,256]{1,0:T(8,128)S(1)}, u32[]{:S(2)}, u32[]{:S(2)}) collective-permute-start(f32[128,256]{1,0:T(8,128)S(1)} %get-tuple-element.5), channel_id=1, source_target_pairs={{0,128},{128,0},{16,144},{144,16},{32,160},{160,32},{48,176},{176,... | collective-permute-start | bytes 393224 | tf_op jit(solution)/shard_map/ppermute | solution.py:16
  395.0 10.0 %collective-permute-start.18 = (f32[128,256]{1,0:T(8,128)S(1)}, f32[128,256]{1,0:T(8,128)S(1)}, u32[]{:S(2)}, u32[]{:S(2)}) collective-permute-start(f32[128,256]{1,0:T(8,128)S(1)} %broadcast_select_fusion), channel_id=1, source_target_pairs={{0,256},{256,0},{16,272},{272,16},{32,288},{288,32},{48,304},{304,... | collective-permute-start | bytes 393224 | tf_op jit(solution)/shard_map/ppermute | solution.py:16
Sparse Core Ops, SparseCore 0:
  9.4 88.3 all-gather.3
  101.0 104.6 all-gather.7
  208.8 125.2 all-gather.5
  413.0 102.9 reduce-scatter.1
where the time goes:
time: 529 us; the launch traced here: 524 us
  waiting for transfers between devices  398 us (75%)
  starting transfers between devices  92.9 us (18%)
  matrix products  16 us (3%)
  between operations  13.5 us (3%)
    all_gather x1, waiting for transfers between devices, local(): value = add_one(lax.all_gather(value_weight, 'seq', axis=0, tiled=True))  108 us
    reduce_scatter x1, waiting for transfers between devices, local(): lax.psum_scatter(partial_sum, 'ch', scatter_dimension=1, tiled=True)  103 us
    ppermute x19, waiting for transfers between devices, partner(): return lax.ppermute(block, axis, route)  102 us
    ppermute x19, starting transfers between devices, partner(): return lax.ppermute(block, axis, route)  92.8 us
    all_gather x1, waiting for transfers between devices, local(): whole = lax.all_gather(tokens, 'ch', axis=1, tiled=True)  83.2 us
  transfers between devices with their start and end apart: 23, of which 19 were waited for; matrix products, arithmetic and copies ran while one was open for 2% of the time, Pallas kernels for 0%

commit v1 on v0

v1 whole, which is shorter than its diff:
```python
import math

import jax
import jax.numpy as jnp
import numpy as np
from jax import lax
from jax.sharding import Mesh
from jax.sharding import PartitionSpec as P

SEQ = ("y", "zh", "core")
CH = ("x", "zl")
N1, N2 = 32, 128
TOTAL = N1 * N2
GROUP = 8


def reverse(count):
    bits = count.bit_length() - 1
    return np.array([int(format(i, f"0{bits}b")[::-1], 2) for i in range(count)])


def dft_tables():
    n1, n2 = np.arange(N1), np.arange(N2)
    k1, k2 = reverse(N1), reverse(N2)
    outer = np.exp(-2j * np.pi * np.outer(k1, n1) / N1)
    twist = np.exp(-2j * np.pi * np.outer(k1, n2) / TOTAL)
    inner = np.exp(-2j * np.pi * np.outer(n2, k2) / N2)
    return outer, twist, inner


def f32(values):
    return jnp.asarray(np.ascontiguousarray(values), jnp.float32)


def high(left, right):
    return jnp.dot(left, right, precision=lax.Precision.HIGHEST, preferred_element_type=jnp.float32)


def convolve(signal, response):
    outer, twist, inner = dft_tables()
    rows = N1 * GROUP
    eye = np.eye(GROUP)
    spread = np.kron(outer, eye)
    forward = np.concatenate([spread.real, spread.imag])
    tw = np.repeat(twist, GROUP, axis=0)
    tr, ti = f32(tw.real), f32(tw.imag)
    mixed = high(f32(forward), signal.reshape(rows, N2))
    ar, ai = mixed[:rows], mixed[rows:]
    turned = jnp.concatenate([ar * tr - ai * ti, ar * ti + ai * tr])
    both = high(turned, f32(np.concatenate([inner.real, inner.imag], axis=1)))
    sr = both[:rows, :N2] - both[rows:, N2:]
    si = both[:rows, N2:] + both[rows:, :N2]
    rr, ri = response[0].reshape(rows, N2), response[1].reshape(rows, N2)
    prod = jnp.concatenate([sr * rr - si * ri, sr * ri + si * rr])
    back = inner.T
    both = high(prod, f32(np.concatenate([back.real, -back.imag], axis=1)))
    br = both[:rows, :N2] - both[rows:, N2:]
    bi = both[:rows, N2:] + both[rows:, :N2]
    turned = jnp.concatenate([br * tr + bi * ti, bi * tr - br * ti])
    home = np.conj(spread).T / TOTAL
    conv = high(f32(np.concatenate([home.real, -home.imag], axis=1)), turned)
    return conv.reshape(N1, GROUP, N2)


def gather_over(block, axis):
    count = lax.axis_size(axis)
    return lax.all_to_all(jnp.broadcast_to(block, (count,) + block.shape), axis, 0, 0)


def project(weight, tokens):
    weight = weight.reshape(4, 512, 256)
    return jnp.einsum("xkc,xtk->ct", weight, tokens, preferred_element_type=jnp.float32)


def local(tokens, gate_weight, value_weight, out_weight, filter_spectrum):
    value_rows = lax.all_gather(value_weight, ("y", "core"), axis=0, tiled=True)
    gate_rows = lax.all_gather(gate_weight, ("y", "core"), axis=0, tiled=True)
    swap = [(zh * 4 + zl, zl * 4 + zh) for zh in range(4) for zl in range(4)]
    swapped = lax.ppermute(tokens, ("zh", "zl"), swap)
    near = lax.all_gather(swapped, "zl", axis=0, tiled=True)
    whole = gather_over(near, "x")

    value = project(value_rows, whole).astype(jnp.bfloat16)
    resp = jnp.transpose(filter_spectrum, (2, 0, 1)).reshape(256, 256)
    resp_hi = resp.astype(jnp.bfloat16)
    resp_lo = (resp - resp_hi.astype(jnp.float32)).astype(jnp.bfloat16)
    packet = jnp.concatenate([value, resp_hi, resp_lo], axis=1).reshape(N1, GROUP, 1024)
    packet = lax.all_to_all(packet, SEQ, 0, 0)

    gate = project(gate_rows, whole)
    gate = jnp.transpose(gate.reshape(256, 4, 128), (1, 0, 2))
    gate = lax.psum_scatter(gate, "zh", scatter_dimension=0)

    signal = packet[:, :, :512].reshape(4, 4, 2, GROUP, 4, N2).astype(jnp.float32).sum(axis=1)
    signal = jnp.transpose(signal, (0, 3, 1, 2, 4)).reshape(N1, GROUP, N2)
    resp = packet[:, :, 512:768].astype(jnp.float32) + packet[:, :, 768:].astype(jnp.float32)
    resp = jnp.transpose(resp.reshape(N1, GROUP, 2, N2), (2, 0, 1, 3))
    conv = lax.all_to_all(convolve(signal, resp), SEQ, 0, 0).reshape(256, 128)

    hidden = (jax.nn.silu(gate) * conv).astype(jnp.bfloat16)
    parts = jnp.einsum("ct,cxd->xtd", hidden, out_weight.reshape(256, 4, 2048), preferred_element_type=jnp.float32)
    parts = lax.all_to_all(parts.astype(jnp.bfloat16), "x", 0, 0)
    total = parts.astype(jnp.float32).sum(axis=0).astype(jnp.bfloat16)
    total = jnp.transpose(total.reshape(128, 4, 512), (1, 0, 2))
    total = lax.all_to_all(total, "zl", 0, 0)
    return total.astype(jnp.float32).sum(axis=0).astype(jnp.bfloat16)


def solution(mesh):
    fine = Mesh(mesh.devices.reshape(4, 4, 2, 4, 4), SEQ + CH)
    return jax.shard_map(
        local,
        mesh=fine,
        in_specs=(P(SEQ, CH), P(SEQ, CH), P(SEQ, CH), P(CH, None), P(None, SEQ, CH)),
        out_specs=P(SEQ, CH),
        check_vma=False,
    )
```

time: 529 us -> 213 us (0.40)
  waiting for transfers between devices: 398 us -> 67.1 us
  blocking collectives: 0 us -> 78.6 us
  starting transfers between devices: 92.9 us -> 38.2 us
  matrix products: 16 us -> 10.4 us
    all_gather x3 -> x2, waiting for transfers between devices: 191 us -> 0.02 us  [the longest x1 0.02 us: local(): gate_rows = lax.all_gather(gate_weight, ('y', 'core'), axis=0, tiled=True)]
    ppermute x19 -> x1, waiting for transfers between devices: 102 us -> 0.01 us  [local(): swapped = lax.ppermute(tokens, ('zh', 'zl'), swap)]
    reduce_scatter x1, waiting for transfers between devices: 103 us -> 1.5 us  [local(): gate = lax.psum_scatter(gate, 'zh', scatter_dimension=0)]
    ppermute x19 -> x1, starting transfers between devices: 92.8 us -> 1.56 us  [local(): swapped = lax.ppermute(tokens, ('zh', 'zl'), swap)]
    all_to_all x0 -> x3, waiting for transfers between devices: none -> 64.1 us  [the longest x1 29.4 us: local(): packet = lax.all_to_all(packet, SEQ, 0, 0)]
    all_to_all x0 -> x2, blocking collectives: none -> 47.1 us  [the longest x1 28.6 us: local(): parts = lax.all_to_all(parts.astype(jnp.bfloat16), 'x', 0, 0)]
    all_to_all x0 -> x3, starting transfers between devices: none -> 36.6 us  [the longest x1 20.4 us: local(): packet = lax.all_to_all(packet, SEQ, 0, 0)]
    all_gather x0 -> x1, blocking collectives: none -> 31.5 us  [local(): near = lax.all_gather(swapped, 'zl', axis=0, tiled=True)]
  transfers between devices with their start and end apart: 23 -> 7, of which waited for: 19 -> 4; matrix products, arithmetic and copies ran while one was open for 2% -> 5% of each run, Pallas kernels for 0% -> 0%
where the time goes in v1:
time: 213 us
  blocking collectives  78.6 us (37%)
  waiting for transfers between devices  67.1 us (32%)
  starting transfers between devices  38.2 us (18%)
  between operations  13.4 us (6%)
  matrix products  10.4 us (5%)
  local copies, waits for them, and re-layouts  2.97 us (1%)
  other arithmetic  2.19 us (1%)
    all_gather x1, blocking collectives, local(): near = lax.all_gather(swapped, 'zl', axis=0, tiled=True)  31.5 us
    all_to_all x1, waiting for transfers between devices, local(): packet = lax.all_to_all(packet, SEQ, 0, 0)  29.4 us
    all_to_all x1, blocking collectives, local(): parts = lax.all_to_all(parts.astype(jnp.bfloat16), 'x', 0, 0)  28.6 us
    all_to_all x1, waiting for transfers between devices, gather_over(): lax.all_to_all(jnp.broadcast_to(block, (count,) + block.shape), axis, 0, 0)  20.5 us
    all_to_all x1, starting transfers between devices, local(): packet = lax.all_to_all(packet, SEQ, 0, 0)  20.4 us
    all_to_all x1, blocking collectives, local(): total = lax.all_to_all(total, 'zl', 0, 0)  18.5 us
    all_to_all x1, waiting for transfers between devices, local(): conv = lax.all_to_all(convolve(signal, resp), SEQ, 0, 0).reshape(256, 128)  14.2 us
    all_to_all x1, starting transfers between devices, local(): conv = lax.all_to_all(convolve(signal, resp), SEQ, 0, 0).reshape(256, 128)  12 us
  transfers between devices with their start and end apart: 7, of which 4 were waited for; matrix products, arithmetic and copies ran while one was open for 5% of the time, Pallas kernels for 0%

profile of v1, /device:TPU:1, one launch (start us, length us, event | category | flops | bytes accessed | tf_op | source)
XLA Modules:
  0.0 212.8 jit_solution(18401346460444797932)
XLA Ops:
  6.5 0.0 all-gather.5.cloned.1.call-start
  6.5 0.7 all-gather.5.cloned.1.call-update
  7.3 1.6 collective-permute-start
  8.8 0.0 collective-permute-done
  8.8 31.5 %all_gather.10 = bf16[512,512]{1,0:T(8,128)(2,1)S(1)} all-gather(bf16[128,512]{1,0:T(8,128)(2,1)S(1)} %collective-permute-done), channel_id=1, replica_groups=mesh['y'=4,'zh'=4,'core'=2,'x'=4,'zl'=4] {'zl'}, dimensions={0}, use_global_device_ids=true | all-gather | bytes 655360 | tf_op jit(solution)/shard_map/all_gather | solution.py:80
  40.3 1.5 broadcast_in_dim.3
  41.8 0.0 copy-start.5
  41.8 4.1 %all-to-all-start = ((bf16[4,512,512]{2,1,0:T(8,128)(2,1)}), bf16[4,512,512]{2,1,0:T(8,128)(2,1)S(1)}, u32[]{:S(2)}, u32[]{:S(2)}) async-start(bf16[4,512,512]{2,1,0:T(8,128)(2,1)} %broadcast_in_dim.3), calls=%async_computation | async-start | bytes 4194304 | tf_op jit(solution)/shard_map/all_to_all | solution.py:67
  46.0 0.0 all-gather.3.cloned.1.call-start
  46.0 0.7 all-gather.3.cloned.1.call-update
  46.7 0.0 copy-done.5
  46.7 0.1 copy.59
  46.9 20.5 %all-to-all-done = bf16[4,512,512]{2,1,0:T(8,128)(2,1)S(1)} async-done(((bf16[4,512,512]{2,1,0:T(8,128)(2,1)}), bf16[4,512,512]{2,1,0:T(8,128)(2,1)S(1)}, u32[]{:S(2)}, u32[]{:S(2)}) %all-to-all-start) | async-done | bytes 2097184 | tf_op jit(solution)/shard_map/all_to_all | solution.py:67
  67.4 0.0 all-gather.5.cloned.1.call-done
  67.4 2.0 fusion.9
  69.4 0.9 maximum_bitcast_fusion
  70.2 20.4 %all-to-all-start.1 = ((bf16[32,8,1024]{2,1,0:T(8,128)(2,1)}), bf16[32,8,1024]{2,1,0:T(8,128)(2,1)S(1)}, u32[]{:S(2)}, u32[]{:S(2)}) async-start(bf16[32,8,1024]{2,1,0:T(8,128)(2,1)} %maximum_bitcast_fusion), calls=%async_computation.2 | async-start | bytes 1048576 | tf_op jit(solution)/shard_map/all_to_all | solution.py:88
  90.6 0.0 reduce-scatter.2.cloned.1.call-start
  90.7 0.0 all-gather.3.cloned.1.call-done
  90.7 0.0 copy-start.2
  90.7 2.8 %convolution_bitcast_fusion = f32[4,256,128]{2,1,0:T(8,128)} fusion(bf16[4,512,256,1]{2,1,3,0:T(8,128)(2,1)} %bitcast.101, bf16[4,128,512,4]{2,1,0,3:T(8,128)(2,1)S(1)} %bitcast.95), kind=kOutput, calls=%fused_computation.5 | convolution fusion | flops 536870912 | bytes 3670016 | tf_op jit(solution)/shard_map/xkc,xtk->ct/dot_general | solution.py:72
  93.6 0.0 copy-start
  93.6 0.0 copy-start.1
  93.6 0.0 copy-start.7
  93.6 0.0 reduce-scatter.2.cloned.1.call-update
  93.6 29.4 %all-to-all-done.1 = bf16[32,8,1024]{2,1,0:T(8,128)(2,1)S(1)} async-done(((bf16[32,8,1024]{2,1,0:T(8,128)(2,1)}), bf16[32,8,1024]{2,1,0:T(8,128)(2,1)S(1)}, u32[]{:S(2)}, u32[]{:S(2)}) %all-to-all-start.1) | async-done | bytes 524320 | tf_op jit(solution)/shard_map/all_to_all | solution.py:88
  123.1 0.0 copy-done.2
  123.1 0.0 copy-start.6
  123.1 0.6 fusion.36
  123.7 0.0 copy-done
  123.7 0.0 copy-done.1
  123.7 0.0 copy-start.4
  123.8 0.0 copy-done.7
  123.8 0.0 copy-start.3
  123.8 0.6 fusion.11
  124.5 0.0 copy-done.6
  124.5 0.6 fusion.15
  125.0 0.0 copy-done.4
  125.1 0.4 fusion.26
  125.5 0.0 copy-done.3
  125.5 0.4 fusion.10
  125.9 0.8 copy.49
  126.7 12.0 %all-to-all-start.2 = ((f32[32,8,128]{2,1,0:T(8,128)}), f32[32,8,128]{2,1,0:T(8,128)S(1)}, u32[]{:S(2)}, u32[]{:S(2)}) async-start(f32[32,8,128]{2,1,0:T(8,128)} %bitcast.21), calls=%async_computation.3 | async-start | bytes 262144 | tf_op jit(solution)/shard_map/all_to_all | solution.py:98
  138.7 1.5 reduce-scatter.2.cloned.1.call-done
  140.2 14.2 %all-to-all-done.2 = f32[32,8,128]{2,1,0:T(8,128)S(1)} async-done(((f32[32,8,128]{2,1,0:T(8,128)}), f32[32,8,128]{2,1,0:T(8,128)S(1)}, u32[]{:S(2)}, u32[]{:S(2)}) %all-to-all-start.2) | async-done | bytes 131104 | tf_op jit(solution)/shard_map/all_to_all | solution.py:98
  154.4 3.0 %fusion.6 = bf16[4,128,2048]{2,1,0:T(8,128)(2,1)S(1)} fusion(bf16[32,4,8,2048]{3,2,1,0:T(8,128)(2,1)} %bitcast.94, f32[32,8,128]{2,1,0:T(8,128)S(1)} %all-to-all-done.2, f32[1,256,128]{2,1,0:T(8,128)} %reduce-scatter.2.cloned.1.call-done), kind=kOutput, calls=%fused_computation.4 | convolution fusion | flops 538116096 | bytes 6553600 | tf_op jit(solution)/shard_map/ct,cxd->xtd/dot_general | solution.py:101
  157.5 28.6 %all_to_all.25 = bf16[4,128,2048]{2,1,0:T(8,128)(2,1)S(1)} all-to-all(bf16[4,128,2048]{2,1,0:T(8,128)(2,1)S(1)} %fusion.6), channel_id=1, replica_groups=mesh['y'=4,'zh'=4,'core'=2,'x'=4,'zl'=4] {'x'}, dimensions={0} | all-to-all | bytes 4194304 | tf_op jit(solution)/shard_map/all_to_all | solution.py:102
  186.1 0.4 reduce_sum.34
  186.5 0.3 copy.52
  186.8 0.2 copy.53
  187.0 18.5 %all_to_all.26 = bf16[4,128,512]{2,1,0:T(8,128)(2,1)S(1)} all-to-all(bf16[4,128,512]{2,1,0:T(8,128)(2,1)S(1)} %copy.53), channel_id=1, replica_groups=mesh['y'=4,'zh'=4,'core'=2,'x'=4,'zl'=4] {'zl'}, dimensions={0} | all-to-all | bytes 1048576 | tf_op jit(solution)/shard_map/all_to_all | solution.py:105
  205.5 0.7 reduce_sum.35
  (7 shorter events, 0.2 us)
Async XLA Ops:
  6.5 60.8 %all-gather.5.cloned.1.call-start = ((), (), s32[]{:S(2)}) async-start(), calls=%async_computation.8 | async-start | bytes 1179648 | tf_op jit(solution)/shard_map/all_gather | solution.py:76
  7.3 1.6 collective-permute-start
  41.8 4.9 %copy-start.5 = (f32[2,128,256]{2,1,0:T(8,128)S(1)}, f32[2,128,256]{2,1,0:T(8,128)}, u32[]{:S(2)}) copy-start(f32[2,128,256]{2,1,0:T(8,128)} %param.15) | copy-start | bytes 786436
  41.8 25.5 %all-to-all-start = ((bf16[4,512,512]{2,1,0:T(8,128)(2,1)}), bf16[4,512,512]{2,1,0:T(8,128)(2,1)S(1)}, u32[]{:S(2)}, u32[]{:S(2)}) async-start(bf16[4,512,512]{2,1,0:T(8,128)(2,1)} %broadcast_in_dim.3), calls=%async_computation | async-start | bytes 4194304 | tf_op jit(solution)/shard_map/all_to_all | solution.py:67
  46.0 44.7 %all-gather.3.cloned.1.call-start = ((), (), s32[]{:S(2)}) async-start(), calls=%async_computation.6 | async-start | bytes 1179648 | tf_op jit(solution)/shard_map/all_gather | solution.py:77
  70.2 52.8 %all-to-all-start.1 = ((bf16[32,8,1024]{2,1,0:T(8,128)(2,1)}), bf16[32,8,1024]{2,1,0:T(8,128)(2,1)S(1)}, u32[]{:S(2)}, u32[]{:S(2)}) async-start(bf16[32,8,1024]{2,1,0:T(8,128)(2,1)} %maximum_bitcast_fusion), calls=%async_computation.2 | async-start | bytes 1048576 | tf_op jit(solution)/shard_map/all_to_all | solution.py:88
  90.6 49.6 %reduce-scatter.2.cloned.1.call-start = ((), (), s32[]{:S(2)}) async-start(), calls=%async_computation.7 | async-start | bytes 655360 | tf_op jit(solution)/shard_map/reduce_scatter | solution.py:92
  90.7 32.4 %copy-start.2 = (f32[512,256]{1,0:T(8,128)S(1)}, f32[512,256]{1,0:T(8,128)}, u32[]{:S(2)}) copy-start(f32[512,256]{1,0:T(8,128)} %constant.28) | copy-start | bytes 1572868
  93.6 30.2 %copy-start = (f32[256,128]{1,0:T(8,128)S(1)}, f32[256,128]{1,0:T(8,128)}, u32[]{:S(2)}) copy-start(f32[256,128]{1,0:T(8,128)} %constant.20.clone) | copy-start | bytes 393220
  93.6 30.2 %copy-start.1 = (f32[256,128]{1,0:T(8,128)S(1)}, f32[256,128]{1,0:T(8,128)}, u32[]{:S(2)}) copy-start(f32[256,128]{1,0:T(8,128)} %constant.21.clone) | copy-start | bytes 393220
  93.6 30.2 %copy-start.7 = (f32[128,256]{1,0:T(8,128)S(1)}, f32[128,256]{1,0:T(8,128)}, u32[]{:S(2)}) copy-start(f32[128,256]{1,0:T(8,128)} %constant.23.clone) | copy-start | bytes 393220
  123.1 1.4 copy-start.6
  123.7 1.3 copy-start.4
  123.8 1.7 copy-start.3
  126.7 27.7 %all-to-all-start.2 = ((f32[32,8,128]{2,1,0:T(8,128)}), f32[32,8,128]{2,1,0:T(8,128)S(1)}, u32[]{:S(2)}, u32[]{:S(2)}) async-start(f32[32,8,128]{2,1,0:T(8,128)} %bitcast.21), calls=%async_computation.3 | async-start | bytes 262144 | tf_op jit(solution)/shard_map/all_to_all | solution.py:98
Sparse Core Ops, SparseCore 0:
  9.5 36.7 all-gather.4
  49.0 38.3 all-gather.2
  94.3 45.8 reduce-scatter.1

commit v2 on v1

--- a/solution.py
+++ b/solution.py
@@ -67,43 +67,72 @@
     return lax.all_to_all(jnp.broadcast_to(block, (count,) + block.shape), axis, 0, 0)
 
 
+def after(block, earlier):
+    return lax.optimization_barrier((block, earlier))[0]
+
+
 def project(weight, tokens):
     weight = weight.reshape(4, 512, 256)
     return jnp.einsum("xkc,xtk->ct", weight, tokens, preferred_element_type=jnp.float32)
 
 
+def exchange(block, axis, apart):
+    return lax.ppermute(block, axis, [(i, i ^ apart) for i in range(lax.axis_size(axis))])
+
+
+def pick(blocks, index):
+    return lax.dynamic_index_in_dim(blocks, index, 0, keepdims=False)
+
+
 def local(tokens, gate_weight, value_weight, out_weight, filter_spectrum):
-    value_rows = lax.all_gather(value_weight, ("y", "core"), axis=0, tiled=True)
-    gate_rows = lax.all_gather(gate_weight, ("y", "core"), axis=0, tiled=True)
+    column, core, row, high_z = (lax.axis_index(axis) for axis in ("x", "core", "y", "zh"))
     swap = [(zh * 4 + zl, zl * 4 + zh) for zh in range(4) for zl in range(4)]
     swapped = lax.ppermute(tokens, ("zh", "zl"), swap)
-    near = lax.all_gather(swapped, "zl", axis=0, tiled=True)
+    near = gather_over(swapped, "zl").reshape(512, 512)
     whole = gather_over(near, "x")
 
+    def rows_of(weight):
+        mine = jnp.stack([exchange(weight, "y", k) if k else weight for k in range(4)])
+        mine = jnp.stack([pick(mine, row ^ y) for y in range(4)])
+        theirs = exchange(mine, "core", 1)
+        return jnp.stack([jnp.where(core == 0, mine, theirs), jnp.where(core == 0, theirs, mine)], axis=1).reshape(2048, 256)
+
+    value_rows = rows_of(after(value_weight, swapped))
+    gate_rows = rows_of(after(gate_weight, near))
+    whole, value_rows = lax.optimization_barrier((whole, value_rows))
+
     value = project(value_rows, whole).astype(jnp.bfloat16)
-    resp = jnp.transpose(filter_spectrum, (2, 0, 1)).reshape(256, 256)
-    resp_hi = resp.astype(jnp.bfloat16)
-    resp_lo = (resp - resp_hi.astype(jnp.float32)).astype(jnp.bfloat16)
-    packet = jnp.concatenate([value, resp_hi, resp_lo], axis=1).reshape(N1, GROUP, 1024)
+    resp = jnp.transpose(filter_spectrum, (2, 0, 1)).reshape(256, 256).astype(jnp.bfloat16)
+    packet = jnp.concatenate([value, resp], axis=1).reshape(N1, GROUP, 768)
     packet = lax.all_to_all(packet, SEQ, 0, 0)
 
-    gate = project(gate_rows, whole)
-    gate = jnp.transpose(gate.reshape(256, 4, 128), (1, 0, 2))
-    gate = lax.psum_scatter(gate, "zh", scatter_dimension=0)
+    gate = jnp.transpose(project(gate_rows, whole).reshape(256, 4, 128), (1, 0, 2))
+    far = [lax.ppermute(pick(gate, high_z ^ k), ("zh", "core"), [(i, i ^ (2 * k + 1)) for i in range(8)]) for k in (1, 2, 3)]
+    gate = pick(gate, high_z) + exchange(sum(far), "core", 1)
+
+    held = after(out_weight, value)
+
+    def share(k):
+        return jnp.concatenate([lax.dynamic_slice_in_dim(held, ((column ^ k) * 4 + zl) * 512 + core * 256, 256, 1) for zl in range(4)], axis=1)
+
+    shares = [exchange(share(k), "x", k) if k else share(k) for k in range(4)]
 
     signal = packet[:, :, :512].reshape(4, 4, 2, GROUP, 4, N2).astype(jnp.float32).sum(axis=1)
     signal = jnp.transpose(signal, (0, 3, 1, 2, 4)).reshape(N1, GROUP, N2)
-    resp = packet[:, :, 512:768].astype(jnp.float32) + packet[:, :, 768:].astype(jnp.float32)
+    resp = packet[:, :, 512:].astype(jnp.float32)
     resp = jnp.transpose(resp.reshape(N1, GROUP, 2, N2), (2, 0, 1, 3))
     conv = lax.all_to_all(convolve(signal, resp), SEQ, 0, 0).reshape(256, 128)
+    conv, gate, shares = lax.optimization_barrier((conv, gate, shares))
 
     hidden = (jax.nn.silu(gate) * conv).astype(jnp.bfloat16)
-    parts = jnp.einsum("ct,cxd->xtd", hidden, out_weight.reshape(256, 4, 2048), preferred_element_type=jnp.float32)
-    parts = lax.all_to_all(parts.astype(jnp.bfloat16), "x", 0, 0)
-    total = parts.astype(jnp.float32).sum(axis=0).astype(jnp.bfloat16)
-    total = jnp.transpose(total.reshape(128, 4, 512), (1, 0, 2))
-    total = lax.all_to_all(total, "zl", 0, 0)
-    return total.astype(jnp.float32).sum(axis=0).astype(jnp.bfloat16)
+    hidden = lax.all_to_all(jnp.broadcast_to(hidden, (8, 256, 128)), ("x", "core"), 0, 0).reshape(4, 2, 256, 128)
+    total = 0.0
+    for k in range(4):
+        total = total + jnp.einsum("ect,cd->etd", pick(hidden, column ^ k), shares[k], preferred_element_type=jnp.float32)
+    total = jnp.transpose(total.astype(jnp.bfloat16).reshape(2, 128, 4, 256), (2, 0, 1, 3)).reshape(8, 128, 256)
+    total = lax.all_to_all(total, ("zl", "core"), 0, 0).reshape(4, 2, 128, 256)
+    total = total.astype(jnp.float32).sum(axis=0)
+    return jnp.concatenate([total[0], total[1]], axis=1).astype(jnp.bfloat16)
 
 
 def solution(mesh):

time: 213 us -> 194 us (0.911)
  starting transfers between devices: 38.2 us -> 118 us
  blocking collectives: 78.6 us -> 17.8 us
  waiting for transfers between devices: 67.1 us -> 26.4 us
  between operations: 13.4 us -> 0.77 us
  other arithmetic: 2.19 us -> 10.9 us
  local copies, waits for them, and re-layouts: 2.97 us -> 7.85 us
    ppermute x0 -> x15, starting transfers between devices: none -> 53.3 us  [the longest x12 36.8 us: exchange(): lax.ppermute(block, axis, [(i, i ^ apart) for i in range(lax.axis_size(ax...]
    all_gather x1 -> x0, blocking collectives: 31.5 us -> none  [local(): near = lax.all_gather(swapped, 'zl', axis=0, tiled=True)]
    all_to_all x1, waiting for transfers between devices: 29.4 us -> 0.01 us  [local(): packet = lax.all_to_all(packet, SEQ, 0, 0)]
    all_to_all x2 -> x1, blocking collectives: 47.1 us -> 17.8 us  [local(): total = lax.all_to_all(total, ('zl', 'core'), 0, 0).reshape(4, 2, 128, 256)]
    all_to_all x1 -> x2, starting transfers between devices: 4.14 us -> 26.9 us  [gather_over(): lax.all_to_all(jnp.broadcast_to(block, (count,) + block.shape), axis, 0, 0)]
    all_to_all x1 -> x2, waiting for transfers between devices: 20.5 us -> 5.1 us  [gather_over(): lax.all_to_all(jnp.broadcast_to(block, (count,) + block.shape), axis, 0, 0)]
    all_to_all x1, waiting for transfers between devices: 14.2 us -> 0.01 us  [local(): conv = lax.all_to_all(convolve(signal, resp), SEQ, 0, 0).reshape(256, 128)]
    ppermute x0 -> x15, waiting for transfers between devices: none -> 11.8 us  [the longest x12 11.8 us: exchange(): lax.ppermute(block, axis, [(i, i ^ apart) for i in range(lax.axis_size(ax...]
  transfers between devices with their start and end apart: 7 -> 21, of which waited for: 4 -> 7; matrix products, arithmetic and copies ran while one was open for 5% -> 13% of each run, Pallas kernels for 0% -> 0%
where the time goes in v2:
time: 194 us; the launch traced here: 192 us
  starting transfers between devices  118 us (61%)
  waiting for transfers between devices  26.4 us (14%)
  blocking collectives  17.8 us (9%)
  matrix products  11 us (6%)
  other arithmetic  10.9 us (6%)
  local copies, waits for them, and re-layouts  7.85 us (4%)
    ppermute x12, starting transfers between devices, exchange(): lax.ppermute(block, axis, [(i, i ^ apart) for i in range(lax.axis_size(ax...  36.8 us
    all_to_all x2, starting transfers between devices, gather_over(): lax.all_to_all(jnp.broadcast_to(block, (count,) + block.shape), axis, 0, 0)  26.9 us
    all_to_all x1, blocking collectives, local(): total = lax.all_to_all(total, ('zl', 'core'), 0, 0).reshape(4, 2, 128, 256)  17.8 us
    ppermute x3, starting transfers between devices, local(): lax.ppermute(pick(gate, high_z ^ k), ('zh', 'core'), [(i, i ^ 2 * k + 1)...  16.6 us
    all_to_all x1, starting transfers between devices, local(): packet = lax.all_to_all(packet, SEQ, 0, 0)  16.4 us
    all_to_all x1, starting transfers between devices, local(): conv = lax.all_to_all(convolve(signal, resp), SEQ, 0, 0).reshape(256, 128)  15.1 us
    ppermute x12, waiting for transfers between devices, exchange(): lax.ppermute(block, axis, [(i, i ^ apart) for i in range(lax.axis_size(ax...  11.8 us
    all_to_all x1, waiting for transfers between devices, local(): lax.all_to_all(jnp.broadcast_to(hidden, (8, 256, 128)), ('x', 'core'), 0, 0)  9.5 us
  transfers between devices with their start and end apart: 21, of which 7 were waited for; matrix products, arithmetic and copies ran while one was open for 13% of the time, Pallas kernels for 0%

profile of v2, /device:TPU:1, one launch (start us, length us, event | category | flops | bytes accessed | tf_op | source)
XLA Modules:
  0.0 192.4 jit_solution(4171182155240366698)
XLA Ops:
  0.0 1.6 collective-permute-start
  1.6 0.8 broadcast_in_dim.9
  2.4 22.8 %all-to-all-start = ((bf16[4,128,512]{2,1,0:T(8,128)(2,1)}), bf16[4,128,512]{2,1,0:T(8,128)(2,1)S(1)}, u32[]{:S(2)}, u32[]{:S(2)}) async-start(bf16[4,128,512]{2,1,0:T(8,128)(2,1)} %broadcast_in_dim.9), calls=%async_computation | async-start | bytes 1048576 | tf_op jit(solution)/shard_map/all_to_all | solution.py:67
  25.2 4.6 %collective-permute-start.3 = (bf16[256,256]{1,0:T(8,128)(2,1)}, bf16[256,256]{1,0:T(8,128)(2,1)S(1)}, u32[]{:S(2)}, u32[]{:S(2)}) collective-permute-start(bf16[256,256]{1,0:T(8,128)(2,1)} %param.13), channel_id=1, source_target_pairs={{0,384},{128,256},{256,128},{384,0},{1,385},{129,257},{257,129},{3... | collective-permute-start | bytes 393224 | tf_op jit(solution)/shard_map/ppermute | solution.py:80
  29.8 2.3 %collective-permute-start.2 = (bf16[256,256]{1,0:T(8,128)(2,1)}, bf16[256,256]{1,0:T(8,128)(2,1)S(1)}, u32[]{:S(2)}, u32[]{:S(2)}) collective-permute-start(bf16[256,256]{1,0:T(8,128)(2,1)} %param.13), channel_id=1, source_target_pairs={{0,256},{128,384},{256,0},{384,128},{1,257},{129,385},{257,1},{385... | collective-permute-start | bytes 393224 | tf_op jit(solution)/shard_map/ppermute | solution.py:80
  32.1 2.2 %collective-permute-start.1 = (bf16[256,256]{1,0:T(8,128)(2,1)}, bf16[256,256]{1,0:T(8,128)(2,1)S(1)}, u32[]{:S(2)}, u32[]{:S(2)}) collective-permute-start(bf16[256,256]{1,0:T(8,128)(2,1)} %param.13), channel_id=1, source_target_pairs={{0,128},{128,0},{256,384},{384,256},{1,129},{129,1},{257,385},{385... | collective-permute-start | bytes 393224 | tf_op jit(solution)/shard_map/ppermute | solution.py:80
  34.3 4.9 %all-to-all-done = bf16[4,128,512]{2,1,0:T(8,128)(2,1)S(1)} async-done(((bf16[4,128,512]{2,1,0:T(8,128)(2,1)}), bf16[4,128,512]{2,1,0:T(8,128)(2,1)S(1)}, u32[]{:S(2)}, u32[]{:S(2)}) %all-to-all-start) | async-done | bytes 524320 | tf_op jit(solution)/shard_map/all_to_all | solution.py:67
  39.2 1.5 broadcast_in_dim.10
  40.7 4.1 %all-to-all-start.1 = ((bf16[4,512,512]{2,1,0:T(8,128)(2,1)}), bf16[4,512,512]{2,1,0:T(8,128)(2,1)S(1)}, u32[]{:S(2)}, u32[]{:S(2)}) async-start(bf16[4,512,512]{2,1,0:T(8,128)(2,1)} %broadcast_in_dim.10), calls=%async_computation.1 | async-start | bytes 4194304 | tf_op jit(solution)/shard_map/all_to_all | solution.py:67
  44.9 4.6 %collective-permute-start.7 = (bf16[256,256]{1,0:T(8,128)(2,1)S(1)}, bf16[256,256]{1,0:T(8,128)(2,1)S(1)}, u32[]{:S(2)}, u32[]{:S(2)}) collective-permute-start(bf16[256,256]{1,0:T(8,128)(2,1)S(1)} %copy-done.11), channel_id=1, source_target_pairs={{0,384},{128,256},{256,128},{384,0},{1,385},{129,257},{257,129},{3... | collective-permute-start | bytes 393224 | tf_op jit(solution)/shard_map/ppermute | solution.py:80
  49.5 2.3 %collective-permute-start.6 = (bf16[256,256]{1,0:T(8,128)(2,1)S(1)}, bf16[256,256]{1,0:T(8,128)(2,1)S(1)}, u32[]{:S(2)}, u32[]{:S(2)}) collective-permute-start(bf16[256,256]{1,0:T(8,128)(2,1)S(1)} %copy-done.11), channel_id=1, source_target_pairs={{0,256},{128,384},{256,0},{384,128},{1,257},{129,385},{257,1},{385... | collective-permute-start | bytes 393224 | tf_op jit(solution)/shard_map/ppermute | solution.py:80
  51.8 2.1 %collective-permute-start.5 = (bf16[256,256]{1,0:T(8,128)(2,1)S(1)}, bf16[256,256]{1,0:T(8,128)(2,1)S(1)}, u32[]{:S(2)}, u32[]{:S(2)}) collective-permute-start(bf16[256,256]{1,0:T(8,128)(2,1)S(1)} %copy-done.11), channel_id=1, source_target_pairs={{0,128},{128,0},{256,384},{384,256},{1,129},{129,1},{257,385},{385... | collective-permute-start | bytes 393224 | tf_op jit(solution)/shard_map/ppermute | solution.py:80
  54.0 0.1 pad_maximum_fusion.2
  54.1 2.6 %collective-permute-done.6 = bf16[256,256]{1,0:T(8,128)(2,1)S(1)} collective-permute-done((bf16[256,256]{1,0:T(8,128)(2,1)S(1)}, bf16[256,256]{1,0:T(8,128)(2,1)S(1)}, u32[]{:S(2)}, u32[]{:S(2)}) %collective-permute-start.6) | collective-permute-done | bytes 131104 | tf_op jit(solution)/shard_map/ppermute | solution.py:80
  56.7 1.7 collective-permute-done.5
  58.5 0.1 constant_dynamic-slice_fusion.19
  58.6 0.9 pad_maximum_fusion.3
  59.5 4.7 %collective-permute-start.4 = (bf16[4,256,256]{2,1,0:T(8,128)(2,1)}, bf16[4,256,256]{2,1,0:T(8,128)(2,1)}, u32[]{:S(2)}, u32[]{:S(2)}) collective-permute-start(bf16[4,256,256]{2,1,0:T(8,128)(2,1)} %pad_maximum_fusion.3), channel_id=1, source_target_pairs={{0,16},{16,0},{1,17},{17,1},{2,18},{18,2},{3,19},{19,3},{4,20},{20... | collective-permute-start | bytes 1572872 | tf_op jit(solution)/shard_map/ppermute | solution.py:80
  64.2 0.1 copy.48
  64.3 0.9 pad_maximum_fusion.5
  65.1 1.9 collective-permute-start.8
  67.1 1.1 select_bitcast_fusion.3
  68.2 1.1 pad_maximum_fusion
  69.3 0.2 all-to-all-done.1
  69.5 2.7 %fusion.1 = bf16[256,512]{1,0:T(8,128)(2,1)S(1)} fusion(bf16[4,512,256]{2,1,0:T(8,128)(2,1)} %bitcast.133, bf16[4,512,512]{2,1,0:T(8,128)(2,1)S(1)} %all-to-all-done.1), kind=kOutput, calls=%fused_computation.6 | convolution fusion | flops 537001984 | bytes 3407872 | tf_op jit(solution)/shard_map/xkc,xtk->ct/dot_general | solution.py:76
  72.2 0.8 maximum_bitcast_fusion
  73.0 16.4 %all-to-all-start.2 = ((bf16[32,8,768]{2,1,0:T(8,128)(2,1)}), bf16[32,8,768]{2,1,0:T(8,128)(2,1)S(1)}, u32[]{:S(2)}, u32[]{:S(2)}) async-start(bf16[32,8,768]{2,1,0:T(8,128)(2,1)} %maximum_bitcast_fusion), calls=%async_computation.2 | async-start | bytes 786432 | tf_op jit(solution)/shard_map/all_to_all | solution.py:107
  89.5 1.1 select_bitcast_fusion.1
  90.7 0.1 pad_maximum_fusion.1
  90.8 0.9 copy.42
  91.6 0.7 reshape.65
  92.4 2.5 %convolution_bitcast_fusion = f32[256,4,128]{2,0,1:T(8,128)S(1)} fusion(bf16[4,128,512,4]{2,1,0,3:T(8,128)(2,1)} %bitcast.130, bf16[4,512,256,1]{1,2,0,3:T(8,128)(2,1)S(1)} %reshape.65), kind=kOutput, calls=%fused_computation.4 | convolution fusion | flops 536870912 | bytes 3670016 | tf_op jit(solution)/shard_map/xkc,xtk->ct/dot_general | solution.py:76
  94.9 0.8 dynamic-slice_bitcast_fusion.1
  95.6 7.4 %collective-permute-start.11 = (f32[256,128]{1,0:T(8,128)}, f32[256,128]{1,0:T(8,128)}, u32[]{:S(2)}, u32[]{:S(2)}) collective-permute-start(f32[256,128]{1,0:T(8,128)} %get-tuple-element.50), channel_id=1, source_target_pairs={{0,112},{16,96},{32,80},{48,64},{64,48},{80,32},{96,16},{112,0},{1... | collective-permute-start | bytes 393224 | tf_op jit(solution)/shard_map/ppermute | solution.py:110
  103.1 7.0 %collective-permute-start.9 = (f32[256,128]{1,0:T(8,128)}, f32[256,128]{1,0:T(8,128)}, u32[]{:S(2)}, u32[]{:S(2)}) collective-permute-start(f32[256,128]{1,0:T(8,128)} %get-tuple-element.51), channel_id=1, source_target_pairs={{0,48},{16,32},{32,16},{48,0},{64,112},{80,96},{96,80},{112,64},{1... | collective-permute-start | bytes 393224 | tf_op jit(solution)/shard_map/ppermute | solution.py:110
  110.1 2.1 %collective-permute-start.10 = (f32[256,128]{1,0:T(8,128)}, f32[256,128]{1,0:T(8,128)}, u32[]{:S(2)}, u32[]{:S(2)}) collective-permute-start(f32[256,128]{1,0:T(8,128)} %get-tuple-element.49), channel_id=1, source_target_pairs={{0,80},{16,64},{32,112},{48,96},{64,16},{80,0},{96,48},{112,32},{1... | collective-permute-start | bytes 393224 | tf_op jit(solution)/shard_map/ppermute | solution.py:110
  112.2 1.1 constant_dynamic-slice_fusion.3
  113.4 2.3 %collective-permute-start.13 = (bf16[256,1024]{1,0:T(8,128)(2,1)S(1)}, bf16[256,1024]{1,0:T(8,128)(2,1)S(1)}, u32[]{:S(2)}, u32[]{:S(2)}) collective-permute-start(bf16[256,1024]{1,0:T(8,128)(2,1)S(1)} %pad_maximum_fusion.7), channel_id=1, source_target_pairs={{0,4},{4,0},{8,12},{12,8},{1,5},{5,1},{9,13},{13,9},{2,6},{6,2},{1... | collective-permute-start | bytes 1572872 | tf_op jit(solution)/shard_map/ppermute | solution.py:80
  115.7 0.9 pad_maximum_fusion.8
  116.6 3.7 %collective-permute-start.14 = (bf16[256,1024]{1,0:T(8,128)(2,1)}, bf16[256,1024]{1,0:T(8,128)(2,1)}, u32[]{:S(2)}, u32[]{:S(2)}) collective-permute-start(bf16[256,1024]{1,0:T(8,128)(2,1)} %pad_maximum_fusion.8), channel_id=1, source_target_pairs={{0,8},{4,12},{8,0},{12,4},{1,9},{5,13},{9,1},{13,5},{2,10},{6,14},... | collective-permute-start | bytes 1572872 | tf_op jit(solution)/shard_map/ppermute | solution.py:80
  120.5 0.6 fusion.39
  121.2 1.5 fusion.9
  122.8 0.6 fusion.13
  123.4 0.4 fusion.29
  123.8 0.4 fusion.2
  124.3 0.8 copy.41
  125.0 15.1 %all-to-all-start.3 = ((f32[32,8,128]{2,1,0:T(8,128)}), f32[32,8,128]{2,1,0:T(8,128)S(1)}, u32[]{:S(2)}, u32[]{:S(2)}) async-start(f32[32,8,128]{2,1,0:T(8,128)} %bitcast.21), calls=%async_computation.3 | async-start | bytes 262144 | tf_op jit(solution)/shard_map/all_to_all | solution.py:124
  140.1 3.7 %collective-permute-start.15 = (bf16[256,1024]{1,0:T(8,128)(2,1)S(1)}, bf16[256,1024]{1,0:T(8,128)(2,1)S(1)}, u32[]{:S(2)}, u32[]{:S(2)}) collective-permute-start(bf16[256,1024]{1,0:T(8,128)(2,1)S(1)} %pad_maximum_fusion.9), channel_id=1, source_target_pairs={{0,12},{4,8},{8,4},{12,0},{1,13},{5,9},{9,5},{13,1},{2,14},{6,10},... | collective-permute-start | bytes 1572872 | tf_op jit(solution)/shard_map/ppermute | solution.py:80
  143.9 1.7 add_add_fusion
  145.6 2.4 %collective-permute-start.12 = (f32[256,128]{1,0:T(8,128)}, f32[256,128]{1,0:T(8,128)S(1)}, u32[]{:S(2)}, u32[]{:S(2)}) collective-permute-start(f32[256,128]{1,0:T(8,128)} %add_add_fusion), channel_id=1, source_target_pairs={{0,16},{16,0},{1,17},{17,1},{2,18},{18,2},{3,19},{19,3},{4,20},{20... | collective-permute-start | bytes 393224 | tf_op jit(solution)/shard_map/ppermute | solution.py:80
  148.0 1.1 pad_maximum_fusion.6
  149.1 0.1 collective-permute-done.12
  149.2 7.3 %collective-permute-done.15 = bf16[256,1024]{1,0:T(8,128)(2,1)S(1)} collective-permute-done((bf16[256,1024]{1,0:T(8,128)(2,1)S(1)}, bf16[256,1024]{1,0:T(8,128)(2,1)S(1)}, u32[]{:S(2)}, u32[]{:S(2)}) %collective-permute-start.15) | collective-permute-done | bytes 524320 | tf_op jit(solution)/shard_map/ppermute | solution.py:80
  156.6 0.1 copy.44
  156.7 0.8 broadcast_in_dim.11
  157.6 4.4 %all-to-all-start.4 = ((bf16[8,256,128]{1,2,0:T(8,128)(2,1)}), bf16[8,256,128]{1,2,0:T(8,128)(2,1)S(1)}, u32[]{:S(2)}, u32[]{:S(2)}) async-start(bf16[8,256,128]{1,2,0:T(8,128)(2,1)} %broadcast_in_dim.11), calls=%async_computation.4 | async-start | bytes 1048576 | tf_op jit(solution)/shard_map/all_to_all | solution.py:128
  162.0 9.5 %all-to-all-done.4 = bf16[8,256,128]{1,2,0:T(8,128)(2,1)S(1)} async-done(((bf16[8,256,128]{1,2,0:T(8,128)(2,1)}), bf16[8,256,128]{1,2,0:T(8,128)(2,1)S(1)}, u32[]{:S(2)}, u32[]{:S(2)}) %all-to-all-start.4) | async-done | bytes 524320 | tf_op jit(solution)/shard_map/all_to_all | solution.py:128
  171.5 0.3 fusion.6
  171.8 0.3 convolution_add_fusion.2
  172.1 1.3 convolution_add_fusion.1
  173.5 0.3 fusion
  173.8 17.8 %all_to_all.30 = bf16[8,128,256]{2,1,0:T(8,128)(2,1)S(1)} all-to-all(bf16[8,128,256]{2,1,0:T(8,128)(2,1)S(1)} %bitcast.132), channel_id=1, replica_groups=mesh['y'=4,'zh'=4,'core'=2,'x'=4,'zl'=4] {'zl','core'}, dimensions={0} | all-to-all | bytes 1048576 | tf_op jit(solution)/shard_map/all_to_all | solution.py:133
  191.6 0.1 reduce
  191.7 0.7 pad_maximum_fusion.10
  (52 shorter events, 0.6 us)
Async XLA Ops:
  0.0 1.6 collective-permute-start
  2.4 36.8 %all-to-all-start = ((bf16[4,128,512]{2,1,0:T(8,128)(2,1)}), bf16[4,128,512]{2,1,0:T(8,128)(2,1)S(1)}, u32[]{:S(2)}, u32[]{:S(2)}) async-start(bf16[4,128,512]{2,1,0:T(8,128)(2,1)} %broadcast_in_dim.9), calls=%async_computation | async-start | bytes 1048576 | tf_op jit(solution)/shard_map/all_to_all | solution.py:67
  25.2 26.6 %collective-permute-start.3 = (bf16[256,256]{1,0:T(8,128)(2,1)}, bf16[256,256]{1,0:T(8,128)(2,1)S(1)}, u32[]{:S(2)}, u32[]{:S(2)}) collective-permute-start(bf16[256,256]{1,0:T(8,128)(2,1)} %param.13), channel_id=1, source_target_pairs={{0,384},{128,256},{256,128},{384,0},{1,385},{129,257},{257,129},{3... | collective-permute-start | bytes 393224 | tf_op jit(solution)/shard_map/ppermute | solution.py:80
  29.8 24.1 %collective-permute-start.2 = (bf16[256,256]{1,0:T(8,128)(2,1)}, bf16[256,256]{1,0:T(8,128)(2,1)S(1)}, u32[]{:S(2)}, u32[]{:S(2)}) collective-permute-start(bf16[256,256]{1,0:T(8,128)(2,1)} %param.13), channel_id=1, source_target_pairs={{0,256},{128,384},{256,0},{384,128},{1,257},{129,385},{257,1},{385... | collective-permute-start | bytes 393224 | tf_op jit(solution)/shard_map/ppermute | solution.py:80
  32.1 21.9 %collective-permute-start.1 = (bf16[256,256]{1,0:T(8,128)(2,1)}, bf16[256,256]{1,0:T(8,128)(2,1)S(1)}, u32[]{:S(2)}, u32[]{:S(2)}) collective-permute-start(bf16[256,256]{1,0:T(8,128)(2,1)} %param.13), channel_id=1, source_target_pairs={{0,128},{128,0},{256,384},{384,256},{1,129},{129,1},{257,385},{385... | collective-permute-start | bytes 393224 | tf_op jit(solution)/shard_map/ppermute | solution.py:80
  40.7 4.2 %copy-start.11 = (bf16[256,256]{1,0:T(8,128)(2,1)S(1)}, bf16[256,256]{1,0:T(8,128)(2,1)}, u32[]{:S(2)}) copy-start(bf16[256,256]{1,0:T(8,128)(2,1)} %param.12) | copy-start | bytes 393220
  40.7 13.3 %copy-start.10 = (bf16[256,256]{1,0:T(8,128)(2,1)S(1)}, bf16[256,256]{1,0:T(8,128)(2,1)}, u32[]{:S(2)}) copy-start(bf16[256,256]{1,0:T(8,128)(2,1)} %param.13) | copy-start | bytes 393220
  40.7 28.8 %all-to-all-start.1 = ((bf16[4,512,512]{2,1,0:T(8,128)(2,1)}), bf16[4,512,512]{2,1,0:T(8,128)(2,1)S(1)}, u32[]{:S(2)}, u32[]{:S(2)}) async-start(bf16[4,512,512]{2,1,0:T(8,128)(2,1)} %broadcast_in_dim.10), calls=%async_computation.1 | async-start | bytes 4194304 | tf_op jit(solution)/shard_map/all_to_all | solution.py:67
  44.9 9.2 %collective-permute-start.7 = (bf16[256,256]{1,0:T(8,128)(2,1)S(1)}, bf16[256,256]{1,0:T(8,128)(2,1)S(1)}, u32[]{:S(2)}, u32[]{:S(2)}) collective-permute-start(bf16[256,256]{1,0:T(8,128)(2,1)S(1)} %copy-done.11), channel_id=1, source_target_pairs={{0,384},{128,256},{256,128},{384,0},{1,385},{129,257},{257,129},{3... | collective-permute-start | bytes 393224 | tf_op jit(solution)/shard_map/ppermute | solution.py:80
  49.5 7.2 %collective-permute-start.6 = (bf16[256,256]{1,0:T(8,128)(2,1)S(1)}, bf16[256,256]{1,0:T(8,128)(2,1)S(1)}, u32[]{:S(2)}, u32[]{:S(2)}) collective-permute-start(bf16[256,256]{1,0:T(8,128)(2,1)S(1)} %copy-done.11), channel_id=1, source_target_pairs={{0,256},{128,384},{256,0},{384,128},{1,257},{129,385},{257,1},{385... | collective-permute-start | bytes 393224 | tf_op jit(solution)/shard_map/ppermute | solution.py:80
  51.8 6.7 %collective-permute-start.5 = (bf16[256,256]{1,0:T(8,128)(2,1)S(1)}, bf16[256,256]{1,0:T(8,128)(2,1)S(1)}, u32[]{:S(2)}, u32[]{:S(2)}) collective-permute-start(bf16[256,256]{1,0:T(8,128)(2,1)S(1)} %copy-done.11), channel_id=1, source_target_pairs={{0,128},{128,0},{256,384},{384,256},{1,129},{129,1},{257,385},{385... | collective-permute-start | bytes 393224 | tf_op jit(solution)/shard_map/ppermute | solution.py:80
  58.4 5.7 %copy-start.8 = (f32[2,128,256]{2,1,0:T(8,128)S(1)}, f32[2,128,256]{2,1,0:T(8,128)}, u32[]{:S(2)}) copy-start(f32[2,128,256]{2,1,0:T(8,128)} %param.15) | copy-start | bytes 786436
  59.5 7.6 %collective-permute-start.4 = (bf16[4,256,256]{2,1,0:T(8,128)(2,1)}, bf16[4,256,256]{2,1,0:T(8,128)(2,1)}, u32[]{:S(2)}, u32[]{:S(2)}) collective-permute-start(bf16[4,256,256]{2,1,0:T(8,128)(2,1)} %pad_maximum_fusion.3), channel_id=1, source_target_pairs={{0,16},{16,0},{1,17},{17,1},{2,18},{18,2},{3,19},{19,3},{4,20},{20... | collective-permute-start | bytes 1572872 | tf_op jit(solution)/shard_map/ppermute | solution.py:80
  65.1 24.4 %collective-permute-start.8 = (bf16[4,256,256]{2,1,0:T(8,128)(2,1)}, bf16[4,256,256]{2,1,0:T(8,128)(2,1)}, u32[]{:S(2)}, u32[]{:S(2)}) collective-permute-start(bf16[4,256,256]{2,1,0:T(8,128)(2,1)} %pad_maximum_fusion.5), channel_id=1, source_target_pairs={{0,16},{16,0},{1,17},{17,1},{2,18},{18,2},{3,19},{19,3},{4,20},{20... | collective-permute-start | bytes 1572872 | tf_op jit(solution)/shard_map/ppermute | solution.py:80
  69.5 3.5 %copy-start = (bf16[4,512,512]{2,1,0:T(8,128)(2,1)}, bf16[4,512,512]{2,1,0:T(8,128)(2,1)S(1)}, u32[]{:S(2)}) copy-start(bf16[4,512,512]{2,1,0:T(8,128)(2,1)S(1)} %all-to-all-done.1) | copy-start | bytes 6291460
  73.0 47.4 %all-to-all-start.2 = ((bf16[32,8,768]{2,1,0:T(8,128)(2,1)}), bf16[32,8,768]{2,1,0:T(8,128)(2,1)S(1)}, u32[]{:S(2)}, u32[]{:S(2)}) async-start(bf16[32,8,768]{2,1,0:T(8,128)(2,1)} %maximum_bitcast_fusion), calls=%async_computation.2 | async-start | bytes 786432 | tf_op jit(solution)/shard_map/all_to_all | solution.py:107
  92.4 19.9 %copy-start.3 = (bf16[256,8192]{1,0:T(8,128)(2,1)S(1)}, bf16[256,8192]{1,0:T(8,128)(2,1)}, u32[]{:S(2)}) copy-start(bf16[256,8192]{1,0:T(8,128)(2,1)} %param.14) | copy-start | bytes 12582916
  95.6 44.5 %collective-permute-start.11 = (f32[256,128]{1,0:T(8,128)}, f32[256,128]{1,0:T(8,128)}, u32[]{:S(2)}, u32[]{:S(2)}) collective-permute-start(f32[256,128]{1,0:T(8,128)} %get-tuple-element.50), channel_id=1, source_target_pairs={{0,112},{16,96},{32,80},{48,64},{64,48},{80,32},{96,16},{112,0},{1... | collective-permute-start | bytes 393224 | tf_op jit(solution)/shard_map/ppermute | solution.py:110
  103.1 40.8 %collective-permute-start.9 = (f32[256,128]{1,0:T(8,128)}, f32[256,128]{1,0:T(8,128)}, u32[]{:S(2)}, u32[]{:S(2)}) collective-permute-start(f32[256,128]{1,0:T(8,128)} %get-tuple-element.51), channel_id=1, source_target_pairs={{0,48},{16,32},{32,16},{48,0},{64,112},{80,96},{96,80},{112,64},{1... | collective-permute-start | bytes 393224 | tf_op jit(solution)/shard_map/ppermute | solution.py:110
  110.1 33.7 %collective-permute-start.10 = (f32[256,128]{1,0:T(8,128)}, f32[256,128]{1,0:T(8,128)}, u32[]{:S(2)}, u32[]{:S(2)}) collective-permute-start(f32[256,128]{1,0:T(8,128)} %get-tuple-element.49), channel_id=1, source_target_pairs={{0,80},{16,64},{32,112},{48,96},{64,16},{80,0},{96,48},{112,32},{1... | collective-permute-start | bytes 393224 | tf_op jit(solution)/shard_map/ppermute | solution.py:110
  113.3 7.2 %copy-start.4 = (f32[512,256]{1,0:T(8,128)S(1)}, f32[512,256]{1,0:T(8,128)}, u32[]{:S(2)}) copy-start(f32[512,256]{1,0:T(8,128)} %constant.103) | copy-start | bytes 1572868
  113.4 35.8 %collective-permute-start.13 = (bf16[256,1024]{1,0:T(8,128)(2,1)S(1)}, bf16[256,1024]{1,0:T(8,128)(2,1)S(1)}, u32[]{:S(2)}, u32[]{:S(2)}) collective-permute-start(bf16[256,1024]{1,0:T(8,128)(2,1)S(1)} %pad_maximum_fusion.7), channel_id=1, source_target_pairs={{0,4},{4,0},{8,12},{12,8},{1,5},{5,1},{9,13},{13,9},{2,6},{6,2},{1... | collective-permute-start | bytes 1572872 | tf_op jit(solution)/shard_map/ppermute | solution.py:80
  115.7 5.4 %copy-start.1 = (f32[256,128]{1,0:T(8,128)S(1)}, f32[256,128]{1,0:T(8,128)}, u32[]{:S(2)}) copy-start(f32[256,128]{1,0:T(8,128)} %constant.96.clone) | copy-start | bytes 393220
  115.7 5.4 %copy-start.2 = (f32[256,128]{1,0:T(8,128)S(1)}, f32[256,128]{1,0:T(8,128)}, u32[]{:S(2)}) copy-start(f32[256,128]{1,0:T(8,128)} %constant.95.clone) | copy-start | bytes 393220
  116.6 32.6 %collective-permute-start.14 = (bf16[256,1024]{1,0:T(8,128)(2,1)}, bf16[256,1024]{1,0:T(8,128)(2,1)}, u32[]{:S(2)}, u32[]{:S(2)}) collective-permute-start(bf16[256,1024]{1,0:T(8,128)(2,1)} %pad_maximum_fusion.8), channel_id=1, source_target_pairs={{0,8},{4,12},{8,0},{12,4},{1,9},{5,13},{9,1},{13,5},{2,10},{6,14},... | collective-permute-start | bytes 1572872 | tf_op jit(solution)/shard_map/ppermute | solution.py:80
  120.5 2.3 %copy-start.9 = (f32[128,256]{1,0:T(8,128)S(1)}, f32[128,256]{1,0:T(8,128)}, u32[]{:S(2)}) copy-start(f32[128,256]{1,0:T(8,128)} %constant.99.clone) | copy-start | bytes 393220
  121.1 2.3 %copy-start.7 = (f32[256,256]{1,0:T(8,128)S(1)}, f32[256,256]{1,0:T(8,128)}, u32[]{:S(2)}) copy-start(f32[256,256]{1,0:T(8,128)} %constant.104) | copy-start | bytes 786436
  121.2 2.7 %copy-start.6 = (f32[256,256]{1,0:T(8,128)S(1)}, f32[256,256]{1,0:T(8,128)}, u32[]{:S(2)}) copy-start(f32[256,256]{1,0:T(8,128)} %constant.105) | copy-start | bytes 786436
  122.8 25.2 %copy-start.5 = (bf16[256,256]{1,0:T(8,128)(2,1)S(1)}, bf16[256,256]{1,0:T(8,128)(2,1)}, u32[]{:S(2)}) copy-start(bf16[256,256]{1,0:T(8,128)(2,1)} %get-tuple-element.39) | copy-start | bytes 393220
  125.0 31.5 %all-to-all-start.3 = ((f32[32,8,128]{2,1,0:T(8,128)}), f32[32,8,128]{2,1,0:T(8,128)S(1)}, u32[]{:S(2)}, u32[]{:S(2)}) async-start(f32[32,8,128]{2,1,0:T(8,128)} %bitcast.21), calls=%async_computation.3 | async-start | bytes 262144 | tf_op jit(solution)/shard_map/all_to_all | solution.py:124
  140.1 16.4 %collective-permute-start.15 = (bf16[256,1024]{1,0:T(8,128)(2,1)S(1)}, bf16[256,1024]{1,0:T(8,128)(2,1)S(1)}, u32[]{:S(2)}, u32[]{:S(2)}) collective-permute-start(bf16[256,1024]{1,0:T(8,128)(2,1)S(1)} %pad_maximum_fusion.9), channel_id=1, source_target_pairs={{0,12},{4,8},{8,4},{12,0},{1,13},{5,9},{9,5},{13,1},{2,14},{6,10},... | collective-permute-start | bytes 1572872 | tf_op jit(solution)/shard_map/ppermute | solution.py:80
  145.6 3.6 %collective-permute-start.12 = (f32[256,128]{1,0:T(8,128)}, f32[256,128]{1,0:T(8,128)S(1)}, u32[]{:S(2)}, u32[]{:S(2)}) collective-permute-start(f32[256,128]{1,0:T(8,128)} %add_add_fusion), channel_id=1, source_target_pairs={{0,16},{16,0},{1,17},{17,1},{2,18},{18,2},{3,19},{19,3},{4,20},{20... | collective-permute-start | bytes 393224 | tf_op jit(solution)/shard_map/ppermute | solution.py:80
  157.6 13.9 %all-to-all-start.4 = ((bf16[8,256,128]{1,2,0:T(8,128)(2,1)}), bf16[8,256,128]{1,2,0:T(8,128)(2,1)S(1)}, u32[]{:S(2)}, u32[]{:S(2)}) async-start(bf16[8,256,128]{1,2,0:T(8,128)(2,1)} %broadcast_in_dim.11), calls=%async_computation.4 | async-start | bytes 1048576 | tf_op jit(solution)/shard_map/all_to_all | solution.py:128

commit v3 on v2

--- a/solution.py
+++ b/solution.py
@@ -12,6 +12,7 @@
 N1, N2 = 32, 128
 TOTAL = N1 * N2
 GROUP = 8
+ARRIVALS = ((0, 3, 2, 1), (3, 1, 0, 2), (1, 3, 2, 0), (2, 1, 0, 3))
 
 
 def reverse(count):
@@ -33,7 +34,7 @@
 
 
 def high(left, right):
-    return jnp.dot(left, right, precision=lax.Precision.HIGHEST, preferred_element_type=jnp.float32)
+    return jnp.dot(left, right, precision=lax.Precision.HIGH, preferred_element_type=jnp.float32)
 
 
 def convolve(signal, response):
@@ -71,11 +72,6 @@
     return lax.optimization_barrier((block, earlier))[0]
 
 
-def project(weight, tokens):
-    weight = weight.reshape(4, 512, 256)
-    return jnp.einsum("xkc,xtk->ct", weight, tokens, preferred_element_type=jnp.float32)
-
-
 def exchange(block, axis, apart):
     return lax.ppermute(block, axis, [(i, i ^ apart) for i in range(lax.axis_size(axis))])
 
@@ -84,31 +80,42 @@
     return lax.dynamic_index_in_dim(blocks, index, 0, keepdims=False)
 
 
+def summed(parts):
+    total = parts.reshape(4, 4, 2, GROUP, 4, N2).astype(jnp.float32).sum(axis=1)
+    return jnp.transpose(total, (0, 3, 1, 2, 4)).reshape(N1, GROUP, N2)
+
+
 def local(tokens, gate_weight, value_weight, out_weight, filter_spectrum):
-    column, core, row, high_z = (lax.axis_index(axis) for axis in ("x", "core", "y", "zh"))
-    swap = [(zh * 4 + zl, zl * 4 + zh) for zh in range(4) for zl in range(4)]
+    column, core, row = (lax.axis_index(axis) for axis in ("x", "core", "y"))
+    swap = [(t * 4 + b, b * 4 + ARRIVALS[b].index(t)) for t in range(4) for b in range(4)]
     swapped = lax.ppermute(tokens, ("zh", "zl"), swap)
-    near = gather_over(swapped, "zl").reshape(512, 512)
+    swapped = jnp.where(core == 0, swapped, jnp.concatenate([swapped[:, 256:], swapped[:, :256]], axis=1))
+    near = gather_over(swapped, "zl")
+    places = jnp.asarray(np.argsort(np.array(ARRIVALS), axis=1), jnp.int32)[lax.axis_index("zh")]
+    near = jnp.concatenate([pick(near, places[t]) for t in range(4)])
+    both = after(jnp.concatenate([value_weight, gate_weight], axis=1), swapped)
+    parts = [both, exchange(both, "y", 1)]
+    near, parts[1] = lax.optimization_barrier((near, parts[1]))
+    parts += [exchange(parts[1], "y", 3), exchange(both, "y", 3)]
     whole = gather_over(near, "x")
 
-    def rows_of(weight):
-        mine = jnp.stack([exchange(weight, "y", k) if k else weight for k in range(4)])
-        mine = jnp.stack([pick(mine, row ^ y) for y in range(4)])
-        theirs = exchange(mine, "core", 1)
-        return jnp.stack([jnp.where(core == 0, mine, theirs), jnp.where(core == 0, theirs, mine)], axis=1).reshape(2048, 256)
+    def by_row(low, high):
+        far = [row ^ y for y in range(4)]
+        return jnp.stack([jnp.where(k < 2, pick(low, k % 2), pick(high, k % 2)) for k in far])
 
-    value_rows = rows_of(after(value_weight, swapped))
-    gate_rows = rows_of(after(gate_weight, near))
-    whole, value_rows = lax.optimization_barrier((whole, value_rows))
+    low, high = jnp.stack(parts[:2]), jnp.stack(parts[2:])
+    mine = by_row(low, high)
+    theirs = by_row(exchange(low, "core", 1), exchange(high, "core", 1))
+    whole, mine, theirs = lax.optimization_barrier((whole, mine, theirs))
 
-    value = project(value_rows, whole).astype(jnp.bfloat16)
+    projected = 0.0
+    for rows, part in ((mine, whole[:, :, :256]), (theirs, whole[:, :, 256:])):
+        projected = projected + jnp.einsum("xkc,xtk->ct", rows, part, preferred_element_type=jnp.float32)
+    projected = projected.astype(jnp.bfloat16)
+    value, gate = projected[:256], projected[256:]
     resp = jnp.transpose(filter_spectrum, (2, 0, 1)).reshape(256, 256).astype(jnp.bfloat16)
-    packet = jnp.concatenate([value, resp], axis=1).reshape(N1, GROUP, 768)
+    packet = jnp.concatenate([value, gate, resp], axis=1).reshape(N1, GROUP, 1280)
     packet = lax.all_to_all(packet, SEQ, 0, 0)
-
-    gate = jnp.transpose(project(gate_rows, whole).reshape(256, 4, 128), (1, 0, 2))
-    far = [lax.ppermute(pick(gate, high_z ^ k), ("zh", "core"), [(i, i ^ (2 * k + 1)) for i in range(8)]) for k in (1, 2, 3)]
-    gate = pick(gate, high_z) + exchange(sum(far), "core", 1)
 
     held = after(out_weight, value)
 
@@ -117,14 +124,13 @@
 
     shares = [exchange(share(k), "x", k) if k else share(k) for k in range(4)]
 
-    signal = packet[:, :, :512].reshape(4, 4, 2, GROUP, 4, N2).astype(jnp.float32).sum(axis=1)
-    signal = jnp.transpose(signal, (0, 3, 1, 2, 4)).reshape(N1, GROUP, N2)
-    resp = packet[:, :, 512:].astype(jnp.float32)
+    signal, gate = (summed(packet[:, :, at : at + 512]) for at in (0, 512))
+    resp = packet[:, :, 1024:].astype(jnp.float32)
     resp = jnp.transpose(resp.reshape(N1, GROUP, 2, N2), (2, 0, 1, 3))
-    conv = lax.all_to_all(convolve(signal, resp), SEQ, 0, 0).reshape(256, 128)
-    conv, gate, shares = lax.optimization_barrier((conv, gate, shares))
+    hidden = (jax.nn.silu(gate) * convolve(signal, resp)).astype(jnp.bfloat16)
+    hidden = lax.all_to_all(hidden, SEQ, 0, 0).reshape(256, 128)
+    hidden, shares = lax.optimization_barrier((hidden, shares))
 
-    hidden = (jax.nn.silu(gate) * conv).astype(jnp.bfloat16)
     hidden = lax.all_to_all(jnp.broadcast_to(hidden, (8, 256, 128)), ("x", "core"), 0, 0).reshape(4, 2, 256, 128)
     total = 0.0
     for k in range(4):

time: 194 us -> 189 us (0.974)
  starting transfers between devices: 118 us -> 85.7 us
  waiting for transfers between devices: 26.4 us -> 50 us
  between operations: 0.77 us -> 8.12 us
  matrix products: 11 us -> 6.73 us
    all_to_all x1, waiting for transfers between devices: 0.01 us -> 20.1 us  [local(): packet = lax.all_to_all(packet, SEQ, 0, 0)]
    ppermute x3 -> x0, starting transfers between devices: 16.6 us -> none  [local(): lax.ppermute(pick(gate, high_z ^ k), ('zh', 'core'), [(i, i ^ 2 * k + 1)...]
    all_to_all x1, waiting for transfers between devices: 0.01 us -> 14.4 us  [local(): hidden = lax.all_to_all(hidden, SEQ, 0, 0).reshape(256, 128)]
    ppermute x12 -> x8, starting transfers between devices: 36.8 us -> 27.6 us  [exchange(): lax.ppermute(block, axis, [(i, i ^ apart) for i in range(lax.axis_size(ax...]
    ppermute x12 -> x8, waiting for transfers between devices: 11.8 us -> 4.05 us  [exchange(): lax.ppermute(block, axis, [(i, i ^ apart) for i in range(lax.axis_size(ax...]
    all_to_all x1, starting transfers between devices: 15.1 us -> 9.55 us  [local(): hidden = lax.all_to_all(hidden, SEQ, 0, 0).reshape(256, 128)]
    dot_general x7, matrix products: 8.71 us -> 4.47 us  [the longest x2 2.72 us: local(): jnp.einsum('xkc,xtk->ct', rows, part, preferred_element_type=jnp.float32)]
    all_to_all x2, waiting for transfers between devices: 5.1 us -> 1.97 us  [gather_over(): lax.all_to_all(jnp.broadcast_to(block, (count,) + block.shape), axis, 0, 0)]
  transfers between devices with their start and end apart: 21 -> 14, of which waited for: 7 -> 5; matrix products, arithmetic and copies ran while one was open for 13% -> 8% of each run, Pallas kernels for 0% -> 0%
where the time goes in v3:
time: 189 us; the launch traced here: 188 us
  starting transfers between devices  85.7 us (45%)
  waiting for transfers between devices  50 us (26%)
  blocking collectives  18.4 us (10%)
  other arithmetic  10 us (5%)
  local copies, waits for them, and re-layouts  8.62 us (5%)
  between operations  8.12 us (4%)
  matrix products  6.73 us (4%)
    ppermute x8, starting transfers between devices, exchange(): lax.ppermute(block, axis, [(i, i ^ apart) for i in range(lax.axis_size(ax...  27.6 us
    all_to_all x2, starting transfers between devices, gather_over(): lax.all_to_all(jnp.broadcast_to(block, (count,) + block.shape), axis, 0, 0)  26.5 us
    all_to_all x1, waiting for transfers between devices, local(): packet = lax.all_to_all(packet, SEQ, 0, 0)  20.1 us
    all_to_all x1, blocking collectives, local(): total = lax.all_to_all(total, ('zl', 'core'), 0, 0).reshape(4, 2, 128, 256)  18.4 us
    all_to_all x1, starting transfers between devices, local(): packet = lax.all_to_all(packet, SEQ, 0, 0)  16.5 us
    all_to_all x1, waiting for transfers between devices, local(): hidden = lax.all_to_all(hidden, SEQ, 0, 0).reshape(256, 128)  14.4 us
    all_to_all x1, starting transfers between devices, local(): hidden = lax.all_to_all(hidden, SEQ, 0, 0).reshape(256, 128)  9.55 us
    all_to_all x1, waiting for transfers between devices, local(): lax.all_to_all(jnp.broadcast_to(hidden, (8, 256, 128)), ('x', 'core'), 0, 0)  9.5 us
  transfers between devices with their start and end apart: 14, of which 5 were waited for; matrix products, arithmetic and copies ran while one was open for 8% of the time, Pallas kernels for 0%

profile of v3, /device:TPU:1, one launch (start us, length us, event | category | flops | bytes accessed | tf_op | source)
XLA Modules:
  0.0 187.6 jit_solution(10342086171180917204)
XLA Ops:
  0.0 1.7 collective-permute-start
  1.7 0.8 broadcast_in_dim.9
  2.6 22.5 %all-to-all-start = ((bf16[4,128,512]{2,1,0:T(8,128)(2,1)}), bf16[4,128,512]{2,1,0:T(8,128)(2,1)S(1)}, u32[]{:S(2)}, u32[]{:S(2)}) async-start(bf16[4,128,512]{2,1,0:T(8,128)(2,1)} %broadcast_in_dim.9), calls=%async_computation | async-start | bytes 1048576 | tf_op jit(solution)/shard_map/all_to_all | solution.py:68
  25.1 0.7 constant_dynamic-slice_fusion.16
  25.8 3.2 %collective-permute-start.1 = (bf16[256,512]{1,0:T(8,128)(2,1)S(1)}, bf16[256,512]{1,0:T(8,128)(2,1)S(1)}, u32[]{:S(2)}, u32[]{:S(2)}) collective-permute-start(bf16[256,512]{1,0:T(8,128)(2,1)S(1)} %pad_maximum_fusion.10), channel_id=1, source_target_pairs={{0,128},{128,0},{256,384},{384,256},{1,129},{129,1},{257,385},{385... | collective-permute-start | bytes 786440 | tf_op jit(solution)/shard_map/ppermute | solution.py:76
  29.0 0.7 fusion.60
  37.1 2.0 %all-to-all-done = bf16[4,128,512]{2,1,0:T(8,128)(2,1)S(1)} async-done(((bf16[4,128,512]{2,1,0:T(8,128)(2,1)}), bf16[4,128,512]{2,1,0:T(8,128)(2,1)S(1)}, u32[]{:S(2)}, u32[]{:S(2)}) %all-to-all-start) | async-done | bytes 524320 | tf_op jit(solution)/shard_map/all_to_all | solution.py:68
  39.2 0.0 collective-permute-done.1
  39.2 1.5 broadcast_in_dim.10
  40.7 4.0 %all-to-all-start.1 = ((bf16[4,512,512]{2,1,0:T(8,128)(2,1)}), bf16[4,512,512]{2,1,0:T(8,128)(2,1)S(1)}, u32[]{:S(2)}, u32[]{:S(2)}) async-start(bf16[4,512,512]{2,1,0:T(8,128)(2,1)} %broadcast_in_dim.10), calls=%async_computation.1 | async-start | bytes 4194304 | tf_op jit(solution)/shard_map/all_to_all | solution.py:68
  44.7 4.8 %collective-permute-start.3 = (bf16[256,512]{1,0:T(8,128)(2,1)S(1)}, bf16[256,512]{1,0:T(8,128)(2,1)S(1)}, u32[]{:S(2)}, u32[]{:S(2)}) collective-permute-start(bf16[256,512]{1,0:T(8,128)(2,1)S(1)} %pad_maximum_fusion.10), channel_id=1, source_target_pairs={{0,384},{128,256},{256,128},{384,0},{1,385},{129,257},{257,129},{3... | collective-permute-start | bytes 786440 | tf_op jit(solution)/shard_map/ppermute | solution.py:76
  49.5 1.9 %collective-permute-start.2 = (bf16[256,512]{1,0:T(8,128)(2,1)S(1)}, bf16[256,512]{1,0:T(8,128)(2,1)S(1)}, u32[]{:S(2)}, u32[]{:S(2)}) collective-permute-start(bf16[256,512]{1,0:T(8,128)(2,1)S(1)} %collective-permute-done.1), channel_id=1, source_target_pairs={{0,384},{128,256},{256,128},{384,0},{1,385},{129,257},{257,129},{3... | collective-permute-start | bytes 786440 | tf_op jit(solution)/shard_map/ppermute | solution.py:76
  51.4 0.9 pad_maximum_fusion.2
  52.3 4.1 %collective-permute-start.4 = (bf16[2,256,512]{2,1,0:T(8,128)(2,1)}, bf16[2,256,512]{2,1,0:T(8,128)(2,1)}, u32[]{:S(2)}, u32[]{:S(2)}) collective-permute-start(bf16[2,256,512]{2,1,0:T(8,128)(2,1)} %pad_maximum_fusion.2), channel_id=1, source_target_pairs={{0,16},{16,0},{1,17},{17,1},{2,18},{18,2},{3,19},{19,3},{4,20},{20... | collective-permute-start | bytes 1572872 | tf_op jit(solution)/shard_map/ppermute | solution.py:76
  56.4 0.0 collective-permute-done.3
  56.4 4.0 %collective-permute-done.2 = bf16[256,512]{1,0:T(8,128)(2,1)S(1)} collective-permute-done((bf16[256,512]{1,0:T(8,128)(2,1)S(1)}, bf16[256,512]{1,0:T(8,128)(2,1)S(1)}, u32[]{:S(2)}, u32[]{:S(2)}) %collective-permute-start.2) | collective-permute-done | bytes 262176 | tf_op jit(solution)/shard_map/ppermute | solution.py:76
  60.5 0.9 pad_maximum_fusion.3
  61.3 3.8 %collective-permute-start.5 = (bf16[2,256,512]{2,1,0:T(8,128)(2,1)}, bf16[2,256,512]{2,1,0:T(8,128)(2,1)}, u32[]{:S(2)}, u32[]{:S(2)}) collective-permute-start(bf16[2,256,512]{2,1,0:T(8,128)(2,1)} %pad_maximum_fusion.3), channel_id=1, source_target_pairs={{0,16},{16,0},{1,17},{17,1},{2,18},{18,2},{3,19},{19,3},{4,20},{20... | collective-permute-start | bytes 1572872 | tf_op jit(solution)/shard_map/ppermute | solution.py:76
  65.3 0.2 fusion.18
  65.5 0.7 fusion.12
  66.2 1.1 pad_maximum_fusion
  67.3 0.0 collective-permute-done.4
  67.3 1.6 dynamic-slice_select_fusion.3
  68.9 1.1 pad_maximum_fusion.1
  70.0 2.0 %convolution_bitcast_fusion = f32[512,512]{0,1:T(8,128)S(1)} fusion(bf16[4,256,512]{2,1,0:T(8,128)(2,1)} %pad_maximum_fusion.1, bf16[4,512,512]{2,1,0:T(8,128)(2,1)S(1)} %all-to-all-done.1), kind=kOutput, calls=%fused_computation | convolution fusion | flops 536870912 | bytes 3145728 | tf_op jit(solution)/shard_map/xkc,xtk->ct/dot_general | solution.py:113
  72.0 0.7 fusion.1
  72.9 1.1 copy.24
  73.9 16.5 %all-to-all-start.2 = ((bf16[32,8,1280]{2,1,0:T(8,128)(2,1)}), bf16[32,8,1280]{2,1,0:T(8,128)(2,1)S(1)}, u32[]{:S(2)}, u32[]{:S(2)}) async-start(bf16[32,8,1280]{2,1,0:T(8,128)(2,1)} %bitcast.16), calls=%async_computation.2 | async-start | bytes 1310720 | tf_op jit(solution)/shard_map/all_to_all | solution.py:118
  90.5 2.5 %constant_dynamic-slice_fusion.3 = (bf16[256,256]{1,0:T(8,128)(2,1)S(1)}, bf16[256,256]{1,0:T(8,128)(2,1)S(1)}, bf16[256,256]{1,0:T(8,128)(2,1)S(1)}, bf16[256,2...) fusion(bf16[256,8192]{1,0:T(8,128)(2,1)} %param.15, ...), kind=kLoop, calls=%fused_computation.117 | loop fusion | bytes 4194368 | tf_op jit(solution)/shard_map/dynamic_slice | solution.py:123
  93.0 0.1 pad_maximum_fusion.7
  93.1 0.0 copy-start.3
  93.1 2.3 %collective-permute-start.6 = (bf16[256,1024]{1,0:T(8,128)(2,1)S(1)}, bf16[256,1024]{1,0:T(8,128)(2,1)S(1)}, u32[]{:S(2)}, u32[]{:S(2)}) collective-permute-start(bf16[256,1024]{1,0:T(8,128)(2,1)S(1)} %pad_maximum_fusion.7), channel_id=1, source_target_pairs={{0,4},{4,0},{8,12},{12,8},{1,5},{5,1},{9,13},{13,9},{2,6},{6,2},{1... | collective-permute-start | bytes 1572872 | tf_op jit(solution)/shard_map/ppermute | solution.py:76
  95.4 0.9 pad_maximum_fusion.8
  96.3 3.8 %collective-permute-start.7 = (bf16[256,1024]{1,0:T(8,128)(2,1)}, bf16[256,1024]{1,0:T(8,128)(2,1)}, u32[]{:S(2)}, u32[]{:S(2)}) collective-permute-start(bf16[256,1024]{1,0:T(8,128)(2,1)} %pad_maximum_fusion.8), channel_id=1, source_target_pairs={{0,8},{4,12},{8,0},{12,4},{1,9},{5,13},{9,1},{13,5},{2,10},{6,14},... | collective-permute-start | bytes 1572872 | tf_op jit(solution)/shard_map/ppermute | solution.py:76
  100.1 0.0 copy-start.9
  100.1 0.9 pad_maximum_fusion.9
  101.0 3.7 %collective-permute-start.8 = (bf16[256,1024]{1,0:T(8,128)(2,1)}, bf16[256,1024]{1,0:T(8,128)(2,1)S(1)}, u32[]{:S(2)}, u32[]{:S(2)}) collective-permute-start(bf16[256,1024]{1,0:T(8,128)(2,1)} %pad_maximum_fusion.9), channel_id=1, source_target_pairs={{0,12},{4,8},{8,4},{12,0},{1,13},{5,9},{9,5},{13,1},{2,14},{6,10},... | collective-permute-start | bytes 1572872 | tf_op jit(solution)/shard_map/ppermute | solution.py:76
  104.7 20.1 %all-to-all-done.2 = bf16[32,8,1280]{2,1,0:T(8,128)(2,1)S(1)} async-done(((bf16[32,8,1280]{2,1,0:T(8,128)(2,1)}), bf16[32,8,1280]{2,1,0:T(8,128)(2,1)S(1)}, u32[]{:S(2)}, u32[]{:S(2)}) %all-to-all-start.2) | async-done | bytes 655392 | tf_op jit(solution)/shard_map/all_to_all | solution.py:118
  124.9 0.0 copy-start.8
  124.9 0.4 fusion.61
  125.3 0.0 copy-start.6
  125.3 0.0 copy-start.5
  125.4 0.4 fusion.23
  125.8 0.0 copy-start.4
  125.8 0.4 fusion.27
  126.2 0.1 copy-done.6
  126.3 0.3 fusion.47
  126.6 0.3 fusion.3
  127.0 0.1 copy.28
  127.1 0.7 fusion.36
  127.8 9.6 %all-to-all-start.3 = ((bf16[32,8,128]{2,1,0:T(8,128)(2,1)}), bf16[32,8,128]{2,1,0:T(8,128)(2,1)S(1)}, u32[]{:S(2)}, u32[]{:S(2)}) async-start(bf16[32,8,128]{2,1,0:T(8,128)(2,1)} %fusion.36), calls=%async_computation.3 | async-start | bytes 131072 | tf_op jit(solution)/shard_map/all_to_all | solution.py:131
  137.3 0.1 pad_maximum_fusion.6
  137.4 14.4 %all-to-all-done.3 = bf16[32,8,128]{2,1,0:T(8,128)(2,1)S(1)} async-done(((bf16[32,8,128]{2,1,0:T(8,128)(2,1)}), bf16[32,8,128]{2,1,0:T(8,128)(2,1)S(1)}, u32[]{:S(2)}, u32[]{:S(2)}) %all-to-all-start.3) | async-done | bytes 65568 | tf_op jit(solution)/shard_map/all_to_all | solution.py:131
  151.9 0.1 copy.29
  152.0 0.8 broadcast_in_dim.11
  152.8 3.8 %all-to-all-start.4 = ((bf16[8,256,128]{1,2,0:T(8,128)(2,1)}), bf16[8,256,128]{1,2,0:T(8,128)(2,1)S(1)}, u32[]{:S(2)}, u32[]{:S(2)}) async-start(bf16[8,256,128]{1,2,0:T(8,128)(2,1)} %broadcast_in_dim.11), calls=%async_computation.4 | async-start | bytes 1048576 | tf_op jit(solution)/shard_map/all_to_all | solution.py:134
  156.6 9.5 %all-to-all-done.4 = bf16[8,256,128]{1,2,0:T(8,128)(2,1)S(1)} async-done(((bf16[8,256,128]{1,2,0:T(8,128)(2,1)}), bf16[8,256,128]{1,2,0:T(8,128)(2,1)S(1)}, u32[]{:S(2)}, u32[]{:S(2)}) %all-to-all-start.4) | async-done | bytes 524320 | tf_op jit(solution)/shard_map/all_to_all | solution.py:134
  166.1 0.3 fusion.8
  166.4 0.3 convolution_add_fusion.2
  166.7 1.3 convolution_add_fusion.1
  168.1 0.3 fusion.2
  168.4 18.4 %all_to_all.30 = bf16[8,128,256]{2,1,0:T(8,128)(2,1)S(1)} all-to-all(bf16[8,128,256]{2,1,0:T(8,128)(2,1)S(1)} %bitcast.137), channel_id=1, replica_groups=mesh['y'=4,'zh'=4,'core'=2,'x'=4,'zl'=4] {'zl','core'}, dimensions={0} | all-to-all | bytes 1048576 | tf_op jit(solution)/shard_map/all_to_all | solution.py:139
  186.8 0.1 reduce
  186.9 0.7 pad_maximum_fusion.11
  (41 shorter events, 0.6 us)
Async XLA Ops:
  0.0 25.8 %copy-start.10 = (bf16[256,256]{1,0:T(8,128)(2,1)S(1)}, bf16[256,256]{1,0:T(8,128)(2,1)}, u32[]{:S(2)}) copy-start(bf16[256,256]{1,0:T(8,128)(2,1)} %param.13) | copy-start | bytes 393220
  0.0 25.8 %copy-start.11 = (bf16[256,256]{1,0:T(8,128)(2,1)S(1)}, bf16[256,256]{1,0:T(8,128)(2,1)}, u32[]{:S(2)}) copy-start(bf16[256,256]{1,0:T(8,128)(2,1)} %param.14) | copy-start | bytes 393220
  0.0 1.7 collective-permute-start
  2.6 36.5 %all-to-all-start = ((bf16[4,128,512]{2,1,0:T(8,128)(2,1)}), bf16[4,128,512]{2,1,0:T(8,128)(2,1)S(1)}, u32[]{:S(2)}, u32[]{:S(2)}) async-start(bf16[4,128,512]{2,1,0:T(8,128)(2,1)} %broadcast_in_dim.9), calls=%async_computation | async-start | bytes 1048576 | tf_op jit(solution)/shard_map/all_to_all | solution.py:68
  25.8 13.4 %collective-permute-start.1 = (bf16[256,512]{1,0:T(8,128)(2,1)S(1)}, bf16[256,512]{1,0:T(8,128)(2,1)S(1)}, u32[]{:S(2)}, u32[]{:S(2)}) collective-permute-start(bf16[256,512]{1,0:T(8,128)(2,1)S(1)} %pad_maximum_fusion.10), channel_id=1, source_target_pairs={{0,128},{128,0},{256,384},{384,256},{1,129},{129,1},{257,385},{385... | collective-permute-start | bytes 786440 | tf_op jit(solution)/shard_map/ppermute | solution.py:76
  40.7 29.3 %all-to-all-start.1 = ((bf16[4,512,512]{2,1,0:T(8,128)(2,1)}), bf16[4,512,512]{2,1,0:T(8,128)(2,1)S(1)}, u32[]{:S(2)}, u32[]{:S(2)}) async-start(bf16[4,512,512]{2,1,0:T(8,128)(2,1)} %broadcast_in_dim.10), calls=%async_computation.1 | async-start | bytes 4194304 | tf_op jit(solution)/shard_map/all_to_all | solution.py:68
  44.7 20.5 %copy-start.7 = (f32[2,128,256]{2,1,0:T(8,128)S(1)}, f32[2,128,256]{2,1,0:T(8,128)}, u32[]{:S(2)}) copy-start(f32[2,128,256]{2,1,0:T(8,128)} %param.16) | copy-start | bytes 786436
  44.7 11.7 %collective-permute-start.3 = (bf16[256,512]{1,0:T(8,128)(2,1)S(1)}, bf16[256,512]{1,0:T(8,128)(2,1)S(1)}, u32[]{:S(2)}, u32[]{:S(2)}) collective-permute-start(bf16[256,512]{1,0:T(8,128)(2,1)S(1)} %pad_maximum_fusion.10), channel_id=1, source_target_pairs={{0,384},{128,256},{256,128},{384,0},{1,385},{129,257},{257,129},{3... | collective-permute-start | bytes 786440 | tf_op jit(solution)/shard_map/ppermute | solution.py:76
  49.5 11.0 %collective-permute-start.2 = (bf16[256,512]{1,0:T(8,128)(2,1)S(1)}, bf16[256,512]{1,0:T(8,128)(2,1)S(1)}, u32[]{:S(2)}, u32[]{:S(2)}) collective-permute-start(bf16[256,512]{1,0:T(8,128)(2,1)S(1)} %collective-permute-done.1), channel_id=1, source_target_pairs={{0,384},{128,256},{256,128},{384,0},{1,385},{129,257},{257,129},{3... | collective-permute-start | bytes 786440 | tf_op jit(solution)/shard_map/ppermute | solution.py:76
  52.3 15.0 %collective-permute-start.4 = (bf16[2,256,512]{2,1,0:T(8,128)(2,1)}, bf16[2,256,512]{2,1,0:T(8,128)(2,1)}, u32[]{:S(2)}, u32[]{:S(2)}) collective-permute-start(bf16[2,256,512]{2,1,0:T(8,128)(2,1)} %pad_maximum_fusion.2), channel_id=1, source_target_pairs={{0,16},{16,0},{1,17},{17,1},{2,18},{18,2},{3,19},{19,3},{4,20},{20... | collective-permute-start | bytes 1572872 | tf_op jit(solution)/shard_map/ppermute | solution.py:76
  61.3 6.0 %collective-permute-start.5 = (bf16[2,256,512]{2,1,0:T(8,128)(2,1)}, bf16[2,256,512]{2,1,0:T(8,128)(2,1)}, u32[]{:S(2)}, u32[]{:S(2)}) collective-permute-start(bf16[2,256,512]{2,1,0:T(8,128)(2,1)} %pad_maximum_fusion.3), channel_id=1, source_target_pairs={{0,16},{16,0},{1,17},{17,1},{2,18},{18,2},{3,19},{19,3},{4,20},{20... | collective-permute-start | bytes 1572872 | tf_op jit(solution)/shard_map/ppermute | solution.py:76
  70.0 2.0 %copy-start.2 = (bf16[4,256,512]{2,1,0:T(8,128)(2,1)S(1)}, bf16[4,256,512]{2,1,0:T(8,128)(2,1)}, u32[]{:S(2)}) copy-start(bf16[4,256,512]{2,1,0:T(8,128)(2,1)} %pad_maximum_fusion) | copy-start | bytes 3145732
  73.9 50.8 %all-to-all-start.2 = ((bf16[32,8,1280]{2,1,0:T(8,128)(2,1)}), bf16[32,8,1280]{2,1,0:T(8,128)(2,1)S(1)}, u32[]{:S(2)}, u32[]{:S(2)}) async-start(bf16[32,8,1280]{2,1,0:T(8,128)(2,1)} %bitcast.16), calls=%async_computation.2 | async-start | bytes 1310720 | tf_op jit(solution)/shard_map/all_to_all | solution.py:118
  93.1 31.8 %copy-start.3 = (f32[512,256]{1,0:T(8,128)S(1)}, f32[512,256]{1,0:T(8,128)}, u32[]{:S(2)}) copy-start(f32[512,256]{1,0:T(8,128)} %constant.167) | copy-start | bytes 1572868
  93.1 44.3 %collective-permute-start.6 = (bf16[256,1024]{1,0:T(8,128)(2,1)S(1)}, bf16[256,1024]{1,0:T(8,128)(2,1)S(1)}, u32[]{:S(2)}, u32[]{:S(2)}) collective-permute-start(bf16[256,1024]{1,0:T(8,128)(2,1)S(1)} %pad_maximum_fusion.7), channel_id=1, source_target_pairs={{0,4},{4,0},{8,12},{12,8},{1,5},{5,1},{9,13},{13,9},{2,6},{6,2},{1... | collective-permute-start | bytes 1572872 | tf_op jit(solution)/shard_map/ppermute | solution.py:76
  96.3 29.0 %copy-start = (f32[256,128]{1,0:T(8,128)S(1)}, f32[256,128]{1,0:T(8,128)}, u32[]{:S(2)}) copy-start(f32[256,128]{1,0:T(8,128)} %constant.160.clone) | copy-start | bytes 393220
  96.3 29.0 %copy-start.1 = (f32[256,128]{1,0:T(8,128)S(1)}, f32[256,128]{1,0:T(8,128)}, u32[]{:S(2)}) copy-start(f32[256,128]{1,0:T(8,128)} %constant.159.clone) | copy-start | bytes 393220
  96.3 41.2 %collective-permute-start.7 = (bf16[256,1024]{1,0:T(8,128)(2,1)}, bf16[256,1024]{1,0:T(8,128)(2,1)}, u32[]{:S(2)}, u32[]{:S(2)}) collective-permute-start(bf16[256,1024]{1,0:T(8,128)(2,1)} %pad_maximum_fusion.8), channel_id=1, source_target_pairs={{0,8},{4,12},{8,0},{12,4},{1,9},{5,13},{9,1},{13,5},{2,10},{6,14},... | collective-permute-start | bytes 1572872 | tf_op jit(solution)/shard_map/ppermute | solution.py:76
  100.1 25.3 %copy-start.9 = (f32[128,256]{1,0:T(8,128)S(1)}, f32[128,256]{1,0:T(8,128)}, u32[]{:S(2)}) copy-start(f32[128,256]{1,0:T(8,128)} %constant.162.clone) | copy-start | bytes 393220
  101.0 36.5 %collective-permute-start.8 = (bf16[256,1024]{1,0:T(8,128)(2,1)}, bf16[256,1024]{1,0:T(8,128)(2,1)S(1)}, u32[]{:S(2)}, u32[]{:S(2)}) collective-permute-start(bf16[256,1024]{1,0:T(8,128)(2,1)} %pad_maximum_fusion.9), channel_id=1, source_target_pairs={{0,12},{4,8},{8,4},{12,0},{1,13},{5,9},{9,5},{13,1},{2,14},{6,10},... | collective-permute-start | bytes 1572872 | tf_op jit(solution)/shard_map/ppermute | solution.py:76
  124.9 1.0 copy-start.8
  125.3 1.0 copy-start.6
  125.3 1.3 copy-start.5
  125.8 11.5 %copy-start.4 = (bf16[256,256]{1,0:T(8,128)(2,1)S(1)}, bf16[256,256]{1,0:T(8,128)(2,1)}, u32[]{:S(2)}) copy-start(bf16[256,256]{1,0:T(8,128)(2,1)} %get-tuple-element.44) | copy-start | bytes 393220
  127.8 24.1 %all-to-all-start.3 = ((bf16[32,8,128]{2,1,0:T(8,128)(2,1)}), bf16[32,8,128]{2,1,0:T(8,128)(2,1)S(1)}, u32[]{:S(2)}, u32[]{:S(2)}) async-start(bf16[32,8,128]{2,1,0:T(8,128)(2,1)} %fusion.36), calls=%async_computation.3 | async-start | bytes 131072 | tf_op jit(solution)/shard_map/all_to_all | solution.py:131
  152.8 13.3 %all-to-all-start.4 = ((bf16[8,256,128]{1,2,0:T(8,128)(2,1)}), bf16[8,256,128]{1,2,0:T(8,128)(2,1)S(1)}, u32[]{:S(2)}, u32[]{:S(2)}) async-start(bf16[8,256,128]{1,2,0:T(8,128)(2,1)} %broadcast_in_dim.11), calls=%async_computation.4 | async-start | bytes 1048576 | tf_op jit(solution)/shard_map/all_to_all | solution.py:134

commit v4 on v3

--- a/solution.py
+++ b/solution.py
@@ -118,27 +118,26 @@
     packet = lax.all_to_all(packet, SEQ, 0, 0)
 
     held = after(out_weight, value)
-
-    def share(k):
-        return jnp.concatenate([lax.dynamic_slice_in_dim(held, ((column ^ k) * 4 + zl) * 512 + core * 256, 256, 1) for zl in range(4)], axis=1)
-
-    shares = [exchange(share(k), "x", k) if k else share(k) for k in range(4)]
+    own = lax.dynamic_slice_in_dim(held, column * 2048, 2048, 1)
+    half = {k: exchange(lax.dynamic_slice(held, (core * 128, (column ^ k) * 2048), (128, 2048)), "x", k) for k in (1, 2, 3)}
+    other = {k: exchange(half[k], "core", 1) for k in (1, 2, 3)}
 
     signal, gate = (summed(packet[:, :, at : at + 512]) for at in (0, 512))
     resp = packet[:, :, 1024:].astype(jnp.float32)
     resp = jnp.transpose(resp.reshape(N1, GROUP, 2, N2), (2, 0, 1, 3))
     hidden = (jax.nn.silu(gate) * convolve(signal, resp)).astype(jnp.bfloat16)
     hidden = lax.all_to_all(hidden, SEQ, 0, 0).reshape(256, 128)
-    hidden, shares = lax.optimization_barrier((hidden, shares))
+    hidden, other[1], half[3], half[2] = lax.optimization_barrier((hidden, other[1], half[3], half[2]))
 
-    hidden = lax.all_to_all(jnp.broadcast_to(hidden, (8, 256, 128)), ("x", "core"), 0, 0).reshape(4, 2, 256, 128)
-    total = 0.0
-    for k in range(4):
-        total = total + jnp.einsum("ect,cd->etd", pick(hidden, column ^ k), shares[k], preferred_element_type=jnp.float32)
-    total = jnp.transpose(total.astype(jnp.bfloat16).reshape(2, 128, 4, 256), (2, 0, 1, 3)).reshape(8, 128, 256)
-    total = lax.all_to_all(total, ("zl", "core"), 0, 0).reshape(4, 2, 128, 256)
-    total = total.astype(jnp.float32).sum(axis=0)
-    return jnp.concatenate([total[0], total[1]], axis=1).astype(jnp.bfloat16)
+    hidden = gather_over(hidden, "x")
+    total = jnp.einsum("ct,cd->td", pick(hidden, column), own, preferred_element_type=jnp.float32)
+    for k in (1, 3, 2):
+        rows = pick(hidden, column ^ k).reshape(2, 128, 128)
+        for part, weight in ((core, half[k]), (1 - core, other[k])):
+            total = total + jnp.einsum("ct,cd->td", pick(rows, part), weight, preferred_element_type=jnp.float32)
+    total = jnp.transpose(total.astype(jnp.bfloat16).reshape(128, 4, 512), (1, 0, 2))
+    total = lax.all_to_all(total, "zl", 0, 0)
+    return total.astype(jnp.float32).sum(axis=0).astype(jnp.bfloat16)
 
 
 def solution(mesh):

time: 189 us -> 186 us (0.984)
  waiting for transfers between devices: 50 us -> 41.2 us
  starting transfers between devices: 85.7 us -> 92.5 us
    all_to_all x1 -> x0, waiting for transfers between devices: 9.5 us -> none  [local(): lax.all_to_all(jnp.broadcast_to(hidden, (8, 256, 128)), ('x', 'core'), 0, 0)]
    ppermute x8 -> x11, starting transfers between devices: 27.6 us -> 34.8 us  [exchange(): lax.ppermute(block, axis, [(i, i ^ apart) for i in range(lax.axis_size(ax...]
    all_to_all x1, waiting for transfers between devices: 20.1 us -> 12.9 us  [local(): packet = lax.all_to_all(packet, SEQ, 0, 0)]
    ppermute x8 -> x11, waiting for transfers between devices: 4.05 us -> 10.2 us  [exchange(): lax.ppermute(block, axis, [(i, i ^ apart) for i in range(lax.axis_size(ax...]
    all_to_all x1 -> x0, starting transfers between devices: 3.79 us -> none  [local(): lax.all_to_all(jnp.broadcast_to(hidden, (8, 256, 128)), ('x', 'core'), 0, 0)]
    all_to_all x2 -> x3, starting transfers between devices: 26.5 us -> 29.9 us  [gather_over(): lax.all_to_all(jnp.broadcast_to(block, (count,) + block.shape), axis, 0, 0)]
    concatenate x5 -> x0, other arithmetic: 2.5 us -> none  [the longest x4 1.84 us: share(): jnp.concatenate([lax.dynamic_slice_in_dim(held, ((column ^ k) * 4 + zl) *...]
  transfers between devices with their start and end apart: 14 -> 17, of which waited for: 5 -> 6; matrix products, arithmetic and copies ran while one was open for 8% -> 8% of each run, Pallas kernels for 0% -> 0%
where the time goes in v4:
time: 186 us; the launch traced here: 185 us
  starting transfers between devices  92.5 us (50%)
  waiting for transfers between devices  41.2 us (22%)
  blocking collectives  18.1 us (10%)
  local copies, waits for them, and re-layouts  8.71 us (5%)
  other arithmetic  8.21 us (4%)
  between operations  8.2 us (4%)
  matrix products  8.13 us (4%)
    ppermute x11, starting transfers between devices, exchange(): lax.ppermute(block, axis, [(i, i ^ apart) for i in range(lax.axis_size(ax...  34.8 us
    all_to_all x3, starting transfers between devices, gather_over(): lax.all_to_all(jnp.broadcast_to(block, (count,) + block.shape), axis, 0, 0)  29.9 us
    all_to_all x1, blocking collectives, local(): total = lax.all_to_all(total, 'zl', 0, 0)  18.1 us
    all_to_all x1, starting transfers between devices, local(): packet = lax.all_to_all(packet, SEQ, 0, 0)  16.5 us
    all_to_all x1, waiting for transfers between devices, local(): hidden = lax.all_to_all(hidden, SEQ, 0, 0).reshape(256, 128)  14.5 us
    all_to_all x1, waiting for transfers between devices, local(): packet = lax.all_to_all(packet, SEQ, 0, 0)  12.9 us
    ppermute x11, waiting for transfers between devices, exchange(): lax.ppermute(block, axis, [(i, i ^ apart) for i in range(lax.axis_size(ax...  10.2 us
    all_to_all x1, starting transfers between devices, local(): hidden = lax.all_to_all(hidden, SEQ, 0, 0).reshape(256, 128)  9.54 us
  transfers between devices with their start and end apart: 17, of which 6 were waited for; matrix products, arithmetic and copies ran while one was open for 8% of the time, Pallas kernels for 0%

profile of v4, /device:TPU:1, one launch (start us, length us, event | category | flops | bytes accessed | tf_op | source)
XLA Modules:
  0.0 185.0 jit_solution(10569445073662587433)
XLA Ops:
  0.0 1.7 collective-permute-start
  1.7 0.8 broadcast_in_dim.9
  2.6 22.5 %all-to-all-start = ((bf16[4,128,512]{2,1,0:T(8,128)(2,1)}), bf16[4,128,512]{2,1,0:T(8,128)(2,1)S(1)}, u32[]{:S(2)}, u32[]{:S(2)}) async-start(bf16[4,128,512]{2,1,0:T(8,128)(2,1)} %broadcast_in_dim.9), calls=%async_computation | async-start | bytes 1048576 | tf_op jit(solution)/shard_map/all_to_all | solution.py:68
  25.1 0.7 constant_dynamic-slice_fusion.3
  25.8 3.2 %collective-permute-start.1 = (bf16[256,512]{1,0:T(8,128)(2,1)S(1)}, bf16[256,512]{1,0:T(8,128)(2,1)S(1)}, u32[]{:S(2)}, u32[]{:S(2)}) collective-permute-start(bf16[256,512]{1,0:T(8,128)(2,1)S(1)} %pad_maximum_fusion.6), channel_id=1, source_target_pairs={{0,128},{128,0},{256,384},{384,256},{1,129},{129,1},{257,385},{385... | collective-permute-start | bytes 786440 | tf_op jit(solution)/shard_map/ppermute | solution.py:76
  29.0 0.7 fusion.75
  37.2 1.8 all-to-all-done
  39.2 0.0 collective-permute-done.1
  39.2 1.5 broadcast_in_dim.10
  40.7 4.0 %all-to-all-start.1 = ((bf16[4,512,512]{2,1,0:T(8,128)(2,1)}), bf16[4,512,512]{2,1,0:T(8,128)(2,1)S(1)}, u32[]{:S(2)}, u32[]{:S(2)}) async-start(bf16[4,512,512]{2,1,0:T(8,128)(2,1)} %broadcast_in_dim.10), calls=%async_computation.1 | async-start | bytes 4194304 | tf_op jit(solution)/shard_map/all_to_all | solution.py:68
  44.7 4.8 %collective-permute-start.3 = (bf16[256,512]{1,0:T(8,128)(2,1)S(1)}, bf16[256,512]{1,0:T(8,128)(2,1)S(1)}, u32[]{:S(2)}, u32[]{:S(2)}) collective-permute-start(bf16[256,512]{1,0:T(8,128)(2,1)S(1)} %pad_maximum_fusion.6), channel_id=1, source_target_pairs={{0,384},{128,256},{256,128},{384,0},{1,385},{129,257},{257,129},{3... | collective-permute-start | bytes 786440 | tf_op jit(solution)/shard_map/ppermute | solution.py:76
  49.5 1.9 %collective-permute-start.2 = (bf16[256,512]{1,0:T(8,128)(2,1)S(1)}, bf16[256,512]{1,0:T(8,128)(2,1)S(1)}, u32[]{:S(2)}, u32[]{:S(2)}) collective-permute-start(bf16[256,512]{1,0:T(8,128)(2,1)S(1)} %collective-permute-done.1), channel_id=1, source_target_pairs={{0,384},{128,256},{256,128},{384,0},{1,385},{129,257},{257,129},{3... | collective-permute-start | bytes 786440 | tf_op jit(solution)/shard_map/ppermute | solution.py:76
  51.4 0.9 pad_maximum_fusion.2
  52.3 4.1 %collective-permute-start.4 = (bf16[2,256,512]{2,1,0:T(8,128)(2,1)}, bf16[2,256,512]{2,1,0:T(8,128)(2,1)}, u32[]{:S(2)}, u32[]{:S(2)}) collective-permute-start(bf16[2,256,512]{2,1,0:T(8,128)(2,1)} %pad_maximum_fusion.2), channel_id=1, source_target_pairs={{0,16},{16,0},{1,17},{17,1},{2,18},{18,2},{3,19},{19,3},{4,20},{20... | collective-permute-start | bytes 1572872 | tf_op jit(solution)/shard_map/ppermute | solution.py:76
  56.4 0.0 collective-permute-done.3
  56.4 4.0 %collective-permute-done.2 = bf16[256,512]{1,0:T(8,128)(2,1)S(1)} collective-permute-done((bf16[256,512]{1,0:T(8,128)(2,1)S(1)}, bf16[256,512]{1,0:T(8,128)(2,1)S(1)}, u32[]{:S(2)}, u32[]{:S(2)}) %collective-permute-start.2) | collective-permute-done | bytes 262176 | tf_op jit(solution)/shard_map/ppermute | solution.py:76
  60.4 0.9 pad_maximum_fusion.3
  61.3 3.8 %collective-permute-start.5 = (bf16[2,256,512]{2,1,0:T(8,128)(2,1)}, bf16[2,256,512]{2,1,0:T(8,128)(2,1)}, u32[]{:S(2)}, u32[]{:S(2)}) collective-permute-start(bf16[2,256,512]{2,1,0:T(8,128)(2,1)} %pad_maximum_fusion.3), channel_id=1, source_target_pairs={{0,16},{16,0},{1,17},{17,1},{2,18},{18,2},{3,19},{19,3},{4,20},{20... | collective-permute-start | bytes 1572872 | tf_op jit(solution)/shard_map/ppermute | solution.py:76
  65.3 0.2 fusion.19
  65.5 0.7 fusion.13
  66.2 1.1 pad_maximum_fusion
  67.3 0.0 collective-permute-done.4
  67.3 0.0 collective-permute-done.5
  67.3 1.6 dynamic-slice_select_fusion.3
  68.9 1.1 pad_maximum_fusion.1
  70.0 2.0 %convolution_bitcast_fusion = f32[512,512]{0,1:T(8,128)S(1)} fusion(bf16[4,256,512]{2,1,0:T(8,128)(2,1)} %pad_maximum_fusion.1, bf16[4,512,512]{2,1,0:T(8,128)(2,1)S(1)} %all-to-all-done.1), kind=kOutput, calls=%fused_computation.7 | convolution fusion | flops 536870912 | bytes 3145728 | tf_op jit(solution)/shard_map/xkc,xtk->ct/dot_general | solution.py:113
  72.0 0.7 fusion.6
  72.9 1.1 copy.22
  73.9 16.5 %all-to-all-start.2 = ((bf16[32,8,1280]{2,1,0:T(8,128)(2,1)}), bf16[32,8,1280]{2,1,0:T(8,128)(2,1)S(1)}, u32[]{:S(2)}, u32[]{:S(2)}) async-start(bf16[32,8,1280]{2,1,0:T(8,128)(2,1)} %bitcast.16), calls=%async_computation.2 | async-start | bytes 1310720 | tf_op jit(solution)/shard_map/all_to_all | solution.py:118
  90.4 0.0 copy-start.3
  90.5 2.6 %fusion.71 = (bf16[128,2048]{1,0:T(8,128)(2,1)}, bf16[128,2048]{1,0:T(8,128)(2,1)}, bf16[128,2048]{1,0:T(8,128)(2,1)S(1)}) fusion(bf16[256,8192]{1,0:T(8,128)(2,1)} %param.15, s32[]{:T(128)S(6)} %select_n.210, s32[]{:T(128)S(6)} %select_n.212, s32[]{:T(128)S(6)} %select_n.213, s32[]{:T(128)S(6)} %select_n.211), kind=kLoop, calls=%fused_computation.130 | loop fusion | bytes 3145744 | tf_op jit(solution)/shard_map/dynamic_slice | solution.py:122
  93.0 2.3 %collective-permute-start.6 = (bf16[128,2048]{1,0:T(8,128)(2,1)S(1)}, bf16[128,2048]{1,0:T(8,128)(2,1)S(1)}, u32[]{:S(2)}, u32[]{:S(2)}) collective-permute-start(bf16[128,2048]{1,0:T(8,128)(2,1)S(1)} %get-tuple-element.29), channel_id=1, source_target_pairs={{0,4},{4,0},{8,12},{12,8},{1,5},{5,1},{9,13},{13,9},{2,6},{6,2},{1... | collective-permute-start | bytes 1572872 | tf_op jit(solution)/shard_map/ppermute | solution.py:76
  95.4 2.8 %collective-permute-start.8 = (bf16[128,2048]{1,0:T(8,128)(2,1)}, bf16[128,2048]{1,0:T(8,128)(2,1)S(1)}, u32[]{:S(2)}, u32[]{:S(2)}) collective-permute-start(bf16[128,2048]{1,0:T(8,128)(2,1)} %get-tuple-element.27), channel_id=1, source_target_pairs={{0,12},{4,8},{8,4},{12,0},{1,13},{5,9},{9,5},{13,1},{2,14},{6,10},... | collective-permute-start | bytes 1572872 | tf_op jit(solution)/shard_map/ppermute | solution.py:76
  98.1 4.0 %collective-permute-start.9 = (bf16[128,2048]{1,0:T(8,128)(2,1)}, bf16[128,2048]{1,0:T(8,128)(2,1)S(1)}, u32[]{:S(2)}, u32[]{:S(2)}) collective-permute-start(bf16[128,2048]{1,0:T(8,128)(2,1)} %get-tuple-element.28), channel_id=1, source_target_pairs={{0,8},{4,12},{8,0},{12,4},{1,9},{5,13},{9,1},{13,5},{2,10},{6,14},... | collective-permute-start | bytes 1572872 | tf_op jit(solution)/shard_map/ppermute | solution.py:76
  102.2 6.2 %collective-permute-done.6 = bf16[128,2048]{1,0:T(8,128)(2,1)S(1)} collective-permute-done((bf16[128,2048]{1,0:T(8,128)(2,1)S(1)}, bf16[128,2048]{1,0:T(8,128)(2,1)S(1)}, u32[]{:S(2)}, u32[]{:S(2)}) %collective-permute-start.6) | collective-permute-done | bytes 524320 | tf_op jit(solution)/shard_map/ppermute | solution.py:76
  108.3 3.6 %collective-permute-start.7 = (bf16[128,2048]{1,0:T(8,128)(2,1)S(1)}, bf16[128,2048]{1,0:T(8,128)(2,1)S(1)}, u32[]{:S(2)}, u32[]{:S(2)}) collective-permute-start(bf16[128,2048]{1,0:T(8,128)(2,1)S(1)} %collective-permute-done.6), channel_id=1, source_target_pairs={{0,16},{16,0},{1,17},{17,1},{2,18},{18,2},{3,19},{19,3},{4,20},{20... | collective-permute-start | bytes 1572872 | tf_op jit(solution)/shard_map/ppermute | solution.py:76
  111.9 12.9 %all-to-all-done.2 = bf16[32,8,1280]{2,1,0:T(8,128)(2,1)S(1)} async-done(((bf16[32,8,1280]{2,1,0:T(8,128)(2,1)}), bf16[32,8,1280]{2,1,0:T(8,128)(2,1)S(1)}, u32[]{:S(2)}, u32[]{:S(2)}) %all-to-all-start.2) | async-done | bytes 655392 | tf_op jit(solution)/shard_map/all_to_all | solution.py:118
  125.0 0.0 copy-start.7
  125.0 0.4 fusion.76
  125.4 0.0 copy-start.5
  125.4 0.0 copy-start.4
  125.5 0.3 copy-done.8
  125.7 0.4 fusion.24
  126.2 0.4 fusion.28
  126.6 0.3 fusion.40
  126.9 0.3 fusion.7
  127.3 0.1 copy.26
  127.4 0.7 fusion.33
  128.1 9.5 %all-to-all-start.3 = ((bf16[32,8,128]{2,1,0:T(8,128)(2,1)}), bf16[32,8,128]{2,1,0:T(8,128)(2,1)S(1)}, u32[]{:S(2)}, u32[]{:S(2)}) async-start(bf16[32,8,128]{2,1,0:T(8,128)(2,1)} %fusion.33), calls=%async_computation.3 | async-start | bytes 131072 | tf_op jit(solution)/shard_map/all_to_all | solution.py:129
  137.7 14.5 %all-to-all-done.3 = bf16[32,8,128]{2,1,0:T(8,128)(2,1)S(1)} async-done(((bf16[32,8,128]{2,1,0:T(8,128)(2,1)}), bf16[32,8,128]{2,1,0:T(8,128)(2,1)S(1)}, u32[]{:S(2)}, u32[]{:S(2)}) %all-to-all-start.3) | async-done | bytes 65568 | tf_op jit(solution)/shard_map/all_to_all | solution.py:129
  152.2 0.7 broadcast_in_dim.11
  152.9 3.4 %all-to-all-start.4 = ((bf16[4,256,128]{2,1,0:T(8,128)(2,1)}), bf16[4,256,128]{2,1,0:T(8,128)(2,1)S(1)}, u32[]{:S(2)}, u32[]{:S(2)}) async-start(bf16[4,256,128]{2,1,0:T(8,128)(2,1)} %broadcast_in_dim.11), calls=%async_computation.4 | async-start | bytes 524288 | tf_op jit(solution)/shard_map/all_to_all | solution.py:68
  156.4 2.3 %collective-permute-start.10 = (bf16[128,2048]{1,0:T(8,128)(2,1)S(1)}, bf16[128,2048]{1,0:T(8,128)(2,1)S(1)}, u32[]{:S(2)}, u32[]{:S(2)}) collective-permute-start(bf16[128,2048]{1,0:T(8,128)(2,1)S(1)} %collective-permute-done.8), channel_id=1, source_target_pairs={{0,16},{16,0},{1,17},{17,1},{2,18},{18,2},{3,19},{19,3},{4,20},{20... | collective-permute-start | bytes 1572872 | tf_op jit(solution)/shard_map/ppermute | solution.py:76
  158.7 2.0 %collective-permute-start.11 = (bf16[128,2048]{1,0:T(8,128)(2,1)S(1)}, bf16[128,2048]{1,0:T(8,128)(2,1)S(1)}, u32[]{:S(2)}, u32[]{:S(2)}) collective-permute-start(bf16[128,2048]{1,0:T(8,128)(2,1)S(1)} %collective-permute-done.9), channel_id=1, source_target_pairs={{0,16},{16,0},{1,17},{17,1},{2,18},{18,2},{3,19},{19,3},{4,20},{20... | collective-permute-start | bytes 1572872 | tf_op jit(solution)/shard_map/ppermute | solution.py:76
  160.7 1.7 all-to-all-done.4
  162.4 0.3 fusion.52
  162.7 0.3 fusion.48
  163.1 0.3 fusion.50
  163.4 0.3 fusion.46
  163.8 1.6 fusion.8
  165.3 0.3 convolution_add_fusion.1
  165.7 0.5 fusion.4
  166.2 18.1 %all_to_all.30 = bf16[4,128,512]{2,1,0:T(8,128)(2,1)S(1)} all-to-all(bf16[4,128,512]{2,1,0:T(8,128)(2,1)S(1)} %bitcast.132), channel_id=1, replica_groups=mesh['y'=4,'zh'=4,'core'=2,'x'=4,'zl'=4] {'zl'}, dimensions={0} | all-to-all | bytes 1048576 | tf_op jit(solution)/shard_map/all_to_all | solution.py:139
  184.3 0.7 reduce_sum.32
  (42 shorter events, 0.6 us)
Async XLA Ops:
  0.0 25.8 %copy-start.9 = (bf16[256,256]{1,0:T(8,128)(2,1)S(1)}, bf16[256,256]{1,0:T(8,128)(2,1)}, u32[]{:S(2)}) copy-start(bf16[256,256]{1,0:T(8,128)(2,1)} %param.13) | copy-start | bytes 393220
  0.0 25.8 %copy-start.10 = (bf16[256,256]{1,0:T(8,128)(2,1)S(1)}, bf16[256,256]{1,0:T(8,128)(2,1)}, u32[]{:S(2)}) copy-start(bf16[256,256]{1,0:T(8,128)(2,1)} %param.14) | copy-start | bytes 393220
  0.0 1.7 collective-permute-start
  2.6 36.5 %all-to-all-start = ((bf16[4,128,512]{2,1,0:T(8,128)(2,1)}), bf16[4,128,512]{2,1,0:T(8,128)(2,1)S(1)}, u32[]{:S(2)}, u32[]{:S(2)}) async-start(bf16[4,128,512]{2,1,0:T(8,128)(2,1)} %broadcast_in_dim.9), calls=%async_computation | async-start | bytes 1048576 | tf_op jit(solution)/shard_map/all_to_all | solution.py:68
  25.8 13.4 %collective-permute-start.1 = (bf16[256,512]{1,0:T(8,128)(2,1)S(1)}, bf16[256,512]{1,0:T(8,128)(2,1)S(1)}, u32[]{:S(2)}, u32[]{:S(2)}) collective-permute-start(bf16[256,512]{1,0:T(8,128)(2,1)S(1)} %pad_maximum_fusion.6), channel_id=1, source_target_pairs={{0,128},{128,0},{256,384},{384,256},{1,129},{129,1},{257,385},{385... | collective-permute-start | bytes 786440 | tf_op jit(solution)/shard_map/ppermute | solution.py:76
  40.7 29.3 %all-to-all-start.1 = ((bf16[4,512,512]{2,1,0:T(8,128)(2,1)}), bf16[4,512,512]{2,1,0:T(8,128)(2,1)S(1)}, u32[]{:S(2)}, u32[]{:S(2)}) async-start(bf16[4,512,512]{2,1,0:T(8,128)(2,1)} %broadcast_in_dim.10), calls=%async_computation.1 | async-start | bytes 4194304 | tf_op jit(solution)/shard_map/all_to_all | solution.py:68
  44.7 20.5 %copy-start.6 = (f32[2,128,256]{2,1,0:T(8,128)S(1)}, f32[2,128,256]{2,1,0:T(8,128)}, u32[]{:S(2)}) copy-start(f32[2,128,256]{2,1,0:T(8,128)} %param.16) | copy-start | bytes 786436
  44.7 11.7 %collective-permute-start.3 = (bf16[256,512]{1,0:T(8,128)(2,1)S(1)}, bf16[256,512]{1,0:T(8,128)(2,1)S(1)}, u32[]{:S(2)}, u32[]{:S(2)}) collective-permute-start(bf16[256,512]{1,0:T(8,128)(2,1)S(1)} %pad_maximum_fusion.6), channel_id=1, source_target_pairs={{0,384},{128,256},{256,128},{384,0},{1,385},{129,257},{257,129},{3... | collective-permute-start | bytes 786440 | tf_op jit(solution)/shard_map/ppermute | solution.py:76
  49.5 11.0 %collective-permute-start.2 = (bf16[256,512]{1,0:T(8,128)(2,1)S(1)}, bf16[256,512]{1,0:T(8,128)(2,1)S(1)}, u32[]{:S(2)}, u32[]{:S(2)}) collective-permute-start(bf16[256,512]{1,0:T(8,128)(2,1)S(1)} %collective-permute-done.1), channel_id=1, source_target_pairs={{0,384},{128,256},{256,128},{384,0},{1,385},{129,257},{257,129},{3... | collective-permute-start | bytes 786440 | tf_op jit(solution)/shard_map/ppermute | solution.py:76
  52.3 15.0 %collective-permute-start.4 = (bf16[2,256,512]{2,1,0:T(8,128)(2,1)}, bf16[2,256,512]{2,1,0:T(8,128)(2,1)}, u32[]{:S(2)}, u32[]{:S(2)}) collective-permute-start(bf16[2,256,512]{2,1,0:T(8,128)(2,1)} %pad_maximum_fusion.2), channel_id=1, source_target_pairs={{0,16},{16,0},{1,17},{17,1},{2,18},{18,2},{3,19},{19,3},{4,20},{20... | collective-permute-start | bytes 1572872 | tf_op jit(solution)/shard_map/ppermute | solution.py:76
  61.3 6.0 %collective-permute-start.5 = (bf16[2,256,512]{2,1,0:T(8,128)(2,1)}, bf16[2,256,512]{2,1,0:T(8,128)(2,1)}, u32[]{:S(2)}, u32[]{:S(2)}) collective-permute-start(bf16[2,256,512]{2,1,0:T(8,128)(2,1)} %pad_maximum_fusion.3), channel_id=1, source_target_pairs={{0,16},{16,0},{1,17},{17,1},{2,18},{18,2},{3,19},{19,3},{4,20},{20... | collective-permute-start | bytes 1572872 | tf_op jit(solution)/shard_map/ppermute | solution.py:76
  70.0 2.0 %copy-start.2 = (bf16[4,256,512]{2,1,0:T(8,128)(2,1)S(1)}, bf16[4,256,512]{2,1,0:T(8,128)(2,1)}, u32[]{:S(2)}) copy-start(bf16[4,256,512]{2,1,0:T(8,128)(2,1)} %pad_maximum_fusion) | copy-start | bytes 3145732
  73.9 50.9 %all-to-all-start.2 = ((bf16[32,8,1280]{2,1,0:T(8,128)(2,1)}), bf16[32,8,1280]{2,1,0:T(8,128)(2,1)S(1)}, u32[]{:S(2)}, u32[]{:S(2)}) async-start(bf16[32,8,1280]{2,1,0:T(8,128)(2,1)} %bitcast.16), calls=%async_computation.2 | async-start | bytes 1310720 | tf_op jit(solution)/shard_map/all_to_all | solution.py:118
  90.4 34.5 %copy-start.3 = (f32[512,256]{1,0:T(8,128)S(1)}, f32[512,256]{1,0:T(8,128)}, u32[]{:S(2)}) copy-start(f32[512,256]{1,0:T(8,128)} %constant.181) | copy-start | bytes 1572868
  93.0 32.3 %copy-start = (f32[256,128]{1,0:T(8,128)S(1)}, f32[256,128]{1,0:T(8,128)}, u32[]{:S(2)}) copy-start(f32[256,128]{1,0:T(8,128)} %constant.173.clone) | copy-start | bytes 393220
  93.0 32.4 %copy-start.1 = (f32[256,128]{1,0:T(8,128)S(1)}, f32[256,128]{1,0:T(8,128)}, u32[]{:S(2)}) copy-start(f32[256,128]{1,0:T(8,128)} %constant.174.clone) | copy-start | bytes 393220
  93.0 15.3 %collective-permute-start.6 = (bf16[128,2048]{1,0:T(8,128)(2,1)S(1)}, bf16[128,2048]{1,0:T(8,128)(2,1)S(1)}, u32[]{:S(2)}, u32[]{:S(2)}) collective-permute-start(bf16[128,2048]{1,0:T(8,128)(2,1)S(1)} %get-tuple-element.29), channel_id=1, source_target_pairs={{0,4},{4,0},{8,12},{12,8},{1,5},{5,1},{9,13},{13,9},{2,6},{6,2},{1... | collective-permute-start | bytes 1572872 | tf_op jit(solution)/shard_map/ppermute | solution.py:76
  95.4 42.3 %collective-permute-start.8 = (bf16[128,2048]{1,0:T(8,128)(2,1)}, bf16[128,2048]{1,0:T(8,128)(2,1)S(1)}, u32[]{:S(2)}, u32[]{:S(2)}) collective-permute-start(bf16[128,2048]{1,0:T(8,128)(2,1)} %get-tuple-element.27), channel_id=1, source_target_pairs={{0,12},{4,8},{8,4},{12,0},{1,13},{5,9},{9,5},{13,1},{2,14},{6,10},... | collective-permute-start | bytes 1572872 | tf_op jit(solution)/shard_map/ppermute | solution.py:76
  98.1 39.5 %collective-permute-start.9 = (bf16[128,2048]{1,0:T(8,128)(2,1)}, bf16[128,2048]{1,0:T(8,128)(2,1)S(1)}, u32[]{:S(2)}, u32[]{:S(2)}) collective-permute-start(bf16[128,2048]{1,0:T(8,128)(2,1)} %get-tuple-element.28), channel_id=1, source_target_pairs={{0,8},{4,12},{8,0},{12,4},{1,9},{5,13},{9,1},{13,5},{2,10},{6,14},... | collective-permute-start | bytes 1572872 | tf_op jit(solution)/shard_map/ppermute | solution.py:76
  108.3 29.3 %collective-permute-start.7 = (bf16[128,2048]{1,0:T(8,128)(2,1)S(1)}, bf16[128,2048]{1,0:T(8,128)(2,1)S(1)}, u32[]{:S(2)}, u32[]{:S(2)}) collective-permute-start(bf16[128,2048]{1,0:T(8,128)(2,1)S(1)} %collective-permute-done.6), channel_id=1, source_target_pairs={{0,16},{16,0},{1,17},{17,1},{2,18},{18,2},{3,19},{19,3},{4,20},{20... | collective-permute-start | bytes 1572872 | tf_op jit(solution)/shard_map/ppermute | solution.py:76
  124.8 0.9 copy-start.8
  125.0 1.2 copy-start.7
  125.4 1.2 copy-start.5
  125.4 1.5 copy-start.4
  128.1 24.1 %all-to-all-start.3 = ((bf16[32,8,128]{2,1,0:T(8,128)(2,1)}), bf16[32,8,128]{2,1,0:T(8,128)(2,1)S(1)}, u32[]{:S(2)}, u32[]{:S(2)}) async-start(bf16[32,8,128]{2,1,0:T(8,128)(2,1)} %fusion.33), calls=%async_computation.3 | async-start | bytes 131072 | tf_op jit(solution)/shard_map/all_to_all | solution.py:129
  152.9 9.5 %all-to-all-start.4 = ((bf16[4,256,128]{2,1,0:T(8,128)(2,1)}), bf16[4,256,128]{2,1,0:T(8,128)(2,1)S(1)}, u32[]{:S(2)}, u32[]{:S(2)}) async-start(bf16[4,256,128]{2,1,0:T(8,128)(2,1)} %broadcast_in_dim.11), calls=%async_computation.4 | async-start | bytes 524288 | tf_op jit(solution)/shard_map/all_to_all | solution.py:68
  156.4 6.7 %collective-permute-start.10 = (bf16[128,2048]{1,0:T(8,128)(2,1)S(1)}, bf16[128,2048]{1,0:T(8,128)(2,1)S(1)}, u32[]{:S(2)}, u32[]{:S(2)}) collective-permute-start(bf16[128,2048]{1,0:T(8,128)(2,1)S(1)} %collective-permute-done.8), channel_id=1, source_target_pairs={{0,16},{16,0},{1,17},{17,1},{2,18},{18,2},{3,19},{19,3},{4,20},{20... | collective-permute-start | bytes 1572872 | tf_op jit(solution)/shard_map/ppermute | solution.py:76
  158.7 4.7 %collective-permute-start.11 = (bf16[128,2048]{1,0:T(8,128)(2,1)S(1)}, bf16[128,2048]{1,0:T(8,128)(2,1)S(1)}, u32[]{:S(2)}, u32[]{:S(2)}) collective-permute-start(bf16[128,2048]{1,0:T(8,128)(2,1)S(1)} %collective-permute-done.9), channel_id=1, source_target_pairs={{0,16},{16,0},{1,17},{17,1},{2,18},{18,2},{3,19},{19,3},{4,20},{20... | collective-permute-start | bytes 1572872 | tf_op jit(solution)/shard_map/ppermute | solution.py:76

commit v5 on v4

--- a/solution.py
+++ b/solution.py
@@ -72,6 +72,13 @@
     return lax.optimization_barrier((block, earlier))[0]
 
 
+def choose(values, index):
+    chosen = jnp.int32(values[0])
+    for at, value in enumerate(values[1:], 1):
+        chosen = jnp.where(index == at, jnp.int32(value), chosen)
+    return chosen
+
+
 def exchange(block, axis, apart):
     return lax.ppermute(block, axis, [(i, i ^ apart) for i in range(lax.axis_size(axis))])
 
@@ -90,10 +97,10 @@
     swap = [(t * 4 + b, b * 4 + ARRIVALS[b].index(t)) for t in range(4) for b in range(4)]
     swapped = lax.ppermute(tokens, ("zh", "zl"), swap)
     swapped = jnp.where(core == 0, swapped, jnp.concatenate([swapped[:, 256:], swapped[:, :256]], axis=1))
-    near = gather_over(swapped, "zl")
-    places = jnp.asarray(np.argsort(np.array(ARRIVALS), axis=1), jnp.int32)[lax.axis_index("zh")]
-    near = jnp.concatenate([pick(near, places[t]) for t in range(4)])
-    both = after(jnp.concatenate([value_weight, gate_weight], axis=1), swapped)
+    near = lax.all_gather(swapped, "zl")
+    high_z = lax.axis_index("zh")
+    near = jnp.concatenate([pick(near, choose([order.index(t) for order in ARRIVALS], high_z)) for t in range(4)])
+    both = jnp.concatenate([value_weight, gate_weight], axis=1)
     parts = [both, exchange(both, "y", 1)]
     near, parts[1] = lax.optimization_barrier((near, parts[1]))
     parts += [exchange(parts[1], "y", 3), exchange(both, "y", 3)]

time: 186 us -> 182 us (0.978)
  blocking collectives: 18.1 us -> 43.7 us
  starting transfers between devices: 92.5 us -> 75.7 us
  between operations: 8.2 us -> 0.71 us
  waiting for transfers between devices: 41.2 us -> 35.8 us
    all_gather x0 -> x1, blocking collectives: none -> 25.2 us  [local(): near = lax.all_gather(swapped, 'zl')]
    all_to_all x3 -> x2, starting transfers between devices: 29.9 us -> 7.42 us  [gather_over(): lax.all_to_all(jnp.broadcast_to(block, (count,) + block.shape), axis, 0, 0)]
    ppermute x11, starting transfers between devices: 34.8 us -> 41.9 us  [exchange(): lax.ppermute(block, axis, [(i, i ^ apart) for i in range(lax.axis_size(ax...]
    ppermute x11, waiting for transfers between devices: 10.2 us -> 6.21 us  [exchange(): lax.ppermute(block, axis, [(i, i ^ apart) for i in range(lax.axis_size(ax...]
  transfers between devices with their start and end apart: 17 -> 16, of which waited for: 6 -> 4; matrix products, arithmetic and copies ran while one was open for 8% -> 8% of each run, Pallas kernels for 0% -> 0%
where the time goes in v5:
time: 182 us; the launch traced here: 181 us
  starting transfers between devices  75.7 us (42%)
  blocking collectives  43.7 us (24%)
  waiting for transfers between devices  35.8 us (20%)
  local copies, waits for them, and re-layouts  8.42 us (5%)
  other arithmetic  8.18 us (4%)
  matrix products  8.15 us (4%)
    ppermute x11, starting transfers between devices, exchange(): lax.ppermute(block, axis, [(i, i ^ apart) for i in range(lax.axis_size(ax...  41.9 us
    all_gather x1, blocking collectives, local(): near = lax.all_gather(swapped, 'zl')  25.2 us
    all_to_all x1, blocking collectives, local(): total = lax.all_to_all(total, 'zl', 0, 0)  18.4 us
    all_to_all x1, starting transfers between devices, local(): packet = lax.all_to_all(packet, SEQ, 0, 0)  15.4 us
    all_to_all x1, waiting for transfers between devices, local(): hidden = lax.all_to_all(hidden, SEQ, 0, 0).reshape(256, 128)  14.7 us
    all_to_all x1, waiting for transfers between devices, local(): packet = lax.all_to_all(packet, SEQ, 0, 0)  13.2 us
    all_to_all x1, starting transfers between devices, local(): hidden = lax.all_to_all(hidden, SEQ, 0, 0).reshape(256, 128)  9.48 us
    all_to_all x2, starting transfers between devices, gather_over(): lax.all_to_all(jnp.broadcast_to(block, (count,) + block.shape), axis, 0, 0)  7.42 us
  transfers between devices with their start and end apart: 16, of which 4 were waited for; matrix products, arithmetic and copies ran while one was open for 8% of the time, Pallas kernels for 0%

profile of v5, /device:TPU:1, one launch (start us, length us, event | category | flops | bytes accessed | tf_op | source)
XLA Modules:
  0.0 180.6 jit_solution(7921896227638713124)
XLA Ops:
  0.0 1.6 collective-permute-start
  1.6 0.9 constant_dynamic-update-slice_fusion.1
  2.5 0.9 constant_dynamic-update-slice_fusion
  3.4 4.0 %collective-permute-start.1 = (bf16[256,512]{1,0:T(8,128)(2,1)S(1)}, bf16[256,512]{1,0:T(8,128)(2,1)S(1)}, u32[]{:S(2)}, u32[]{:S(2)}) collective-permute-start(bf16[256,512]{1,0:T(8,128)(2,1)S(1)} %constant_dynamic-update-slice_fusion), channel_id=1, source_target_pairs={{0,128},{128,0},{256,384},{384,256},{1,129},{129,1},{257,385},{385... | collective-permute-start | bytes 786440 | tf_op jit(solution)/shard_map/ppermute | solution.py:83
  7.5 0.0 collective-permute-done
  7.5 25.2 %all-gather = bf16[512,512]{1,0:T(8,128)(2,1)S(1)} all-gather(bf16[128,512]{1,0:T(8,128)(2,1)S(1)} %maximum_select_fusion), channel_id=2, replica_groups=mesh['y'=4,'zh'=4,'core'=2,'x'=4,'zl'=4] {'zl'}, dimensions={0}, use_global_device_ids=true | all-gather | bytes 655360 | tf_op jit(solution)/shard_map/all_gather | solution.py:100
  32.9 1.5 broadcast_in_dim.6
  34.4 4.0 %all-to-all-start = ((bf16[4,512,512]{2,1,0:T(8,128)(2,1)}), bf16[4,512,512]{2,1,0:T(8,128)(2,1)S(1)}, u32[]{:S(2)}, u32[]{:S(2)}) async-start(bf16[4,512,512]{2,1,0:T(8,128)(2,1)} %broadcast_in_dim.6), calls=%async_computation | async-start | bytes 4194304 | tf_op jit(solution)/shard_map/all_to_all | solution.py:68
  38.4 4.7 %collective-permute-start.3 = (bf16[256,512]{1,0:T(8,128)(2,1)S(1)}, bf16[256,512]{1,0:T(8,128)(2,1)S(1)}, u32[]{:S(2)}, u32[]{:S(2)}) collective-permute-start(bf16[256,512]{1,0:T(8,128)(2,1)S(1)} %constant_dynamic-update-slice_fusion), channel_id=1, source_target_pairs={{0,384},{128,256},{256,128},{384,0},{1,385},{129,257},{257,129},{3... | collective-permute-start | bytes 786440 | tf_op jit(solution)/shard_map/ppermute | solution.py:83
  43.1 1.9 %collective-permute-start.2 = (bf16[256,512]{1,0:T(8,128)(2,1)S(1)}, bf16[256,512]{1,0:T(8,128)(2,1)S(1)}, u32[]{:S(2)}, u32[]{:S(2)}) collective-permute-start(bf16[256,512]{1,0:T(8,128)(2,1)S(1)} %collective-permute-done.1), channel_id=1, source_target_pairs={{0,384},{128,256},{256,128},{384,0},{1,385},{129,257},{257,129},{3... | collective-permute-start | bytes 786440 | tf_op jit(solution)/shard_map/ppermute | solution.py:83
  45.1 0.9 pad_maximum_fusion.2
  45.9 7.8 %collective-permute-start.4 = (bf16[2,256,512]{2,1,0:T(8,128)(2,1)}, bf16[2,256,512]{2,1,0:T(8,128)(2,1)}, u32[]{:S(2)}, u32[]{:S(2)}) collective-permute-start(bf16[2,256,512]{2,1,0:T(8,128)(2,1)} %pad_maximum_fusion.2), channel_id=1, source_target_pairs={{0,16},{16,0},{1,17},{17,1},{2,18},{18,2},{3,19},{19,3},{4,20},{20... | collective-permute-start | bytes 1572872 | tf_op jit(solution)/shard_map/ppermute | solution.py:83
  53.7 0.0 collective-permute-done.3
  53.8 0.9 pad_maximum_fusion.3
  54.6 6.4 %collective-permute-start.5 = (bf16[2,256,512]{2,1,0:T(8,128)(2,1)}, bf16[2,256,512]{2,1,0:T(8,128)(2,1)}, u32[]{:S(2)}, u32[]{:S(2)}) collective-permute-start(bf16[2,256,512]{2,1,0:T(8,128)(2,1)} %pad_maximum_fusion.3), channel_id=1, source_target_pairs={{0,16},{16,0},{1,17},{17,1},{2,18},{18,2},{3,19},{19,3},{4,20},{20... | collective-permute-start | bytes 1572872 | tf_op jit(solution)/shard_map/ppermute | solution.py:83
  61.2 0.2 fusion.19
  61.4 0.7 fusion.13
  62.1 1.1 pad_maximum_fusion
  63.2 0.0 collective-permute-done.4
  63.2 1.6 dynamic-slice_select_fusion.3
  64.8 1.1 pad_maximum_fusion.1
  65.9 0.0 all-to-all-done
  65.9 2.0 %convolution_bitcast_fusion = f32[512,512]{0,1:T(8,128)S(1)} fusion(bf16[4,256,512]{2,1,0:T(8,128)(2,1)} %pad_maximum_fusion.1, bf16[4,512,512]{2,1,0:T(8,128)(2,1)S(1)} %all-to-all-done), kind=kOutput, calls=%fused_computation.7 | convolution fusion | flops 536870912 | bytes 3145728 | tf_op jit(solution)/shard_map/xkc,xtk->ct/dot_general | solution.py:120
  68.0 0.7 fusion.6
  68.8 1.1 copy.21
  69.9 15.4 %all-to-all-start.1 = ((bf16[32,8,1280]{2,1,0:T(8,128)(2,1)}), bf16[32,8,1280]{2,1,0:T(8,128)(2,1)S(1)}, u32[]{:S(2)}, u32[]{:S(2)}) async-start(bf16[32,8,1280]{2,1,0:T(8,128)(2,1)} %bitcast.13), calls=%async_computation.1 | async-start | bytes 1310720 | tf_op jit(solution)/shard_map/all_to_all | solution.py:125
  85.3 0.0 copy-start.3
  85.3 2.6 %fusion.71 = (bf16[128,2048]{1,0:T(8,128)(2,1)}, bf16[128,2048]{1,0:T(8,128)(2,1)}, bf16[128,2048]{1,0:T(8,128)(2,1)S(1)}) fusion(bf16[256,8192]{1,0:T(8,128)(2,1)} %param.14, s32[]{:T(128)S(6)} %select_n.242, s32[]{:T(128)S(6)} %select_n.244, s32[]{:T(128)S(6)} %select_n.245, s32[]{:T(128)S(6)} %select_n.243), kind=kLoop, calls=%fused_computation.130 | loop fusion | bytes 3145744 | tf_op jit(solution)/shard_map/dynamic_slice | solution.py:129
  87.9 2.3 %collective-permute-start.6 = (bf16[128,2048]{1,0:T(8,128)(2,1)S(1)}, bf16[128,2048]{1,0:T(8,128)(2,1)S(1)}, u32[]{:S(2)}, u32[]{:S(2)}) collective-permute-start(bf16[128,2048]{1,0:T(8,128)(2,1)S(1)} %get-tuple-element.27), channel_id=1, source_target_pairs={{0,4},{4,0},{8,12},{12,8},{1,5},{5,1},{9,13},{13,9},{2,6},{6,2},{1... | collective-permute-start | bytes 1572872 | tf_op jit(solution)/shard_map/ppermute | solution.py:83
  90.2 2.7 %collective-permute-start.8 = (bf16[128,2048]{1,0:T(8,128)(2,1)}, bf16[128,2048]{1,0:T(8,128)(2,1)S(1)}, u32[]{:S(2)}, u32[]{:S(2)}) collective-permute-start(bf16[128,2048]{1,0:T(8,128)(2,1)} %get-tuple-element.25), channel_id=1, source_target_pairs={{0,12},{4,8},{8,4},{12,0},{1,13},{5,9},{9,5},{13,1},{2,14},{6,10},... | collective-permute-start | bytes 1572872 | tf_op jit(solution)/shard_map/ppermute | solution.py:83
  93.0 4.0 %collective-permute-start.9 = (bf16[128,2048]{1,0:T(8,128)(2,1)}, bf16[128,2048]{1,0:T(8,128)(2,1)S(1)}, u32[]{:S(2)}, u32[]{:S(2)}) collective-permute-start(bf16[128,2048]{1,0:T(8,128)(2,1)} %get-tuple-element.26), channel_id=1, source_target_pairs={{0,8},{4,12},{8,0},{12,4},{1,9},{5,13},{9,1},{13,5},{2,10},{6,14},... | collective-permute-start | bytes 1572872 | tf_op jit(solution)/shard_map/ppermute | solution.py:83
  97.0 6.2 %collective-permute-done.6 = bf16[128,2048]{1,0:T(8,128)(2,1)S(1)} collective-permute-done((bf16[128,2048]{1,0:T(8,128)(2,1)S(1)}, bf16[128,2048]{1,0:T(8,128)(2,1)S(1)}, u32[]{:S(2)}, u32[]{:S(2)}) %collective-permute-start.6) | collective-permute-done | bytes 524320 | tf_op jit(solution)/shard_map/ppermute | solution.py:83
  103.2 3.6 %collective-permute-start.7 = (bf16[128,2048]{1,0:T(8,128)(2,1)S(1)}, bf16[128,2048]{1,0:T(8,128)(2,1)S(1)}, u32[]{:S(2)}, u32[]{:S(2)}) collective-permute-start(bf16[128,2048]{1,0:T(8,128)(2,1)S(1)} %collective-permute-done.6), channel_id=1, source_target_pairs={{0,16},{16,0},{1,17},{17,1},{2,18},{18,2},{3,19},{19,3},{4,20},{20... | collective-permute-start | bytes 1572872 | tf_op jit(solution)/shard_map/ppermute | solution.py:83
  106.8 13.2 %all-to-all-done.1 = bf16[32,8,1280]{2,1,0:T(8,128)(2,1)S(1)} async-done(((bf16[32,8,1280]{2,1,0:T(8,128)(2,1)}), bf16[32,8,1280]{2,1,0:T(8,128)(2,1)S(1)}, u32[]{:S(2)}, u32[]{:S(2)}) %all-to-all-start.1) | async-done | bytes 655392 | tf_op jit(solution)/shard_map/all_to_all | solution.py:125
  120.1 0.0 copy-start.7
  120.1 0.4 fusion.75
  120.5 0.0 copy-start.5
  120.6 0.0 copy-start.4
  120.6 0.3 copy-done.8
  120.9 0.4 fusion.24
  121.3 0.4 fusion.28
  121.7 0.3 fusion.40
  122.0 0.3 fusion.7
  122.4 0.1 copy.25
  122.5 0.7 fusion.33
  123.2 9.5 %all-to-all-start.2 = ((bf16[32,8,128]{2,1,0:T(8,128)(2,1)}), bf16[32,8,128]{2,1,0:T(8,128)(2,1)S(1)}, u32[]{:S(2)}, u32[]{:S(2)}) async-start(bf16[32,8,128]{2,1,0:T(8,128)(2,1)} %fusion.33), calls=%async_computation.2 | async-start | bytes 131072 | tf_op jit(solution)/shard_map/all_to_all | solution.py:136
  132.7 0.0 collective-permute-done.8
  132.7 0.0 collective-permute-done.9
  132.7 14.7 %all-to-all-done.2 = bf16[32,8,128]{2,1,0:T(8,128)(2,1)S(1)} async-done(((bf16[32,8,128]{2,1,0:T(8,128)(2,1)}), bf16[32,8,128]{2,1,0:T(8,128)(2,1)S(1)}, u32[]{:S(2)}, u32[]{:S(2)}) %all-to-all-start.2) | async-done | bytes 65568 | tf_op jit(solution)/shard_map/all_to_all | solution.py:136
  147.4 0.7 broadcast_in_dim.7
  148.2 3.4 %all-to-all-start.3 = ((bf16[4,256,128]{2,1,0:T(8,128)(2,1)}), bf16[4,256,128]{2,1,0:T(8,128)(2,1)S(1)}, u32[]{:S(2)}, u32[]{:S(2)}) async-start(bf16[4,256,128]{2,1,0:T(8,128)(2,1)} %broadcast_in_dim.7), calls=%async_computation.3 | async-start | bytes 524288 | tf_op jit(solution)/shard_map/all_to_all | solution.py:68
  151.6 2.3 %collective-permute-start.10 = (bf16[128,2048]{1,0:T(8,128)(2,1)S(1)}, bf16[128,2048]{1,0:T(8,128)(2,1)S(1)}, u32[]{:S(2)}, u32[]{:S(2)}) collective-permute-start(bf16[128,2048]{1,0:T(8,128)(2,1)S(1)} %collective-permute-done.8), channel_id=1, source_target_pairs={{0,16},{16,0},{1,17},{17,1},{2,18},{18,2},{3,19},{19,3},{4,20},{20... | collective-permute-start | bytes 1572872 | tf_op jit(solution)/shard_map/ppermute | solution.py:83
  153.9 2.0 %collective-permute-start.11 = (bf16[128,2048]{1,0:T(8,128)(2,1)S(1)}, bf16[128,2048]{1,0:T(8,128)(2,1)S(1)}, u32[]{:S(2)}, u32[]{:S(2)}) collective-permute-start(bf16[128,2048]{1,0:T(8,128)(2,1)S(1)} %collective-permute-done.9), channel_id=1, source_target_pairs={{0,16},{16,0},{1,17},{17,1},{2,18},{18,2},{3,19},{19,3},{4,20},{20... | collective-permute-start | bytes 1572872 | tf_op jit(solution)/shard_map/ppermute | solution.py:83
  155.9 1.7 all-to-all-done.3
  157.7 0.3 fusion.52
  158.0 0.3 fusion.48
  158.3 0.3 fusion.50
  158.7 0.0 collective-permute-done.11
  158.7 0.3 fusion.46
  159.0 1.6 fusion.8
  160.6 0.3 convolution_add_fusion.1
  160.9 0.5 fusion.4
  161.4 18.4 %all_to_all.25 = bf16[4,128,512]{2,1,0:T(8,128)(2,1)S(1)} all-to-all(bf16[4,128,512]{2,1,0:T(8,128)(2,1)S(1)} %bitcast.130), channel_id=1, replica_groups=mesh['y'=4,'zh'=4,'core'=2,'x'=4,'zl'=4] {'zl'}, dimensions={0} | all-to-all | bytes 1048576 | tf_op jit(solution)/shard_map/all_to_all | solution.py:146
  179.9 0.7 reduce_sum.32
  (35 shorter events, 0.6 us)
Async XLA Ops:
  0.0 7.5 %collective-permute-start = (bf16[128,512]{1,0:T(8,128)(2,1)}, bf16[128,512]{1,0:T(8,128)(2,1)S(1)}, u32[]{:S(2)}, u32[]{:S(2)}) collective-permute-start(bf16[128,512]{1,0:T(8,128)(2,1)} %param.11), channel_id=1, source_target_pairs={{0,0},{1,34},{2,67},{3,98},{32,3},{33,33},{34,64},{35,97},{64,2},{... | collective-permute-start | bytes 393224 | tf_op jit(solution)/shard_map/ppermute | solution.py:98
  3.4 29.5 %collective-permute-start.1 = (bf16[256,512]{1,0:T(8,128)(2,1)S(1)}, bf16[256,512]{1,0:T(8,128)(2,1)S(1)}, u32[]{:S(2)}, u32[]{:S(2)}) collective-permute-start(bf16[256,512]{1,0:T(8,128)(2,1)S(1)} %constant_dynamic-update-slice_fusion), channel_id=1, source_target_pairs={{0,128},{128,0},{256,384},{384,256},{1,129},{129,1},{257,385},{385... | collective-permute-start | bytes 786440 | tf_op jit(solution)/shard_map/ppermute | solution.py:83
  34.4 31.5 %all-to-all-start = ((bf16[4,512,512]{2,1,0:T(8,128)(2,1)}), bf16[4,512,512]{2,1,0:T(8,128)(2,1)S(1)}, u32[]{:S(2)}, u32[]{:S(2)}) async-start(bf16[4,512,512]{2,1,0:T(8,128)(2,1)} %broadcast_in_dim.6), calls=%async_computation | async-start | bytes 4194304 | tf_op jit(solution)/shard_map/all_to_all | solution.py:68
  38.4 22.7 %copy-start.6 = (f32[2,128,256]{2,1,0:T(8,128)S(1)}, f32[2,128,256]{2,1,0:T(8,128)}, u32[]{:S(2)}) copy-start(f32[2,128,256]{2,1,0:T(8,128)} %param.15) | copy-start | bytes 786436
  38.4 15.3 %collective-permute-start.3 = (bf16[256,512]{1,0:T(8,128)(2,1)S(1)}, bf16[256,512]{1,0:T(8,128)(2,1)S(1)}, u32[]{:S(2)}, u32[]{:S(2)}) collective-permute-start(bf16[256,512]{1,0:T(8,128)(2,1)S(1)} %constant_dynamic-update-slice_fusion), channel_id=1, source_target_pairs={{0,384},{128,256},{256,128},{384,0},{1,385},{129,257},{257,129},{3... | collective-permute-start | bytes 786440 | tf_op jit(solution)/shard_map/ppermute | solution.py:83
  43.1 10.7 %collective-permute-start.2 = (bf16[256,512]{1,0:T(8,128)(2,1)S(1)}, bf16[256,512]{1,0:T(8,128)(2,1)S(1)}, u32[]{:S(2)}, u32[]{:S(2)}) collective-permute-start(bf16[256,512]{1,0:T(8,128)(2,1)S(1)} %collective-permute-done.1), channel_id=1, source_target_pairs={{0,384},{128,256},{256,128},{384,0},{1,385},{129,257},{257,129},{3... | collective-permute-start | bytes 786440 | tf_op jit(solution)/shard_map/ppermute | solution.py:83
  45.9 17.3 %collective-permute-start.4 = (bf16[2,256,512]{2,1,0:T(8,128)(2,1)}, bf16[2,256,512]{2,1,0:T(8,128)(2,1)}, u32[]{:S(2)}, u32[]{:S(2)}) collective-permute-start(bf16[2,256,512]{2,1,0:T(8,128)(2,1)} %pad_maximum_fusion.2), channel_id=1, source_target_pairs={{0,16},{16,0},{1,17},{17,1},{2,18},{18,2},{3,19},{19,3},{4,20},{20... | collective-permute-start | bytes 1572872 | tf_op jit(solution)/shard_map/ppermute | solution.py:83
  54.6 8.6 %collective-permute-start.5 = (bf16[2,256,512]{2,1,0:T(8,128)(2,1)}, bf16[2,256,512]{2,1,0:T(8,128)(2,1)}, u32[]{:S(2)}, u32[]{:S(2)}) collective-permute-start(bf16[2,256,512]{2,1,0:T(8,128)(2,1)} %pad_maximum_fusion.3), channel_id=1, source_target_pairs={{0,16},{16,0},{1,17},{17,1},{2,18},{18,2},{3,19},{19,3},{4,20},{20... | collective-permute-start | bytes 1572872 | tf_op jit(solution)/shard_map/ppermute | solution.py:83
  65.9 2.0 %copy-start.2 = (bf16[4,256,512]{2,1,0:T(8,128)(2,1)S(1)}, bf16[4,256,512]{2,1,0:T(8,128)(2,1)}, u32[]{:S(2)}) copy-start(bf16[4,256,512]{2,1,0:T(8,128)(2,1)} %pad_maximum_fusion) | copy-start | bytes 3145732
  69.9 50.1 %all-to-all-start.1 = ((bf16[32,8,1280]{2,1,0:T(8,128)(2,1)}), bf16[32,8,1280]{2,1,0:T(8,128)(2,1)S(1)}, u32[]{:S(2)}, u32[]{:S(2)}) async-start(bf16[32,8,1280]{2,1,0:T(8,128)(2,1)} %bitcast.13), calls=%async_computation.1 | async-start | bytes 1310720 | tf_op jit(solution)/shard_map/all_to_all | solution.py:125
  85.3 34.8 %copy-start.3 = (f32[512,256]{1,0:T(8,128)S(1)}, f32[512,256]{1,0:T(8,128)}, u32[]{:S(2)}) copy-start(f32[512,256]{1,0:T(8,128)} %constant.181) | copy-start | bytes 1572868
  87.9 32.6 %copy-start = (f32[256,128]{1,0:T(8,128)S(1)}, f32[256,128]{1,0:T(8,128)}, u32[]{:S(2)}) copy-start(f32[256,128]{1,0:T(8,128)} %constant.173.clone) | copy-start | bytes 393220
  87.9 32.6 %copy-start.1 = (f32[256,128]{1,0:T(8,128)S(1)}, f32[256,128]{1,0:T(8,128)}, u32[]{:S(2)}) copy-start(f32[256,128]{1,0:T(8,128)} %constant.174.clone) | copy-start | bytes 393220
  87.9 15.3 %collective-permute-start.6 = (bf16[128,2048]{1,0:T(8,128)(2,1)S(1)}, bf16[128,2048]{1,0:T(8,128)(2,1)S(1)}, u32[]{:S(2)}, u32[]{:S(2)}) collective-permute-start(bf16[128,2048]{1,0:T(8,128)(2,1)S(1)} %get-tuple-element.27), channel_id=1, source_target_pairs={{0,4},{4,0},{8,12},{12,8},{1,5},{5,1},{9,13},{13,9},{2,6},{6,2},{1... | collective-permute-start | bytes 1572872 | tf_op jit(solution)/shard_map/ppermute | solution.py:83
  90.2 42.5 %collective-permute-start.8 = (bf16[128,2048]{1,0:T(8,128)(2,1)}, bf16[128,2048]{1,0:T(8,128)(2,1)S(1)}, u32[]{:S(2)}, u32[]{:S(2)}) collective-permute-start(bf16[128,2048]{1,0:T(8,128)(2,1)} %get-tuple-element.25), channel_id=1, source_target_pairs={{0,12},{4,8},{8,4},{12,0},{1,13},{5,9},{9,5},{13,1},{2,14},{6,10},... | collective-permute-start | bytes 1572872 | tf_op jit(solution)/shard_map/ppermute | solution.py:83
  93.0 39.8 %collective-permute-start.9 = (bf16[128,2048]{1,0:T(8,128)(2,1)}, bf16[128,2048]{1,0:T(8,128)(2,1)S(1)}, u32[]{:S(2)}, u32[]{:S(2)}) collective-permute-start(bf16[128,2048]{1,0:T(8,128)(2,1)} %get-tuple-element.26), channel_id=1, source_target_pairs={{0,8},{4,12},{8,0},{12,4},{1,9},{5,13},{9,1},{13,5},{2,10},{6,14},... | collective-permute-start | bytes 1572872 | tf_op jit(solution)/shard_map/ppermute | solution.py:83
  103.2 29.5 %collective-permute-start.7 = (bf16[128,2048]{1,0:T(8,128)(2,1)S(1)}, bf16[128,2048]{1,0:T(8,128)(2,1)S(1)}, u32[]{:S(2)}, u32[]{:S(2)}) collective-permute-start(bf16[128,2048]{1,0:T(8,128)(2,1)S(1)} %collective-permute-done.6), channel_id=1, source_target_pairs={{0,16},{16,0},{1,17},{17,1},{2,18},{18,2},{3,19},{19,3},{4,20},{20... | collective-permute-start | bytes 1572872 | tf_op jit(solution)/shard_map/ppermute | solution.py:83
  120.0 0.9 copy-start.8
  120.1 1.2 copy-start.7
  120.5 1.2 copy-start.5
  120.6 1.5 copy-start.4
  123.2 24.2 %all-to-all-start.2 = ((bf16[32,8,128]{2,1,0:T(8,128)(2,1)}), bf16[32,8,128]{2,1,0:T(8,128)(2,1)S(1)}, u32[]{:S(2)}, u32[]{:S(2)}) async-start(bf16[32,8,128]{2,1,0:T(8,128)(2,1)} %fusion.33), calls=%async_computation.2 | async-start | bytes 131072 | tf_op jit(solution)/shard_map/all_to_all | solution.py:136
  148.2 9.5 %all-to-all-start.3 = ((bf16[4,256,128]{2,1,0:T(8,128)(2,1)}), bf16[4,256,128]{2,1,0:T(8,128)(2,1)S(1)}, u32[]{:S(2)}, u32[]{:S(2)}) async-start(bf16[4,256,128]{2,1,0:T(8,128)(2,1)} %broadcast_in_dim.7), calls=%async_computation.3 | async-start | bytes 524288 | tf_op jit(solution)/shard_map/all_to_all | solution.py:68
  151.6 6.7 %collective-permute-start.10 = (bf16[128,2048]{1,0:T(8,128)(2,1)S(1)}, bf16[128,2048]{1,0:T(8,128)(2,1)S(1)}, u32[]{:S(2)}, u32[]{:S(2)}) collective-permute-start(bf16[128,2048]{1,0:T(8,128)(2,1)S(1)} %collective-permute-done.8), channel_id=1, source_target_pairs={{0,16},{16,0},{1,17},{17,1},{2,18},{18,2},{3,19},{19,3},{4,20},{20... | collective-permute-start | bytes 1572872 | tf_op jit(solution)/shard_map/ppermute | solution.py:83
  153.9 4.8 %collective-permute-start.11 = (bf16[128,2048]{1,0:T(8,128)(2,1)S(1)}, bf16[128,2048]{1,0:T(8,128)(2,1)S(1)}, u32[]{:S(2)}, u32[]{:S(2)}) collective-permute-start(bf16[128,2048]{1,0:T(8,128)(2,1)S(1)} %collective-permute-done.9), channel_id=1, source_target_pairs={{0,16},{16,0},{1,17},{17,1},{2,18},{18,2},{3,19},{19,3},{4,20},{20... | collective-permute-start | bytes 1572872 | tf_op jit(solution)/shard_map/ppermute | solution.py:83

commit v6 on v5

--- a/solution.py
+++ b/solution.py
@@ -8,6 +8,7 @@
 from jax.sharding import PartitionSpec as P
 
 SEQ = ("y", "zh", "core")
+SPREAD = ("zh", "y", "core")
 CH = ("x", "zl")
 N1, N2 = 32, 128
 TOTAL = N1 * N2
@@ -21,8 +22,8 @@
 
 
 def dft_tables():
-    n1, n2 = np.arange(N1), np.arange(N2)
-    k1, k2 = reverse(N1), reverse(N2)
+    n1, n2 = np.array([y * 8 + zh * 2 + core for zh in range(4) for y in range(4) for core in range(2)]), np.arange(N2)
+    k1, k2 = reverse(N1)[n1], reverse(N2)
     outer = np.exp(-2j * np.pi * np.outer(k1, n1) / N1)
     twist = np.exp(-2j * np.pi * np.outer(k1, n2) / TOTAL)
     inner = np.exp(-2j * np.pi * np.outer(n2, k2) / N2)
@@ -88,8 +89,8 @@
 
 
 def summed(parts):
-    total = parts.reshape(4, 4, 2, GROUP, 4, N2).astype(jnp.float32).sum(axis=1)
-    return jnp.transpose(total, (0, 3, 1, 2, 4)).reshape(N1, GROUP, N2)
+    total = parts.reshape(4, 4, 2, GROUP, 4, N2).astype(jnp.float32).sum(axis=0)
+    return jnp.transpose(total, (3, 0, 1, 2, 4)).reshape(N1, GROUP, N2)
 
 
 def local(tokens, gate_weight, value_weight, out_weight, filter_spectrum):
@@ -122,10 +123,10 @@
     value, gate = projected[:256], projected[256:]
     resp = jnp.transpose(filter_spectrum, (2, 0, 1)).reshape(256, 256).astype(jnp.bfloat16)
     packet = jnp.concatenate([value, gate, resp], axis=1).reshape(N1, GROUP, 1280)
-    packet = lax.all_to_all(packet, SEQ, 0, 0)
+    packet = lax.all_to_all(packet, SPREAD, 0, 0)
 
     held = after(out_weight, value)
-    own = lax.dynamic_slice_in_dim(held, column * 2048, 2048, 1)
+    own = jnp.concatenate([lax.dynamic_slice(held, (part * 128, column * 2048), (128, 2048)) for part in (core, 1 - core)])
     half = {k: exchange(lax.dynamic_slice(held, (core * 128, (column ^ k) * 2048), (128, 2048)), "x", k) for k in (1, 2, 3)}
     other = {k: exchange(half[k], "core", 1) for k in (1, 2, 3)}
 
@@ -133,15 +134,16 @@
     resp = packet[:, :, 1024:].astype(jnp.float32)
     resp = jnp.transpose(resp.reshape(N1, GROUP, 2, N2), (2, 0, 1, 3))
     hidden = (jax.nn.silu(gate) * convolve(signal, resp)).astype(jnp.bfloat16)
-    hidden = lax.all_to_all(hidden, SEQ, 0, 0).reshape(256, 128)
+    hidden = lax.all_to_all(hidden, SPREAD, 0, 0).reshape(256, 128)
     hidden, other[1], half[3], half[2] = lax.optimization_barrier((hidden, other[1], half[3], half[2]))
 
+    hidden = jnp.where(core == 0, hidden, jnp.concatenate([hidden[128:], hidden[:128]]))
     hidden = gather_over(hidden, "x")
     total = jnp.einsum("ct,cd->td", pick(hidden, column), own, preferred_element_type=jnp.float32)
     for k in (1, 3, 2):
-        rows = pick(hidden, column ^ k).reshape(2, 128, 128)
-        for part, weight in ((core, half[k]), (1 - core, other[k])):
-            total = total + jnp.einsum("ct,cd->td", pick(rows, part), weight, preferred_element_type=jnp.float32)
+        rows = pick(hidden, column ^ k)
+        for part, weight in ((rows[:128], half[k]), (rows[128:], other[k])):
+            total = total + jnp.einsum("ct,cd->td", part, weight, preferred_element_type=jnp.float32)
     total = jnp.transpose(total.astype(jnp.bfloat16).reshape(128, 4, 512), (1, 0, 2))
     total = lax.all_to_all(total, "zl", 0, 0)
     return total.astype(jnp.float32).sum(axis=0).astype(jnp.bfloat16)

time: 182 us -> 180 us (0.989)
  blocking collectives: 43.7 us -> 41.4 us
    all_to_all x1, blocking collectives: 18.4 us -> 16.1 us  [local(): total = lax.all_to_all(total, 'zl', 0, 0)]
    dot_general x6, matrix products: 2.11 us -> 4.18 us  [local(): jnp.einsum('ct,cd->td', part, weight, preferred_element_type=jnp.float32)]
    all_to_all x2, waiting for transfers between devices: 1.7 us -> 3.73 us  [gather_over(): lax.all_to_all(jnp.broadcast_to(block, (count,) + block.shape), axis, 0, 0)]
  transfers between devices with their start and end apart: 16 -> 16, of which waited for: 4 -> 4; matrix products, arithmetic and copies ran while one was open for 8% -> 9% of each run, Pallas kernels for 0% -> 0%
where the time goes in v6:
time: 180 us; the launch traced here: 179 us
  starting transfers between devices  75.5 us (42%)
  blocking collectives  41.4 us (23%)
  waiting for transfers between devices  35.5 us (20%)
  matrix products  8.96 us (5%)
  local copies, waits for them, and re-layouts  8.79 us (5%)
  other arithmetic  8.21 us (5%)
    ppermute x11, starting transfers between devices, exchange(): lax.ppermute(block, axis, [(i, i ^ apart) for i in range(lax.axis_size(ax...  42.6 us
    all_gather x1, blocking collectives, local(): near = lax.all_gather(swapped, 'zl')  25.2 us
    all_to_all x1, blocking collectives, local(): total = lax.all_to_all(total, 'zl', 0, 0)  16.1 us
    all_to_all x1, starting transfers between devices, local(): packet = lax.all_to_all(packet, SPREAD, 0, 0)  15.4 us
    all_to_all x1, waiting for transfers between devices, local(): packet = lax.all_to_all(packet, SPREAD, 0, 0)  13.6 us
    all_to_all x1, waiting for transfers between devices, local(): hidden = lax.all_to_all(hidden, SPREAD, 0, 0).reshape(256, 128)  12.4 us
    all_to_all x1, starting transfers between devices, local(): hidden = lax.all_to_all(hidden, SPREAD, 0, 0).reshape(256, 128)  8.5 us
    all_to_all x2, starting transfers between devices, gather_over(): lax.all_to_all(jnp.broadcast_to(block, (count,) + block.shape), axis, 0, 0)  7.42 us
  transfers between devices with their start and end apart: 16, of which 4 were waited for; matrix products, arithmetic and copies ran while one was open for 9% of the time, Pallas kernels for 0%

profile of v6, /device:TPU:1, one launch (start us, length us, event | category | flops | bytes accessed | tf_op | source)
XLA Modules:
  0.0 178.9 jit_solution(6577337648706924804)
XLA Ops:
  0.0 1.6 collective-permute-start
  1.6 0.9 constant_dynamic-update-slice_fusion.1
  2.5 0.9 constant_dynamic-update-slice_fusion
  3.4 4.0 %collective-permute-start.1 = (bf16[256,512]{1,0:T(8,128)(2,1)S(1)}, bf16[256,512]{1,0:T(8,128)(2,1)S(1)}, u32[]{:S(2)}, u32[]{:S(2)}) collective-permute-start(bf16[256,512]{1,0:T(8,128)(2,1)S(1)} %constant_dynamic-update-slice_fusion), channel_id=1, source_target_pairs={{0,128},{128,0},{256,384},{384,256},{1,129},{129,1},{257,385},{385... | collective-permute-start | bytes 786440 | tf_op jit(solution)/shard_map/ppermute | solution.py:84
  7.5 0.0 collective-permute-done
  7.5 25.2 %all-gather = bf16[512,512]{1,0:T(8,128)(2,1)S(1)} all-gather(bf16[128,512]{1,0:T(8,128)(2,1)S(1)} %maximum_select_fusion), channel_id=2, replica_groups=mesh['y'=4,'zh'=4,'core'=2,'x'=4,'zl'=4] {'zl'}, dimensions={0}, use_global_device_ids=true | all-gather | bytes 655360 | tf_op jit(solution)/shard_map/all_gather | solution.py:101
  32.9 0.0 collective-permute-done.1
  32.9 1.5 broadcast_in_dim.6
  34.4 4.0 %all-to-all-start = ((bf16[4,512,512]{2,1,0:T(8,128)(2,1)}), bf16[4,512,512]{2,1,0:T(8,128)(2,1)S(1)}, u32[]{:S(2)}, u32[]{:S(2)}) async-start(bf16[4,512,512]{2,1,0:T(8,128)(2,1)} %broadcast_in_dim.6), calls=%async_computation | async-start | bytes 4194304 | tf_op jit(solution)/shard_map/all_to_all | solution.py:69
  38.4 4.7 %collective-permute-start.3 = (bf16[256,512]{1,0:T(8,128)(2,1)S(1)}, bf16[256,512]{1,0:T(8,128)(2,1)S(1)}, u32[]{:S(2)}, u32[]{:S(2)}) collective-permute-start(bf16[256,512]{1,0:T(8,128)(2,1)S(1)} %constant_dynamic-update-slice_fusion), channel_id=1, source_target_pairs={{0,384},{128,256},{256,128},{384,0},{1,385},{129,257},{257,129},{3... | collective-permute-start | bytes 786440 | tf_op jit(solution)/shard_map/ppermute | solution.py:84
  43.1 1.9 %collective-permute-start.2 = (bf16[256,512]{1,0:T(8,128)(2,1)S(1)}, bf16[256,512]{1,0:T(8,128)(2,1)S(1)}, u32[]{:S(2)}, u32[]{:S(2)}) collective-permute-start(bf16[256,512]{1,0:T(8,128)(2,1)S(1)} %collective-permute-done.1), channel_id=1, source_target_pairs={{0,384},{128,256},{256,128},{384,0},{1,385},{129,257},{257,129},{3... | collective-permute-start | bytes 786440 | tf_op jit(solution)/shard_map/ppermute | solution.py:84
  45.1 0.9 pad_maximum_fusion.2
  45.9 7.8 %collective-permute-start.4 = (bf16[2,256,512]{2,1,0:T(8,128)(2,1)}, bf16[2,256,512]{2,1,0:T(8,128)(2,1)}, u32[]{:S(2)}, u32[]{:S(2)}) collective-permute-start(bf16[2,256,512]{2,1,0:T(8,128)(2,1)} %pad_maximum_fusion.2), channel_id=1, source_target_pairs={{0,16},{16,0},{1,17},{17,1},{2,18},{18,2},{3,19},{19,3},{4,20},{20... | collective-permute-start | bytes 1572872 | tf_op jit(solution)/shard_map/ppermute | solution.py:84
  53.7 0.0 collective-permute-done.3
  53.8 0.9 pad_maximum_fusion.3
  54.6 6.4 %collective-permute-start.5 = (bf16[2,256,512]{2,1,0:T(8,128)(2,1)}, bf16[2,256,512]{2,1,0:T(8,128)(2,1)}, u32[]{:S(2)}, u32[]{:S(2)}) collective-permute-start(bf16[2,256,512]{2,1,0:T(8,128)(2,1)} %pad_maximum_fusion.3), channel_id=1, source_target_pairs={{0,16},{16,0},{1,17},{17,1},{2,18},{18,2},{3,19},{19,3},{4,20},{20... | collective-permute-start | bytes 1572872 | tf_op jit(solution)/shard_map/ppermute | solution.py:84
  61.2 0.2 fusion.21
  61.4 0.7 fusion.15
  62.1 1.1 pad_maximum_fusion
  63.2 1.6 dynamic-slice_select_fusion.3
  64.8 1.1 pad_maximum_fusion.1
  65.9 0.0 all-to-all-done
  65.9 2.0 %convolution_bitcast_fusion = f32[512,512]{0,1:T(8,128)S(1)} fusion(bf16[4,256,512]{2,1,0:T(8,128)(2,1)} %pad_maximum_fusion.1, bf16[4,512,512]{2,1,0:T(8,128)(2,1)S(1)} %all-to-all-done), kind=kOutput, calls=%fused_computation.7 | convolution fusion | flops 536870912 | bytes 3145728 | tf_op jit(solution)/shard_map/xkc,xtk->ct/dot_general | solution.py:121
  68.0 0.7 fusion.6
  68.8 1.1 copy.21
  69.9 15.4 %all-to-all-start.1 = ((bf16[32,8,1280]{2,1,0:T(8,128)(2,1)}), bf16[32,8,1280]{2,1,0:T(8,128)(2,1)S(1)}, u32[]{:S(2)}, u32[]{:S(2)}) async-start(bf16[32,8,1280]{2,1,0:T(8,128)(2,1)} %bitcast.13), calls=%async_computation.1 | async-start | bytes 1310720 | tf_op jit(solution)/shard_map/all_to_all | solution.py:126
  85.3 0.0 copy-start.3
  85.3 3.0 %fusion.62 = (bf16[128,2048]{1,0:T(8,128)(2,1)S(1)}, bf16[128,2048]{1,0:T(8,128)(2,1)S(1)}, bf16[128,2048]{1,0:T(8,128)(2,1)}, bf16[128,2048]{1,0:T(8,128)(2,1)}, bf16[128,2048]{1,0:T(8,128)(2,1)S(1)}) fusion(bf16[256,8192]{1,0:T(8,128)(2,1)} %param.14, s32[]{:T(128)S(6)} %select_n.245, s32[]{:T(128)S(6)} %select_n.251, s32[]{:T(128)S(6)} %select_n.252, ...), kind=kLoop, calls=%fused_computation.125 | loop fusion | bytes 5242904 | tf_op jit(solution)/shard_map/dynamic_slice | solution.py:129
  88.3 2.3 %collective-permute-start.6 = (bf16[128,2048]{1,0:T(8,128)(2,1)S(1)}, bf16[128,2048]{1,0:T(8,128)(2,1)}, u32[]{:S(2)}, u32[]{:S(2)}) collective-permute-start(bf16[128,2048]{1,0:T(8,128)(2,1)S(1)} %get-tuple-element.29), channel_id=1, source_target_pairs={{0,4},{4,0},{8,12},{12,8},{1,5},{5,1},{9,13},{13,9},{2,6},{6,2},{1... | collective-permute-start | bytes 1572872 | tf_op jit(solution)/shard_map/ppermute | solution.py:84
  90.6 3.7 %collective-permute-start.9 = (bf16[128,2048]{1,0:T(8,128)(2,1)}, bf16[128,2048]{1,0:T(8,128)(2,1)S(1)}, u32[]{:S(2)}, u32[]{:S(2)}) collective-permute-start(bf16[128,2048]{1,0:T(8,128)(2,1)} %get-tuple-element.27), channel_id=1, source_target_pairs={{0,8},{4,12},{8,0},{12,4},{1,9},{5,13},{9,1},{13,5},{2,10},{6,14},... | collective-permute-start | bytes 1572872 | tf_op jit(solution)/shard_map/ppermute | solution.py:84
  94.3 3.7 %collective-permute-start.8 = (bf16[128,2048]{1,0:T(8,128)(2,1)}, bf16[128,2048]{1,0:T(8,128)(2,1)S(1)}, u32[]{:S(2)}, u32[]{:S(2)}) collective-permute-start(bf16[128,2048]{1,0:T(8,128)(2,1)} %get-tuple-element.28), channel_id=1, source_target_pairs={{0,12},{4,8},{8,4},{12,0},{1,13},{5,9},{9,5},{13,1},{2,14},{6,10},... | collective-permute-start | bytes 1572872 | tf_op jit(solution)/shard_map/ppermute | solution.py:84
  98.0 5.7 %collective-permute-done.6 = bf16[128,2048]{1,0:T(8,128)(2,1)} collective-permute-done((bf16[128,2048]{1,0:T(8,128)(2,1)S(1)}, bf16[128,2048]{1,0:T(8,128)(2,1)}, u32[]{:S(2)}, u32[]{:S(2)}) %collective-permute-start.6) | collective-permute-done | bytes 524320 | tf_op jit(solution)/shard_map/ppermute | solution.py:84
  103.7 3.6 %collective-permute-start.7 = (bf16[128,2048]{1,0:T(8,128)(2,1)}, bf16[128,2048]{1,0:T(8,128)(2,1)}, u32[]{:S(2)}, u32[]{:S(2)}) collective-permute-start(bf16[128,2048]{1,0:T(8,128)(2,1)} %collective-permute-done.6), channel_id=1, source_target_pairs={{0,16},{16,0},{1,17},{17,1},{2,18},{18,2},{3,19},{19,3},{4,20},{20... | collective-permute-start | bytes 1572872 | tf_op jit(solution)/shard_map/ppermute | solution.py:84
  107.3 13.6 %all-to-all-done.1 = bf16[32,8,1280]{2,1,0:T(8,128)(2,1)S(1)} async-done(((bf16[32,8,1280]{2,1,0:T(8,128)(2,1)}), bf16[32,8,1280]{2,1,0:T(8,128)(2,1)S(1)}, u32[]{:S(2)}, u32[]{:S(2)}) %all-to-all-start.1) | async-done | bytes 655392 | tf_op jit(solution)/shard_map/all_to_all | solution.py:126
  121.0 0.0 copy-start.7
  121.0 0.4 fusion.67
  121.4 0.0 copy-start.5
  121.5 0.0 copy-start.4
  121.5 0.3 copy-done.8
  121.8 0.4 fusion.26
  122.2 0.4 fusion.30
  122.6 0.3 fusion.42
  123.0 0.3 fusion.7
  123.3 0.1 copy.25
  123.4 0.7 fusion.35
  124.1 8.5 %all-to-all-start.2 = ((bf16[32,8,128]{2,1,0:T(8,128)(2,1)}), bf16[32,8,128]{2,1,0:T(8,128)(2,1)S(1)}, u32[]{:S(2)}, u32[]{:S(2)}) async-start(bf16[32,8,128]{2,1,0:T(8,128)(2,1)} %fusion.35), calls=%async_computation.2 | async-start | bytes 131072 | tf_op jit(solution)/shard_map/all_to_all | solution.py:137
  132.6 2.1 %collective-permute-start.11 = (bf16[128,2048]{1,0:T(8,128)(2,1)S(1)}, bf16[128,2048]{1,0:T(8,128)(2,1)S(1)}, u32[]{:S(2)}, u32[]{:S(2)}) collective-permute-start(bf16[128,2048]{1,0:T(8,128)(2,1)S(1)} %collective-permute-done.9), channel_id=1, source_target_pairs={{0,16},{16,0},{1,17},{17,1},{2,18},{18,2},{3,19},{19,3},{4,20},{20... | collective-permute-start | bytes 1572872 | tf_op jit(solution)/shard_map/ppermute | solution.py:84
  134.8 0.0 collective-permute-done.8
  134.8 12.4 %all-to-all-done.2 = bf16[32,8,128]{2,1,0:T(8,128)(2,1)S(1)} async-done(((bf16[32,8,128]{2,1,0:T(8,128)(2,1)}), bf16[32,8,128]{2,1,0:T(8,128)(2,1)S(1)}, u32[]{:S(2)}, u32[]{:S(2)}) %all-to-all-start.2) | async-done | bytes 65568 | tf_op jit(solution)/shard_map/all_to_all | solution.py:137
  147.3 0.7 broadcast_in_dim.7
  148.0 3.4 %all-to-all-start.3 = ((bf16[4,256,128]{2,1,0:T(8,128)(2,1)}), bf16[4,256,128]{2,1,0:T(8,128)(2,1)S(1)}, u32[]{:S(2)}, u32[]{:S(2)}) async-start(bf16[4,256,128]{2,1,0:T(8,128)(2,1)} %broadcast_in_dim.7), calls=%async_computation.3 | async-start | bytes 524288 | tf_op jit(solution)/shard_map/all_to_all | solution.py:69
  151.4 2.3 %collective-permute-start.10 = (bf16[128,2048]{1,0:T(8,128)(2,1)S(1)}, bf16[128,2048]{1,0:T(8,128)(2,1)S(1)}, u32[]{:S(2)}, u32[]{:S(2)}) collective-permute-start(bf16[128,2048]{1,0:T(8,128)(2,1)S(1)} %collective-permute-done.8), channel_id=1, source_target_pairs={{0,16},{16,0},{1,17},{17,1},{2,18},{18,2},{3,19},{19,3},{4,20},{20... | collective-permute-start | bytes 1572872 | tf_op jit(solution)/shard_map/ppermute | solution.py:84
  153.8 3.7 %all-to-all-done.3 = bf16[4,256,128]{2,1,0:T(8,128)(2,1)S(1)} async-done(((bf16[4,256,128]{2,1,0:T(8,128)(2,1)}), bf16[4,256,128]{2,1,0:T(8,128)(2,1)S(1)}, u32[]{:S(2)}, u32[]{:S(2)}) %all-to-all-start.3) | async-done | bytes 262176 | tf_op jit(solution)/shard_map/all_to_all | solution.py:69
  157.5 0.3 fusion.49
  157.8 0.0 collective-permute-done.11
  157.8 0.3 fusion.48
  158.1 0.3 fusion.51
  158.5 0.0 collective-permute-done.10
  158.5 0.3 fusion.50
  158.8 0.3 fusion.8
  159.2 1.4 convolution_add_fusion.1
  160.5 1.5 fusion.4
  162.1 16.1 %all_to_all.25 = bf16[4,128,512]{2,1,0:T(8,128)(2,1)S(1)} all-to-all(bf16[4,128,512]{2,1,0:T(8,128)(2,1)S(1)} %bitcast.126), channel_id=1, replica_groups=mesh['y'=4,'zh'=4,'core'=2,'x'=4,'zl'=4] {'zl'}, dimensions={0} | all-to-all | bytes 1048576 | tf_op jit(solution)/shard_map/all_to_all | solution.py:148
  178.2 0.7 reduce_sum.32
  (36 shorter events, 0.6 us)
Async XLA Ops:
  0.0 7.5 %collective-permute-start = (bf16[128,512]{1,0:T(8,128)(2,1)}, bf16[128,512]{1,0:T(8,128)(2,1)S(1)}, u32[]{:S(2)}, u32[]{:S(2)}) collective-permute-start(bf16[128,512]{1,0:T(8,128)(2,1)} %param.11), channel_id=1, source_target_pairs={{0,0},{1,34},{2,67},{3,98},{32,3},{33,33},{34,64},{35,97},{64,2},{... | collective-permute-start | bytes 393224 | tf_op jit(solution)/shard_map/ppermute | solution.py:99
  3.4 29.5 %collective-permute-start.1 = (bf16[256,512]{1,0:T(8,128)(2,1)S(1)}, bf16[256,512]{1,0:T(8,128)(2,1)S(1)}, u32[]{:S(2)}, u32[]{:S(2)}) collective-permute-start(bf16[256,512]{1,0:T(8,128)(2,1)S(1)} %constant_dynamic-update-slice_fusion), channel_id=1, source_target_pairs={{0,128},{128,0},{256,384},{384,256},{1,129},{129,1},{257,385},{385... | collective-permute-start | bytes 786440 | tf_op jit(solution)/shard_map/ppermute | solution.py:84
  34.4 31.5 %all-to-all-start = ((bf16[4,512,512]{2,1,0:T(8,128)(2,1)}), bf16[4,512,512]{2,1,0:T(8,128)(2,1)S(1)}, u32[]{:S(2)}, u32[]{:S(2)}) async-start(bf16[4,512,512]{2,1,0:T(8,128)(2,1)} %broadcast_in_dim.6), calls=%async_computation | async-start | bytes 4194304 | tf_op jit(solution)/shard_map/all_to_all | solution.py:69
  38.4 22.7 %copy-start.6 = (f32[2,128,256]{2,1,0:T(8,128)S(1)}, f32[2,128,256]{2,1,0:T(8,128)}, u32[]{:S(2)}) copy-start(f32[2,128,256]{2,1,0:T(8,128)} %param.15) | copy-start | bytes 786436
  38.4 15.3 %collective-permute-start.3 = (bf16[256,512]{1,0:T(8,128)(2,1)S(1)}, bf16[256,512]{1,0:T(8,128)(2,1)S(1)}, u32[]{:S(2)}, u32[]{:S(2)}) collective-permute-start(bf16[256,512]{1,0:T(8,128)(2,1)S(1)} %constant_dynamic-update-slice_fusion), channel_id=1, source_target_pairs={{0,384},{128,256},{256,128},{384,0},{1,385},{129,257},{257,129},{3... | collective-permute-start | bytes 786440 | tf_op jit(solution)/shard_map/ppermute | solution.py:84
  43.1 10.7 %collective-permute-start.2 = (bf16[256,512]{1,0:T(8,128)(2,1)S(1)}, bf16[256,512]{1,0:T(8,128)(2,1)S(1)}, u32[]{:S(2)}, u32[]{:S(2)}) collective-permute-start(bf16[256,512]{1,0:T(8,128)(2,1)S(1)} %collective-permute-done.1), channel_id=1, source_target_pairs={{0,384},{128,256},{256,128},{384,0},{1,385},{129,257},{257,129},{3... | collective-permute-start | bytes 786440 | tf_op jit(solution)/shard_map/ppermute | solution.py:84
  45.9 17.3 %collective-permute-start.4 = (bf16[2,256,512]{2,1,0:T(8,128)(2,1)}, bf16[2,256,512]{2,1,0:T(8,128)(2,1)}, u32[]{:S(2)}, u32[]{:S(2)}) collective-permute-start(bf16[2,256,512]{2,1,0:T(8,128)(2,1)} %pad_maximum_fusion.2), channel_id=1, source_target_pairs={{0,16},{16,0},{1,17},{17,1},{2,18},{18,2},{3,19},{19,3},{4,20},{20... | collective-permute-start | bytes 1572872 | tf_op jit(solution)/shard_map/ppermute | solution.py:84
  54.6 8.6 %collective-permute-start.5 = (bf16[2,256,512]{2,1,0:T(8,128)(2,1)}, bf16[2,256,512]{2,1,0:T(8,128)(2,1)}, u32[]{:S(2)}, u32[]{:S(2)}) collective-permute-start(bf16[2,256,512]{2,1,0:T(8,128)(2,1)} %pad_maximum_fusion.3), channel_id=1, source_target_pairs={{0,16},{16,0},{1,17},{17,1},{2,18},{18,2},{3,19},{19,3},{4,20},{20... | collective-permute-start | bytes 1572872 | tf_op jit(solution)/shard_map/ppermute | solution.py:84
  65.9 2.0 %copy-start.2 = (bf16[4,256,512]{2,1,0:T(8,128)(2,1)S(1)}, bf16[4,256,512]{2,1,0:T(8,128)(2,1)}, u32[]{:S(2)}) copy-start(bf16[4,256,512]{2,1,0:T(8,128)(2,1)} %pad_maximum_fusion) | copy-start | bytes 3145732
  69.9 51.0 %all-to-all-start.1 = ((bf16[32,8,1280]{2,1,0:T(8,128)(2,1)}), bf16[32,8,1280]{2,1,0:T(8,128)(2,1)S(1)}, u32[]{:S(2)}, u32[]{:S(2)}) async-start(bf16[32,8,1280]{2,1,0:T(8,128)(2,1)} %bitcast.13), calls=%async_computation.1 | async-start | bytes 1310720 | tf_op jit(solution)/shard_map/all_to_all | solution.py:126
  85.3 35.8 %copy-start.3 = (f32[512,256]{1,0:T(8,128)S(1)}, f32[512,256]{1,0:T(8,128)}, u32[]{:S(2)}) copy-start(f32[512,256]{1,0:T(8,128)} %constant.166) | copy-start | bytes 1572868
  88.3 33.2 %copy-start = (f32[256,128]{1,0:T(8,128)S(1)}, f32[256,128]{1,0:T(8,128)}, u32[]{:S(2)}) copy-start(f32[256,128]{1,0:T(8,128)} %constant.159.clone) | copy-start | bytes 393220
  88.3 33.2 %copy-start.1 = (f32[256,128]{1,0:T(8,128)S(1)}, f32[256,128]{1,0:T(8,128)}, u32[]{:S(2)}) copy-start(f32[256,128]{1,0:T(8,128)} %constant.158.clone) | copy-start | bytes 393220
  88.3 15.4 %collective-permute-start.6 = (bf16[128,2048]{1,0:T(8,128)(2,1)S(1)}, bf16[128,2048]{1,0:T(8,128)(2,1)}, u32[]{:S(2)}, u32[]{:S(2)}) collective-permute-start(bf16[128,2048]{1,0:T(8,128)(2,1)S(1)} %get-tuple-element.29), channel_id=1, source_target_pairs={{0,4},{4,0},{8,12},{12,8},{1,5},{5,1},{9,13},{13,9},{2,6},{6,2},{1... | collective-permute-start | bytes 1572872 | tf_op jit(solution)/shard_map/ppermute | solution.py:84
  90.6 42.0 %collective-permute-start.9 = (bf16[128,2048]{1,0:T(8,128)(2,1)}, bf16[128,2048]{1,0:T(8,128)(2,1)S(1)}, u32[]{:S(2)}, u32[]{:S(2)}) collective-permute-start(bf16[128,2048]{1,0:T(8,128)(2,1)} %get-tuple-element.27), channel_id=1, source_target_pairs={{0,8},{4,12},{8,0},{12,4},{1,9},{5,13},{9,1},{13,5},{2,10},{6,14},... | collective-permute-start | bytes 1572872 | tf_op jit(solution)/shard_map/ppermute | solution.py:84
  94.3 40.5 %collective-permute-start.8 = (bf16[128,2048]{1,0:T(8,128)(2,1)}, bf16[128,2048]{1,0:T(8,128)(2,1)S(1)}, u32[]{:S(2)}, u32[]{:S(2)}) collective-permute-start(bf16[128,2048]{1,0:T(8,128)(2,1)} %get-tuple-element.28), channel_id=1, source_target_pairs={{0,12},{4,8},{8,4},{12,0},{1,13},{5,9},{9,5},{13,1},{2,14},{6,10},... | collective-permute-start | bytes 1572872 | tf_op jit(solution)/shard_map/ppermute | solution.py:84
  103.7 31.1 %collective-permute-start.7 = (bf16[128,2048]{1,0:T(8,128)(2,1)}, bf16[128,2048]{1,0:T(8,128)(2,1)}, u32[]{:S(2)}, u32[]{:S(2)}) collective-permute-start(bf16[128,2048]{1,0:T(8,128)(2,1)} %collective-permute-done.6), channel_id=1, source_target_pairs={{0,16},{16,0},{1,17},{17,1},{2,18},{18,2},{3,19},{19,3},{4,20},{20... | collective-permute-start | bytes 1572872 | tf_op jit(solution)/shard_map/ppermute | solution.py:84
  120.9 0.9 copy-start.8
  121.0 1.2 copy-start.7
  121.4 1.2 copy-start.5
  121.5 1.5 copy-start.4
  124.1 23.1 %all-to-all-start.2 = ((bf16[32,8,128]{2,1,0:T(8,128)(2,1)}), bf16[32,8,128]{2,1,0:T(8,128)(2,1)S(1)}, u32[]{:S(2)}, u32[]{:S(2)}) async-start(bf16[32,8,128]{2,1,0:T(8,128)(2,1)} %fusion.35), calls=%async_computation.2 | async-start | bytes 131072 | tf_op jit(solution)/shard_map/all_to_all | solution.py:137
  132.6 25.2 %collective-permute-start.11 = (bf16[128,2048]{1,0:T(8,128)(2,1)S(1)}, bf16[128,2048]{1,0:T(8,128)(2,1)S(1)}, u32[]{:S(2)}, u32[]{:S(2)}) collective-permute-start(bf16[128,2048]{1,0:T(8,128)(2,1)S(1)} %collective-permute-done.9), channel_id=1, source_target_pairs={{0,16},{16,0},{1,17},{17,1},{2,18},{18,2},{3,19},{19,3},{4,20},{20... | collective-permute-start | bytes 1572872 | tf_op jit(solution)/shard_map/ppermute | solution.py:84
  148.0 9.5 %all-to-all-start.3 = ((bf16[4,256,128]{2,1,0:T(8,128)(2,1)}), bf16[4,256,128]{2,1,0:T(8,128)(2,1)S(1)}, u32[]{:S(2)}, u32[]{:S(2)}) async-start(bf16[4,256,128]{2,1,0:T(8,128)(2,1)} %broadcast_in_dim.7), calls=%async_computation.3 | async-start | bytes 524288 | tf_op jit(solution)/shard_map/all_to_all | solution.py:69
  151.4 7.0 %collective-permute-start.10 = (bf16[128,2048]{1,0:T(8,128)(2,1)S(1)}, bf16[128,2048]{1,0:T(8,128)(2,1)S(1)}, u32[]{:S(2)}, u32[]{:S(2)}) collective-permute-start(bf16[128,2048]{1,0:T(8,128)(2,1)S(1)} %collective-permute-done.8), channel_id=1, source_target_pairs={{0,16},{16,0},{1,17},{17,1},{2,18},{18,2},{3,19},{19,3},{4,20},{20... | collective-permute-start | bytes 1572872 | tf_op jit(solution)/shard_map/ppermute | solution.py:84

commit v7 on v6

--- a/solution.py
+++ b/solution.py
@@ -13,7 +13,7 @@
 N1, N2 = 32, 128
 TOTAL = N1 * N2
 GROUP = 8
-ARRIVALS = ((0, 3, 2, 1), (3, 1, 0, 2), (1, 3, 2, 0), (2, 1, 0, 3))
+ARRIVALS = ((0, 3, 1, 2), (0, 1, 2, 3), (0, 1, 2, 3), (1, 2, 0, 3))
 
 
 def reverse(count):

time: 180 us -> 179 us (level)
  starting transfers between devices: 75.5 us -> 70 us
  waiting for transfers between devices: 35.5 us -> 38.6 us
    ppermute x11, starting transfers between devices: 42.6 us -> 38.2 us  [exchange(): lax.ppermute(block, axis, [(i, i ^ apart) for i in range(lax.axis_size(ax...]
    ppermute x11, waiting for transfers between devices: 5.71 us -> 8.36 us  [exchange(): lax.ppermute(block, axis, [(i, i ^ apart) for i in range(lax.axis_size(ax...]
  transfers between devices with their start and end apart: 16 -> 16, of which waited for: 4 -> 5; matrix products, arithmetic and copies ran while one was open for 9% -> 9% of each run, Pallas kernels for 0% -> 0%
where the time goes in v7:
time: 179 us; the launch traced here: 178 us
  starting transfers between devices  70 us (39%)
  blocking collectives  42.4 us (24%)
  waiting for transfers between devices  38.6 us (22%)
  matrix products  8.95 us (5%)
  local copies, waits for them, and re-layouts  8.79 us (5%)
  other arithmetic  8.21 us (5%)
    ppermute x11, starting transfers between devices, exchange(): lax.ppermute(block, axis, [(i, i ^ apart) for i in range(lax.axis_size(ax...  38.2 us
    all_gather x1, blocking collectives, local(): near = lax.all_gather(swapped, 'zl')  26.5 us
    all_to_all x1, blocking collectives, local(): total = lax.all_to_all(total, 'zl', 0, 0)  16 us
    all_to_all x1, starting transfers between devices, local(): packet = lax.all_to_all(packet, SPREAD, 0, 0)  14.3 us
    all_to_all x1, waiting for transfers between devices, local(): packet = lax.all_to_all(packet, SPREAD, 0, 0)  14.1 us
    all_to_all x1, waiting for transfers between devices, local(): hidden = lax.all_to_all(hidden, SPREAD, 0, 0).reshape(256, 128)  12.4 us
    all_to_all x1, starting transfers between devices, local(): hidden = lax.all_to_all(hidden, SPREAD, 0, 0).reshape(256, 128)  8.58 us
    ppermute x11, waiting for transfers between devices, exchange(): lax.ppermute(block, axis, [(i, i ^ apart) for i in range(lax.axis_size(ax...  8.36 us
  transfers between devices with their start and end apart: 16, of which 5 were waited for; matrix products, arithmetic and copies ran while one was open for 9% of the time, Pallas kernels for 0%

profile of v7, /device:TPU:1, one launch (start us, length us, event | category | flops | bytes accessed | tf_op | source)
XLA Modules:
  0.0 177.7 jit_solution(2060058221532138187)
XLA Ops:
  0.0 1.6 collective-permute-start
  1.6 0.9 constant_dynamic-update-slice_fusion.1
  2.5 0.9 constant_dynamic-update-slice_fusion
  3.4 4.0 %collective-permute-start.1 = (bf16[256,512]{1,0:T(8,128)(2,1)S(1)}, bf16[256,512]{1,0:T(8,128)(2,1)S(1)}, u32[]{:S(2)}, u32[]{:S(2)}) collective-permute-start(bf16[256,512]{1,0:T(8,128)(2,1)S(1)} %constant_dynamic-update-slice_fusion), channel_id=1, source_target_pairs={{0,128},{128,0},{256,384},{384,256},{1,129},{129,1},{257,385},{385... | collective-permute-start | bytes 786440 | tf_op jit(solution)/shard_map/ppermute | solution.py:84
  7.5 26.5 %all-gather = bf16[512,512]{1,0:T(8,128)(2,1)S(1)} all-gather(bf16[128,512]{1,0:T(8,128)(2,1)S(1)} %maximum_select_fusion), channel_id=2, replica_groups=mesh['y'=4,'zh'=4,'core'=2,'x'=4,'zl'=4] {'zl'}, dimensions={0}, use_global_device_ids=true | all-gather | bytes 655360 | tf_op jit(solution)/shard_map/all_gather | solution.py:101
  34.1 0.0 collective-permute-done.1
  34.1 1.5 broadcast_in_dim.6
  35.6 4.0 %all-to-all-start = ((bf16[4,512,512]{2,1,0:T(8,128)(2,1)}), bf16[4,512,512]{2,1,0:T(8,128)(2,1)S(1)}, u32[]{:S(2)}, u32[]{:S(2)}) async-start(bf16[4,512,512]{2,1,0:T(8,128)(2,1)} %broadcast_in_dim.6), calls=%async_computation | async-start | bytes 4194304 | tf_op jit(solution)/shard_map/all_to_all | solution.py:69
  39.6 4.8 %collective-permute-start.3 = (bf16[256,512]{1,0:T(8,128)(2,1)S(1)}, bf16[256,512]{1,0:T(8,128)(2,1)S(1)}, u32[]{:S(2)}, u32[]{:S(2)}) collective-permute-start(bf16[256,512]{1,0:T(8,128)(2,1)S(1)} %constant_dynamic-update-slice_fusion), channel_id=1, source_target_pairs={{0,384},{128,256},{256,128},{384,0},{1,385},{129,257},{257,129},{3... | collective-permute-start | bytes 786440 | tf_op jit(solution)/shard_map/ppermute | solution.py:84
  44.4 1.9 %collective-permute-start.2 = (bf16[256,512]{1,0:T(8,128)(2,1)S(1)}, bf16[256,512]{1,0:T(8,128)(2,1)S(1)}, u32[]{:S(2)}, u32[]{:S(2)}) collective-permute-start(bf16[256,512]{1,0:T(8,128)(2,1)S(1)} %collective-permute-done.1), channel_id=1, source_target_pairs={{0,384},{128,256},{256,128},{384,0},{1,385},{129,257},{257,129},{3... | collective-permute-start | bytes 786440 | tf_op jit(solution)/shard_map/ppermute | solution.py:84
  46.3 0.9 pad_maximum_fusion.2
  47.2 5.2 %collective-permute-start.4 = (bf16[2,256,512]{2,1,0:T(8,128)(2,1)}, bf16[2,256,512]{2,1,0:T(8,128)(2,1)}, u32[]{:S(2)}, u32[]{:S(2)}) collective-permute-start(bf16[2,256,512]{2,1,0:T(8,128)(2,1)} %pad_maximum_fusion.2), channel_id=1, source_target_pairs={{0,16},{16,0},{1,17},{17,1},{2,18},{18,2},{3,19},{19,3},{4,20},{20... | collective-permute-start | bytes 1572872 | tf_op jit(solution)/shard_map/ppermute | solution.py:84
  52.4 0.0 collective-permute-done.3
  52.4 2.7 %collective-permute-done.2 = bf16[256,512]{1,0:T(8,128)(2,1)S(1)} collective-permute-done((bf16[256,512]{1,0:T(8,128)(2,1)S(1)}, bf16[256,512]{1,0:T(8,128)(2,1)S(1)}, u32[]{:S(2)}, u32[]{:S(2)}) %collective-permute-start.2) | collective-permute-done | bytes 262176 | tf_op jit(solution)/shard_map/ppermute | solution.py:84
  55.1 0.9 pad_maximum_fusion.3
  56.0 4.5 %collective-permute-start.5 = (bf16[2,256,512]{2,1,0:T(8,128)(2,1)}, bf16[2,256,512]{2,1,0:T(8,128)(2,1)}, u32[]{:S(2)}, u32[]{:S(2)}) collective-permute-start(bf16[2,256,512]{2,1,0:T(8,128)(2,1)} %pad_maximum_fusion.3), channel_id=1, source_target_pairs={{0,16},{16,0},{1,17},{17,1},{2,18},{18,2},{3,19},{19,3},{4,20},{20... | collective-permute-start | bytes 1572872 | tf_op jit(solution)/shard_map/ppermute | solution.py:84
  60.6 0.2 fusion.21
  60.8 0.7 fusion.15
  61.5 1.1 pad_maximum_fusion
  62.6 0.0 collective-permute-done.4
  62.6 0.0 collective-permute-done.5
  62.6 1.6 dynamic-slice_select_fusion.3
  64.2 1.1 pad_maximum_fusion.1
  65.3 2.0 %convolution_bitcast_fusion = f32[512,512]{0,1:T(8,128)S(1)} fusion(bf16[4,256,512]{2,1,0:T(8,128)(2,1)} %pad_maximum_fusion.1, bf16[4,512,512]{2,1,0:T(8,128)(2,1)S(1)} %all-to-all-done), kind=kOutput, calls=%fused_computation.7 | convolution fusion | flops 536870912 | bytes 3145728 | tf_op jit(solution)/shard_map/xkc,xtk->ct/dot_general | solution.py:121
  67.4 0.7 fusion.6
  68.2 1.1 copy.21
  69.3 14.3 %all-to-all-start.1 = ((bf16[32,8,1280]{2,1,0:T(8,128)(2,1)}), bf16[32,8,1280]{2,1,0:T(8,128)(2,1)S(1)}, u32[]{:S(2)}, u32[]{:S(2)}) async-start(bf16[32,8,1280]{2,1,0:T(8,128)(2,1)} %bitcast.13), calls=%async_computation.1 | async-start | bytes 1310720 | tf_op jit(solution)/shard_map/all_to_all | solution.py:126
  83.6 0.0 copy-start.3
  83.6 3.0 %fusion.62 = (bf16[128,2048]{1,0:T(8,128)(2,1)S(1)}, bf16[128,2048]{1,0:T(8,128)(2,1)S(1)}, bf16[128,2048]{1,0:T(8,128)(2,1)}, bf16[128,2048]{1,0:T(8,128)(2,1)}, bf16[128,2048]{1,0:T(8,128)(2,1)S(1)}) fusion(bf16[256,8192]{1,0:T(8,128)(2,1)} %param.14, s32[]{:T(128)S(6)} %select_n.239, s32[]{:T(128)S(6)} %select_n.245, s32[]{:T(128)S(6)} %select_n.246, ...), kind=kLoop, calls=%fused_computation.125 | loop fusion | bytes 5242904 | tf_op jit(solution)/shard_map/dynamic_slice | solution.py:129
  86.6 2.3 %collective-permute-start.6 = (bf16[128,2048]{1,0:T(8,128)(2,1)S(1)}, bf16[128,2048]{1,0:T(8,128)(2,1)}, u32[]{:S(2)}, u32[]{:S(2)}) collective-permute-start(bf16[128,2048]{1,0:T(8,128)(2,1)S(1)} %get-tuple-element.29), channel_id=1, source_target_pairs={{0,4},{4,0},{8,12},{12,8},{1,5},{5,1},{9,13},{13,9},{2,6},{6,2},{1... | collective-permute-start | bytes 1572872 | tf_op jit(solution)/shard_map/ppermute | solution.py:84
  88.9 3.7 %collective-permute-start.9 = (bf16[128,2048]{1,0:T(8,128)(2,1)}, bf16[128,2048]{1,0:T(8,128)(2,1)S(1)}, u32[]{:S(2)}, u32[]{:S(2)}) collective-permute-start(bf16[128,2048]{1,0:T(8,128)(2,1)} %get-tuple-element.27), channel_id=1, source_target_pairs={{0,8},{4,12},{8,0},{12,4},{1,9},{5,13},{9,1},{13,5},{2,10},{6,14},... | collective-permute-start | bytes 1572872 | tf_op jit(solution)/shard_map/ppermute | solution.py:84
  92.6 3.7 %collective-permute-start.8 = (bf16[128,2048]{1,0:T(8,128)(2,1)}, bf16[128,2048]{1,0:T(8,128)(2,1)S(1)}, u32[]{:S(2)}, u32[]{:S(2)}) collective-permute-start(bf16[128,2048]{1,0:T(8,128)(2,1)} %get-tuple-element.28), channel_id=1, source_target_pairs={{0,12},{4,8},{8,4},{12,0},{1,13},{5,9},{9,5},{13,1},{2,14},{6,10},... | collective-permute-start | bytes 1572872 | tf_op jit(solution)/shard_map/ppermute | solution.py:84
  96.3 5.7 %collective-permute-done.6 = bf16[128,2048]{1,0:T(8,128)(2,1)} collective-permute-done((bf16[128,2048]{1,0:T(8,128)(2,1)S(1)}, bf16[128,2048]{1,0:T(8,128)(2,1)}, u32[]{:S(2)}, u32[]{:S(2)}) %collective-permute-start.6) | collective-permute-done | bytes 524320 | tf_op jit(solution)/shard_map/ppermute | solution.py:84
  102.0 3.6 %collective-permute-start.7 = (bf16[128,2048]{1,0:T(8,128)(2,1)}, bf16[128,2048]{1,0:T(8,128)(2,1)}, u32[]{:S(2)}, u32[]{:S(2)}) collective-permute-start(bf16[128,2048]{1,0:T(8,128)(2,1)} %collective-permute-done.6), channel_id=1, source_target_pairs={{0,16},{16,0},{1,17},{17,1},{2,18},{18,2},{3,19},{19,3},{4,20},{20... | collective-permute-start | bytes 1572872 | tf_op jit(solution)/shard_map/ppermute | solution.py:84
  105.6 14.1 %all-to-all-done.1 = bf16[32,8,1280]{2,1,0:T(8,128)(2,1)S(1)} async-done(((bf16[32,8,1280]{2,1,0:T(8,128)(2,1)}), bf16[32,8,1280]{2,1,0:T(8,128)(2,1)S(1)}, u32[]{:S(2)}, u32[]{:S(2)}) %all-to-all-start.1) | async-done | bytes 655392 | tf_op jit(solution)/shard_map/all_to_all | solution.py:126
  119.8 0.0 copy-start.7
  119.8 0.4 fusion.67
  120.2 0.0 copy-start.5
  120.3 0.0 copy-start.4
  120.3 0.3 copy-done.8
  120.6 0.4 fusion.26
  121.0 0.4 fusion.30
  121.4 0.3 fusion.42
  121.8 0.3 fusion.7
  122.1 0.1 copy.25
  122.2 0.7 fusion.35
  122.9 8.6 %all-to-all-start.2 = ((bf16[32,8,128]{2,1,0:T(8,128)(2,1)}), bf16[32,8,128]{2,1,0:T(8,128)(2,1)S(1)}, u32[]{:S(2)}, u32[]{:S(2)}) async-start(bf16[32,8,128]{2,1,0:T(8,128)(2,1)} %fusion.35), calls=%async_computation.2 | async-start | bytes 131072 | tf_op jit(solution)/shard_map/all_to_all | solution.py:137
  131.5 0.0 collective-permute-done.9
  131.5 2.1 %collective-permute-start.11 = (bf16[128,2048]{1,0:T(8,128)(2,1)S(1)}, bf16[128,2048]{1,0:T(8,128)(2,1)S(1)}, u32[]{:S(2)}, u32[]{:S(2)}) collective-permute-start(bf16[128,2048]{1,0:T(8,128)(2,1)S(1)} %collective-permute-done.9), channel_id=1, source_target_pairs={{0,16},{16,0},{1,17},{17,1},{2,18},{18,2},{3,19},{19,3},{4,20},{20... | collective-permute-start | bytes 1572872 | tf_op jit(solution)/shard_map/ppermute | solution.py:84
  133.7 0.0 collective-permute-done.8
  133.7 12.4 %all-to-all-done.2 = bf16[32,8,128]{2,1,0:T(8,128)(2,1)S(1)} async-done(((bf16[32,8,128]{2,1,0:T(8,128)(2,1)}), bf16[32,8,128]{2,1,0:T(8,128)(2,1)S(1)}, u32[]{:S(2)}, u32[]{:S(2)}) %all-to-all-start.2) | async-done | bytes 65568 | tf_op jit(solution)/shard_map/all_to_all | solution.py:137
  146.1 0.7 broadcast_in_dim.7
  146.9 3.4 %all-to-all-start.3 = ((bf16[4,256,128]{2,1,0:T(8,128)(2,1)}), bf16[4,256,128]{2,1,0:T(8,128)(2,1)S(1)}, u32[]{:S(2)}, u32[]{:S(2)}) async-start(bf16[4,256,128]{2,1,0:T(8,128)(2,1)} %broadcast_in_dim.7), calls=%async_computation.3 | async-start | bytes 524288 | tf_op jit(solution)/shard_map/all_to_all | solution.py:69
  150.3 2.3 %collective-permute-start.10 = (bf16[128,2048]{1,0:T(8,128)(2,1)S(1)}, bf16[128,2048]{1,0:T(8,128)(2,1)S(1)}, u32[]{:S(2)}, u32[]{:S(2)}) collective-permute-start(bf16[128,2048]{1,0:T(8,128)(2,1)S(1)} %collective-permute-done.8), channel_id=1, source_target_pairs={{0,16},{16,0},{1,17},{17,1},{2,18},{18,2},{3,19},{19,3},{4,20},{20... | collective-permute-start | bytes 1572872 | tf_op jit(solution)/shard_map/ppermute | solution.py:84
  152.6 3.7 %all-to-all-done.3 = bf16[4,256,128]{2,1,0:T(8,128)(2,1)S(1)} async-done(((bf16[4,256,128]{2,1,0:T(8,128)(2,1)}), bf16[4,256,128]{2,1,0:T(8,128)(2,1)S(1)}, u32[]{:S(2)}, u32[]{:S(2)}) %all-to-all-start.3) | async-done | bytes 262176 | tf_op jit(solution)/shard_map/all_to_all | solution.py:69
  156.4 0.3 fusion.49
  156.7 0.3 fusion.48
  157.0 0.3 fusion.51
  157.4 0.3 fusion.50
  157.7 0.3 fusion.8
  158.0 1.4 convolution_add_fusion.1
  159.4 1.5 fusion.4
  161.0 16.0 %all_to_all.25 = bf16[4,128,512]{2,1,0:T(8,128)(2,1)S(1)} all-to-all(bf16[4,128,512]{2,1,0:T(8,128)(2,1)S(1)} %bitcast.126), channel_id=1, replica_groups=mesh['y'=4,'zh'=4,'core'=2,'x'=4,'zl'=4] {'zl'}, dimensions={0} | all-to-all | bytes 1048576 | tf_op jit(solution)/shard_map/all_to_all | solution.py:148
  176.9 0.7 reduce_sum.32
  (36 shorter events, 0.6 us)
Async XLA Ops:
  0.0 7.5 %collective-permute-start = (bf16[128,512]{1,0:T(8,128)(2,1)}, bf16[128,512]{1,0:T(8,128)(2,1)S(1)}, u32[]{:S(2)}, u32[]{:S(2)}) collective-permute-start(bf16[128,512]{1,0:T(8,128)(2,1)} %param.11), channel_id=1, source_target_pairs={{0,0},{1,32},{2,64},{3,98},{32,2},{33,33},{34,65},{35,96},{64,3},{... | collective-permute-start | bytes 393224 | tf_op jit(solution)/shard_map/ppermute | solution.py:99
  3.4 30.7 %collective-permute-start.1 = (bf16[256,512]{1,0:T(8,128)(2,1)S(1)}, bf16[256,512]{1,0:T(8,128)(2,1)S(1)}, u32[]{:S(2)}, u32[]{:S(2)}) collective-permute-start(bf16[256,512]{1,0:T(8,128)(2,1)S(1)} %constant_dynamic-update-slice_fusion), channel_id=1, source_target_pairs={{0,128},{128,0},{256,384},{384,256},{1,129},{129,1},{257,385},{385... | collective-permute-start | bytes 786440 | tf_op jit(solution)/shard_map/ppermute | solution.py:84
  35.6 29.7 %all-to-all-start = ((bf16[4,512,512]{2,1,0:T(8,128)(2,1)}), bf16[4,512,512]{2,1,0:T(8,128)(2,1)S(1)}, u32[]{:S(2)}, u32[]{:S(2)}) async-start(bf16[4,512,512]{2,1,0:T(8,128)(2,1)} %broadcast_in_dim.6), calls=%async_computation | async-start | bytes 4194304 | tf_op jit(solution)/shard_map/all_to_all | solution.py:69
  39.6 20.9 %copy-start.6 = (f32[2,128,256]{2,1,0:T(8,128)S(1)}, f32[2,128,256]{2,1,0:T(8,128)}, u32[]{:S(2)}) copy-start(f32[2,128,256]{2,1,0:T(8,128)} %param.15) | copy-start | bytes 786436
  39.6 12.8 %collective-permute-start.3 = (bf16[256,512]{1,0:T(8,128)(2,1)S(1)}, bf16[256,512]{1,0:T(8,128)(2,1)S(1)}, u32[]{:S(2)}, u32[]{:S(2)}) collective-permute-start(bf16[256,512]{1,0:T(8,128)(2,1)S(1)} %constant_dynamic-update-slice_fusion), channel_id=1, source_target_pairs={{0,384},{128,256},{256,128},{384,0},{1,385},{129,257},{257,129},{3... | collective-permute-start | bytes 786440 | tf_op jit(solution)/shard_map/ppermute | solution.py:84
  44.4 10.7 %collective-permute-start.2 = (bf16[256,512]{1,0:T(8,128)(2,1)S(1)}, bf16[256,512]{1,0:T(8,128)(2,1)S(1)}, u32[]{:S(2)}, u32[]{:S(2)}) collective-permute-start(bf16[256,512]{1,0:T(8,128)(2,1)S(1)} %collective-permute-done.1), channel_id=1, source_target_pairs={{0,384},{128,256},{256,128},{384,0},{1,385},{129,257},{257,129},{3... | collective-permute-start | bytes 786440 | tf_op jit(solution)/shard_map/ppermute | solution.py:84
  47.2 15.4 %collective-permute-start.4 = (bf16[2,256,512]{2,1,0:T(8,128)(2,1)}, bf16[2,256,512]{2,1,0:T(8,128)(2,1)}, u32[]{:S(2)}, u32[]{:S(2)}) collective-permute-start(bf16[2,256,512]{2,1,0:T(8,128)(2,1)} %pad_maximum_fusion.2), channel_id=1, source_target_pairs={{0,16},{16,0},{1,17},{17,1},{2,18},{18,2},{3,19},{19,3},{4,20},{20... | collective-permute-start | bytes 1572872 | tf_op jit(solution)/shard_map/ppermute | solution.py:84
  56.0 6.6 %collective-permute-start.5 = (bf16[2,256,512]{2,1,0:T(8,128)(2,1)}, bf16[2,256,512]{2,1,0:T(8,128)(2,1)}, u32[]{:S(2)}, u32[]{:S(2)}) collective-permute-start(bf16[2,256,512]{2,1,0:T(8,128)(2,1)} %pad_maximum_fusion.3), channel_id=1, source_target_pairs={{0,16},{16,0},{1,17},{17,1},{2,18},{18,2},{3,19},{19,3},{4,20},{20... | collective-permute-start | bytes 1572872 | tf_op jit(solution)/shard_map/ppermute | solution.py:84
  65.3 2.0 %copy-start.2 = (bf16[4,256,512]{2,1,0:T(8,128)(2,1)S(1)}, bf16[4,256,512]{2,1,0:T(8,128)(2,1)}, u32[]{:S(2)}) copy-start(bf16[4,256,512]{2,1,0:T(8,128)(2,1)} %pad_maximum_fusion) | copy-start | bytes 3145732
  69.3 50.4 %all-to-all-start.1 = ((bf16[32,8,1280]{2,1,0:T(8,128)(2,1)}), bf16[32,8,1280]{2,1,0:T(8,128)(2,1)S(1)}, u32[]{:S(2)}, u32[]{:S(2)}) async-start(bf16[32,8,1280]{2,1,0:T(8,128)(2,1)} %bitcast.13), calls=%async_computation.1 | async-start | bytes 1310720 | tf_op jit(solution)/shard_map/all_to_all | solution.py:126
  83.6 36.2 %copy-start.3 = (f32[512,256]{1,0:T(8,128)S(1)}, f32[512,256]{1,0:T(8,128)}, u32[]{:S(2)}) copy-start(f32[512,256]{1,0:T(8,128)} %constant.166) | copy-start | bytes 1572868
  86.6 33.6 %copy-start = (f32[256,128]{1,0:T(8,128)S(1)}, f32[256,128]{1,0:T(8,128)}, u32[]{:S(2)}) copy-start(f32[256,128]{1,0:T(8,128)} %constant.159.clone) | copy-start | bytes 393220
  86.6 33.6 %copy-start.1 = (f32[256,128]{1,0:T(8,128)S(1)}, f32[256,128]{1,0:T(8,128)}, u32[]{:S(2)}) copy-start(f32[256,128]{1,0:T(8,128)} %constant.158.clone) | copy-start | bytes 393220
  86.6 15.4 %collective-permute-start.6 = (bf16[128,2048]{1,0:T(8,128)(2,1)S(1)}, bf16[128,2048]{1,0:T(8,128)(2,1)}, u32[]{:S(2)}, u32[]{:S(2)}) collective-permute-start(bf16[128,2048]{1,0:T(8,128)(2,1)S(1)} %get-tuple-element.29), channel_id=1, source_target_pairs={{0,4},{4,0},{8,12},{12,8},{1,5},{5,1},{9,13},{13,9},{2,6},{6,2},{1... | collective-permute-start | bytes 1572872 | tf_op jit(solution)/shard_map/ppermute | solution.py:84
  88.9 42.6 %collective-permute-start.9 = (bf16[128,2048]{1,0:T(8,128)(2,1)}, bf16[128,2048]{1,0:T(8,128)(2,1)S(1)}, u32[]{:S(2)}, u32[]{:S(2)}) collective-permute-start(bf16[128,2048]{1,0:T(8,128)(2,1)} %get-tuple-element.27), channel_id=1, source_target_pairs={{0,8},{4,12},{8,0},{12,4},{1,9},{5,13},{9,1},{13,5},{2,10},{6,14},... | collective-permute-start | bytes 1572872 | tf_op jit(solution)/shard_map/ppermute | solution.py:84
  92.6 41.0 %collective-permute-start.8 = (bf16[128,2048]{1,0:T(8,128)(2,1)}, bf16[128,2048]{1,0:T(8,128)(2,1)S(1)}, u32[]{:S(2)}, u32[]{:S(2)}) collective-permute-start(bf16[128,2048]{1,0:T(8,128)(2,1)} %get-tuple-element.28), channel_id=1, source_target_pairs={{0,12},{4,8},{8,4},{12,0},{1,13},{5,9},{9,5},{13,1},{2,14},{6,10},... | collective-permute-start | bytes 1572872 | tf_op jit(solution)/shard_map/ppermute | solution.py:84
  102.0 31.7 %collective-permute-start.7 = (bf16[128,2048]{1,0:T(8,128)(2,1)}, bf16[128,2048]{1,0:T(8,128)(2,1)}, u32[]{:S(2)}, u32[]{:S(2)}) collective-permute-start(bf16[128,2048]{1,0:T(8,128)(2,1)} %collective-permute-done.6), channel_id=1, source_target_pairs={{0,16},{16,0},{1,17},{17,1},{2,18},{18,2},{3,19},{19,3},{4,20},{20... | collective-permute-start | bytes 1572872 | tf_op jit(solution)/shard_map/ppermute | solution.py:84
  119.7 0.9 copy-start.8
  119.8 1.2 copy-start.7
  120.2 1.2 copy-start.5
  120.3 1.5 copy-start.4
  122.9 23.2 %all-to-all-start.2 = ((bf16[32,8,128]{2,1,0:T(8,128)(2,1)}), bf16[32,8,128]{2,1,0:T(8,128)(2,1)S(1)}, u32[]{:S(2)}, u32[]{:S(2)}) async-start(bf16[32,8,128]{2,1,0:T(8,128)(2,1)} %fusion.35), calls=%async_computation.2 | async-start | bytes 131072 | tf_op jit(solution)/shard_map/all_to_all | solution.py:137
  131.5 25.2 %collective-permute-start.11 = (bf16[128,2048]{1,0:T(8,128)(2,1)S(1)}, bf16[128,2048]{1,0:T(8,128)(2,1)S(1)}, u32[]{:S(2)}, u32[]{:S(2)}) collective-permute-start(bf16[128,2048]{1,0:T(8,128)(2,1)S(1)} %collective-permute-done.9), channel_id=1, source_target_pairs={{0,16},{16,0},{1,17},{17,1},{2,18},{18,2},{3,19},{19,3},{4,20},{20... | collective-permute-start | bytes 1572872 | tf_op jit(solution)/shard_map/ppermute | solution.py:84
  146.9 9.5 %all-to-all-start.3 = ((bf16[4,256,128]{2,1,0:T(8,128)(2,1)}), bf16[4,256,128]{2,1,0:T(8,128)(2,1)S(1)}, u32[]{:S(2)}, u32[]{:S(2)}) async-start(bf16[4,256,128]{2,1,0:T(8,128)(2,1)} %broadcast_in_dim.7), calls=%async_computation.3 | async-start | bytes 524288 | tf_op jit(solution)/shard_map/all_to_all | solution.py:69
  150.3 7.0 %collective-permute-start.10 = (bf16[128,2048]{1,0:T(8,128)(2,1)S(1)}, bf16[128,2048]{1,0:T(8,128)(2,1)S(1)}, u32[]{:S(2)}, u32[]{:S(2)}) collective-permute-start(bf16[128,2048]{1,0:T(8,128)(2,1)S(1)} %collective-permute-done.8), channel_id=1, source_target_pairs={{0,16},{16,0},{1,17},{17,1},{2,18},{18,2},{3,19},{19,3},{4,20},{20... | collective-permute-start | bytes 1572872 | tf_op jit(solution)/shard_map/ppermute | solution.py:84

commit v8 on v7

--- a/solution.py
+++ b/solution.py
@@ -126,7 +126,7 @@
     packet = lax.all_to_all(packet, SPREAD, 0, 0)
 
     held = after(out_weight, value)
-    own = jnp.concatenate([lax.dynamic_slice(held, (part * 128, column * 2048), (128, 2048)) for part in (core, 1 - core)])
+    own = lax.dynamic_slice_in_dim(held, column * 2048, 2048, 1)
     half = {k: exchange(lax.dynamic_slice(held, (core * 128, (column ^ k) * 2048), (128, 2048)), "x", k) for k in (1, 2, 3)}
     other = {k: exchange(half[k], "core", 1) for k in (1, 2, 3)}
 
@@ -137,9 +137,9 @@
     hidden = lax.all_to_all(hidden, SPREAD, 0, 0).reshape(256, 128)
     hidden, other[1], half[3], half[2] = lax.optimization_barrier((hidden, other[1], half[3], half[2]))
 
+    total = jnp.einsum("ct,cd->td", hidden, own, preferred_element_type=jnp.float32)
     hidden = jnp.where(core == 0, hidden, jnp.concatenate([hidden[128:], hidden[:128]]))
     hidden = gather_over(hidden, "x")
-    total = jnp.einsum("ct,cd->td", pick(hidden, column), own, preferred_element_type=jnp.float32)
     for k in (1, 3, 2):
         rows = pick(hidden, column ^ k)
         for part, weight in ((rows[:128], half[k]), (rows[128:], other[k])):

time: 179 us -> 178 us (level)
    dot_general x6, matrix products: 4.18 us -> 1.97 us  [local(): jnp.einsum('ct,cd->td', part, weight, preferred_element_type=jnp.float32)]
where the time goes in v8:
time: 178 us; the launch traced here: 177 us
  starting transfers between devices  69.4 us (39%)
  blocking collectives  42.4 us (24%)
  waiting for transfers between devices  39.6 us (22%)
  local copies, waits for them, and re-layouts  8.43 us (5%)
  other arithmetic  8.21 us (5%)
  matrix products  8.19 us (5%)
    ppermute x11, starting transfers between devices, exchange(): lax.ppermute(block, axis, [(i, i ^ apart) for i in range(lax.axis_size(ax...  37.6 us
    all_gather x1, blocking collectives, local(): near = lax.all_gather(swapped, 'zl')  26.5 us
    all_to_all x1, blocking collectives, local(): total = lax.all_to_all(total, 'zl', 0, 0)  16 us
    all_to_all x1, waiting for transfers between devices, local(): packet = lax.all_to_all(packet, SPREAD, 0, 0)  14.5 us
    all_to_all x1, starting transfers between devices, local(): packet = lax.all_to_all(packet, SPREAD, 0, 0)  14.3 us
    all_to_all x1, waiting for transfers between devices, local(): hidden = lax.all_to_all(hidden, SPREAD, 0, 0).reshape(256, 128)  12.4 us
    ppermute x11, waiting for transfers between devices, exchange(): lax.ppermute(block, axis, [(i, i ^ apart) for i in range(lax.axis_size(ax...  8.86 us
    all_to_all x1, starting transfers between devices, local(): hidden = lax.all_to_all(hidden, SPREAD, 0, 0).reshape(256, 128)  8.57 us
  transfers between devices with their start and end apart: 16, of which 5 were waited for; matrix products, arithmetic and copies ran while one was open for 9% of the time, Pallas kernels for 0%

profile of v8, /device:TPU:1, one launch (start us, length us, event | category | flops | bytes accessed | tf_op | source)
XLA Modules:
  0.0 176.9 jit_solution(11391509582694717822)
XLA Ops:
  0.0 1.6 collective-permute-start
  1.6 0.9 constant_dynamic-update-slice_fusion.1
  2.5 0.9 constant_dynamic-update-slice_fusion
  3.4 4.0 %collective-permute-start.1 = (bf16[256,512]{1,0:T(8,128)(2,1)S(1)}, bf16[256,512]{1,0:T(8,128)(2,1)S(1)}, u32[]{:S(2)}, u32[]{:S(2)}) collective-permute-start(bf16[256,512]{1,0:T(8,128)(2,1)S(1)} %constant_dynamic-update-slice_fusion), channel_id=1, source_target_pairs={{0,128},{128,0},{256,384},{384,256},{1,129},{129,1},{257,385},{385... | collective-permute-start | bytes 786440 | tf_op jit(solution)/shard_map/ppermute | solution.py:84
  7.5 26.5 %all-gather = bf16[512,512]{1,0:T(8,128)(2,1)S(1)} all-gather(bf16[128,512]{1,0:T(8,128)(2,1)S(1)} %maximum_select_fusion), channel_id=2, replica_groups=mesh['y'=4,'zh'=4,'core'=2,'x'=4,'zl'=4] {'zl'}, dimensions={0}, use_global_device_ids=true | all-gather | bytes 655360 | tf_op jit(solution)/shard_map/all_gather | solution.py:101
  34.1 0.0 collective-permute-done.1
  34.1 1.5 broadcast_in_dim.6
  35.6 4.0 %all-to-all-start = ((bf16[4,512,512]{2,1,0:T(8,128)(2,1)}), bf16[4,512,512]{2,1,0:T(8,128)(2,1)S(1)}, u32[]{:S(2)}, u32[]{:S(2)}) async-start(bf16[4,512,512]{2,1,0:T(8,128)(2,1)} %broadcast_in_dim.6), calls=%async_computation | async-start | bytes 4194304 | tf_op jit(solution)/shard_map/all_to_all | solution.py:69
  39.6 4.8 %collective-permute-start.3 = (bf16[256,512]{1,0:T(8,128)(2,1)S(1)}, bf16[256,512]{1,0:T(8,128)(2,1)S(1)}, u32[]{:S(2)}, u32[]{:S(2)}) collective-permute-start(bf16[256,512]{1,0:T(8,128)(2,1)S(1)} %constant_dynamic-update-slice_fusion), channel_id=1, source_target_pairs={{0,384},{128,256},{256,128},{384,0},{1,385},{129,257},{257,129},{3... | collective-permute-start | bytes 786440 | tf_op jit(solution)/shard_map/ppermute | solution.py:84
  44.4 1.9 %collective-permute-start.2 = (bf16[256,512]{1,0:T(8,128)(2,1)S(1)}, bf16[256,512]{1,0:T(8,128)(2,1)S(1)}, u32[]{:S(2)}, u32[]{:S(2)}) collective-permute-start(bf16[256,512]{1,0:T(8,128)(2,1)S(1)} %collective-permute-done.1), channel_id=1, source_target_pairs={{0,384},{128,256},{256,128},{384,0},{1,385},{129,257},{257,129},{3... | collective-permute-start | bytes 786440 | tf_op jit(solution)/shard_map/ppermute | solution.py:84
  46.3 0.9 pad_maximum_fusion.2
  47.2 5.2 %collective-permute-start.4 = (bf16[2,256,512]{2,1,0:T(8,128)(2,1)}, bf16[2,256,512]{2,1,0:T(8,128)(2,1)}, u32[]{:S(2)}, u32[]{:S(2)}) collective-permute-start(bf16[2,256,512]{2,1,0:T(8,128)(2,1)} %pad_maximum_fusion.2), channel_id=1, source_target_pairs={{0,16},{16,0},{1,17},{17,1},{2,18},{18,2},{3,19},{19,3},{4,20},{20... | collective-permute-start | bytes 1572872 | tf_op jit(solution)/shard_map/ppermute | solution.py:84
  52.4 0.0 collective-permute-done.3
  52.4 2.7 %collective-permute-done.2 = bf16[256,512]{1,0:T(8,128)(2,1)S(1)} collective-permute-done((bf16[256,512]{1,0:T(8,128)(2,1)S(1)}, bf16[256,512]{1,0:T(8,128)(2,1)S(1)}, u32[]{:S(2)}, u32[]{:S(2)}) %collective-permute-start.2) | collective-permute-done | bytes 262176 | tf_op jit(solution)/shard_map/ppermute | solution.py:84
  55.1 0.9 pad_maximum_fusion.3
  56.0 4.5 %collective-permute-start.5 = (bf16[2,256,512]{2,1,0:T(8,128)(2,1)}, bf16[2,256,512]{2,1,0:T(8,128)(2,1)}, u32[]{:S(2)}, u32[]{:S(2)}) collective-permute-start(bf16[2,256,512]{2,1,0:T(8,128)(2,1)} %pad_maximum_fusion.3), channel_id=1, source_target_pairs={{0,16},{16,0},{1,17},{17,1},{2,18},{18,2},{3,19},{19,3},{4,20},{20... | collective-permute-start | bytes 1572872 | tf_op jit(solution)/shard_map/ppermute | solution.py:84
  60.6 0.2 fusion.19
  60.8 0.7 fusion.13
  61.5 1.1 pad_maximum_fusion
  62.6 0.0 collective-permute-done.4
  62.6 0.0 collective-permute-done.5
  62.6 1.6 dynamic-slice_select_fusion.3
  64.2 1.1 pad_maximum_fusion.1
  65.3 2.0 %convolution_bitcast_fusion = f32[512,512]{0,1:T(8,128)S(1)} fusion(bf16[4,256,512]{2,1,0:T(8,128)(2,1)} %pad_maximum_fusion.1, bf16[4,512,512]{2,1,0:T(8,128)(2,1)S(1)} %all-to-all-done), kind=kOutput, calls=%fused_computation.7 | convolution fusion | flops 536870912 | bytes 3145728 | tf_op jit(solution)/shard_map/xkc,xtk->ct/dot_general | solution.py:121
  67.4 0.7 fusion.7
  68.2 1.1 copy.21
  69.3 14.3 %all-to-all-start.1 = ((bf16[32,8,1280]{2,1,0:T(8,128)(2,1)}), bf16[32,8,1280]{2,1,0:T(8,128)(2,1)S(1)}, u32[]{:S(2)}, u32[]{:S(2)}) async-start(bf16[32,8,1280]{2,1,0:T(8,128)(2,1)} %bitcast.13), calls=%async_computation.1 | async-start | bytes 1310720 | tf_op jit(solution)/shard_map/all_to_all | solution.py:126
  83.6 0.0 copy-start.3
  83.6 2.6 %fusion.59 = (bf16[128,2048]{1,0:T(8,128)(2,1)}, bf16[128,2048]{1,0:T(8,128)(2,1)}, bf16[128,2048]{1,0:T(8,128)(2,1)S(1)}) fusion(bf16[256,8192]{1,0:T(8,128)(2,1)} %param.14, s32[]{:T(128)S(6)} %select_n.230, s32[]{:T(128)S(6)} %select_n.232, s32[]{:T(128)S(6)} %select_n.233, s32[]{:T(128)S(6)} %select_n.231), kind=kLoop, calls=%fused_computation.121 | loop fusion | bytes 3145744 | tf_op jit(solution)/shard_map/dynamic_slice | solution.py:130
  86.2 2.3 %collective-permute-start.6 = (bf16[128,2048]{1,0:T(8,128)(2,1)S(1)}, bf16[128,2048]{1,0:T(8,128)(2,1)S(1)}, u32[]{:S(2)}, u32[]{:S(2)}) collective-permute-start(bf16[128,2048]{1,0:T(8,128)(2,1)S(1)} %get-tuple-element.27), channel_id=1, source_target_pairs={{0,4},{4,0},{8,12},{12,8},{1,5},{5,1},{9,13},{13,9},{2,6},{6,2},{1... | collective-permute-start | bytes 1572872 | tf_op jit(solution)/shard_map/ppermute | solution.py:84
  88.6 2.8 %collective-permute-start.8 = (bf16[128,2048]{1,0:T(8,128)(2,1)}, bf16[128,2048]{1,0:T(8,128)(2,1)S(1)}, u32[]{:S(2)}, u32[]{:S(2)}) collective-permute-start(bf16[128,2048]{1,0:T(8,128)(2,1)} %get-tuple-element.25), channel_id=1, source_target_pairs={{0,12},{4,8},{8,4},{12,0},{1,13},{5,9},{9,5},{13,1},{2,14},{6,10},... | collective-permute-start | bytes 1572872 | tf_op jit(solution)/shard_map/ppermute | solution.py:84
  91.3 4.0 %collective-permute-start.9 = (bf16[128,2048]{1,0:T(8,128)(2,1)}, bf16[128,2048]{1,0:T(8,128)(2,1)S(1)}, u32[]{:S(2)}, u32[]{:S(2)}) collective-permute-start(bf16[128,2048]{1,0:T(8,128)(2,1)} %get-tuple-element.26), channel_id=1, source_target_pairs={{0,8},{4,12},{8,0},{12,4},{1,9},{5,13},{9,1},{13,5},{2,10},{6,14},... | collective-permute-start | bytes 1572872 | tf_op jit(solution)/shard_map/ppermute | solution.py:84
  95.4 6.2 %collective-permute-done.6 = bf16[128,2048]{1,0:T(8,128)(2,1)S(1)} collective-permute-done((bf16[128,2048]{1,0:T(8,128)(2,1)S(1)}, bf16[128,2048]{1,0:T(8,128)(2,1)S(1)}, u32[]{:S(2)}, u32[]{:S(2)}) %collective-permute-start.6) | collective-permute-done | bytes 524320 | tf_op jit(solution)/shard_map/ppermute | solution.py:84
  101.5 3.6 %collective-permute-start.7 = (bf16[128,2048]{1,0:T(8,128)(2,1)S(1)}, bf16[128,2048]{1,0:T(8,128)(2,1)S(1)}, u32[]{:S(2)}, u32[]{:S(2)}) collective-permute-start(bf16[128,2048]{1,0:T(8,128)(2,1)S(1)} %collective-permute-done.6), channel_id=1, source_target_pairs={{0,16},{16,0},{1,17},{17,1},{2,18},{18,2},{3,19},{19,3},{4,20},{20... | collective-permute-start | bytes 1572872 | tf_op jit(solution)/shard_map/ppermute | solution.py:84
  105.1 14.5 %all-to-all-done.1 = bf16[32,8,1280]{2,1,0:T(8,128)(2,1)S(1)} async-done(((bf16[32,8,1280]{2,1,0:T(8,128)(2,1)}), bf16[32,8,1280]{2,1,0:T(8,128)(2,1)S(1)}, u32[]{:S(2)}, u32[]{:S(2)}) %all-to-all-start.1) | async-done | bytes 655392 | tf_op jit(solution)/shard_map/all_to_all | solution.py:126
  119.8 0.0 copy-start.7
  119.8 0.4 fusion.64
  120.2 0.0 copy-start.5
  120.3 0.0 copy-start.4
  120.3 0.3 copy-done.8
  120.6 0.4 fusion.24
  121.0 0.4 fusion.28
  121.4 0.3 fusion.40
  121.8 0.3 fusion.8
  122.2 0.1 copy.25
  122.3 0.7 fusion.33
  122.9 8.6 %all-to-all-start.2 = ((bf16[32,8,128]{2,1,0:T(8,128)(2,1)}), bf16[32,8,128]{2,1,0:T(8,128)(2,1)S(1)}, u32[]{:S(2)}, u32[]{:S(2)}) async-start(bf16[32,8,128]{2,1,0:T(8,128)(2,1)} %fusion.33), calls=%async_computation.2 | async-start | bytes 131072 | tf_op jit(solution)/shard_map/all_to_all | solution.py:137
  131.5 0.0 collective-permute-done.9
  131.5 2.1 %collective-permute-start.11 = (bf16[128,2048]{1,0:T(8,128)(2,1)S(1)}, bf16[128,2048]{1,0:T(8,128)(2,1)S(1)}, u32[]{:S(2)}, u32[]{:S(2)}) collective-permute-start(bf16[128,2048]{1,0:T(8,128)(2,1)S(1)} %collective-permute-done.9), channel_id=1, source_target_pairs={{0,16},{16,0},{1,17},{17,1},{2,18},{18,2},{3,19},{19,3},{4,20},{20... | collective-permute-start | bytes 1572872 | tf_op jit(solution)/shard_map/ppermute | solution.py:84
  133.7 0.0 collective-permute-done.8
  133.7 12.4 %all-to-all-done.2 = bf16[32,8,128]{2,1,0:T(8,128)(2,1)S(1)} async-done(((bf16[32,8,128]{2,1,0:T(8,128)(2,1)}), bf16[32,8,128]{2,1,0:T(8,128)(2,1)S(1)}, u32[]{:S(2)}, u32[]{:S(2)}) %all-to-all-start.2) | async-done | bytes 65568 | tf_op jit(solution)/shard_map/all_to_all | solution.py:137
  146.2 0.7 broadcast_in_dim.7
  146.9 3.4 %all-to-all-start.3 = ((bf16[4,256,128]{2,1,0:T(8,128)(2,1)}), bf16[4,256,128]{2,1,0:T(8,128)(2,1)S(1)}, u32[]{:S(2)}, u32[]{:S(2)}) async-start(bf16[4,256,128]{2,1,0:T(8,128)(2,1)} %broadcast_in_dim.7), calls=%async_computation.3 | async-start | bytes 524288 | tf_op jit(solution)/shard_map/all_to_all | solution.py:69
  150.4 2.3 %collective-permute-start.10 = (bf16[128,2048]{1,0:T(8,128)(2,1)S(1)}, bf16[128,2048]{1,0:T(8,128)(2,1)S(1)}, u32[]{:S(2)}, u32[]{:S(2)}) collective-permute-start(bf16[128,2048]{1,0:T(8,128)(2,1)S(1)} %collective-permute-done.8), channel_id=1, source_target_pairs={{0,16},{16,0},{1,17},{17,1},{2,18},{18,2},{3,19},{19,3},{4,20},{20... | collective-permute-start | bytes 1572872 | tf_op jit(solution)/shard_map/ppermute | solution.py:84
  152.7 3.7 %all-to-all-done.3 = bf16[4,256,128]{2,1,0:T(8,128)(2,1)S(1)} async-done(((bf16[4,256,128]{2,1,0:T(8,128)(2,1)}), bf16[4,256,128]{2,1,0:T(8,128)(2,1)S(1)}, u32[]{:S(2)}, u32[]{:S(2)}) %all-to-all-start.3) | async-done | bytes 262176 | tf_op jit(solution)/shard_map/all_to_all | solution.py:69
  156.4 0.3 fusion.45
  156.7 0.3 fusion.44
  157.1 0.3 fusion.47
  157.4 0.3 fusion.46
  157.7 0.3 fusion.49
  158.1 0.3 fusion.48
  158.4 1.7 fusion.5
  160.2 16.0 %all_to_all.25 = bf16[4,128,512]{2,1,0:T(8,128)(2,1)S(1)} all-to-all(bf16[4,128,512]{2,1,0:T(8,128)(2,1)S(1)} %bitcast.125), channel_id=1, replica_groups=mesh['y'=4,'zh'=4,'core'=2,'x'=4,'zl'=4] {'zl'}, dimensions={0} | all-to-all | bytes 1048576 | tf_op jit(solution)/shard_map/all_to_all | solution.py:148
  176.2 0.7 reduce_sum.32
  (36 shorter events, 0.6 us)
Async XLA Ops:
  0.0 7.5 %collective-permute-start = (bf16[128,512]{1,0:T(8,128)(2,1)}, bf16[128,512]{1,0:T(8,128)(2,1)S(1)}, u32[]{:S(2)}, u32[]{:S(2)}) collective-permute-start(bf16[128,512]{1,0:T(8,128)(2,1)} %param.11), channel_id=1, source_target_pairs={{0,0},{1,32},{2,64},{3,98},{32,2},{33,33},{34,65},{35,96},{64,3},{... | collective-permute-start | bytes 393224 | tf_op jit(solution)/shard_map/ppermute | solution.py:99
  3.4 30.7 %collective-permute-start.1 = (bf16[256,512]{1,0:T(8,128)(2,1)S(1)}, bf16[256,512]{1,0:T(8,128)(2,1)S(1)}, u32[]{:S(2)}, u32[]{:S(2)}) collective-permute-start(bf16[256,512]{1,0:T(8,128)(2,1)S(1)} %constant_dynamic-update-slice_fusion), channel_id=1, source_target_pairs={{0,128},{128,0},{256,384},{384,256},{1,129},{129,1},{257,385},{385... | collective-permute-start | bytes 786440 | tf_op jit(solution)/shard_map/ppermute | solution.py:84
  35.6 29.7 %all-to-all-start = ((bf16[4,512,512]{2,1,0:T(8,128)(2,1)}), bf16[4,512,512]{2,1,0:T(8,128)(2,1)S(1)}, u32[]{:S(2)}, u32[]{:S(2)}) async-start(bf16[4,512,512]{2,1,0:T(8,128)(2,1)} %broadcast_in_dim.6), calls=%async_computation | async-start | bytes 4194304 | tf_op jit(solution)/shard_map/all_to_all | solution.py:69
  39.6 20.9 %copy-start.6 = (f32[2,128,256]{2,1,0:T(8,128)S(1)}, f32[2,128,256]{2,1,0:T(8,128)}, u32[]{:S(2)}) copy-start(f32[2,128,256]{2,1,0:T(8,128)} %param.15) | copy-start | bytes 786436
  39.6 12.8 %collective-permute-start.3 = (bf16[256,512]{1,0:T(8,128)(2,1)S(1)}, bf16[256,512]{1,0:T(8,128)(2,1)S(1)}, u32[]{:S(2)}, u32[]{:S(2)}) collective-permute-start(bf16[256,512]{1,0:T(8,128)(2,1)S(1)} %constant_dynamic-update-slice_fusion), channel_id=1, source_target_pairs={{0,384},{128,256},{256,128},{384,0},{1,385},{129,257},{257,129},{3... | collective-permute-start | bytes 786440 | tf_op jit(solution)/shard_map/ppermute | solution.py:84
  44.4 10.7 %collective-permute-start.2 = (bf16[256,512]{1,0:T(8,128)(2,1)S(1)}, bf16[256,512]{1,0:T(8,128)(2,1)S(1)}, u32[]{:S(2)}, u32[]{:S(2)}) collective-permute-start(bf16[256,512]{1,0:T(8,128)(2,1)S(1)} %collective-permute-done.1), channel_id=1, source_target_pairs={{0,384},{128,256},{256,128},{384,0},{1,385},{129,257},{257,129},{3... | collective-permute-start | bytes 786440 | tf_op jit(solution)/shard_map/ppermute | solution.py:84
  47.2 15.4 %collective-permute-start.4 = (bf16[2,256,512]{2,1,0:T(8,128)(2,1)}, bf16[2,256,512]{2,1,0:T(8,128)(2,1)}, u32[]{:S(2)}, u32[]{:S(2)}) collective-permute-start(bf16[2,256,512]{2,1,0:T(8,128)(2,1)} %pad_maximum_fusion.2), channel_id=1, source_target_pairs={{0,16},{16,0},{1,17},{17,1},{2,18},{18,2},{3,19},{19,3},{4,20},{20... | collective-permute-start | bytes 1572872 | tf_op jit(solution)/shard_map/ppermute | solution.py:84
  56.0 6.6 %collective-permute-start.5 = (bf16[2,256,512]{2,1,0:T(8,128)(2,1)}, bf16[2,256,512]{2,1,0:T(8,128)(2,1)}, u32[]{:S(2)}, u32[]{:S(2)}) collective-permute-start(bf16[2,256,512]{2,1,0:T(8,128)(2,1)} %pad_maximum_fusion.3), channel_id=1, source_target_pairs={{0,16},{16,0},{1,17},{17,1},{2,18},{18,2},{3,19},{19,3},{4,20},{20... | collective-permute-start | bytes 1572872 | tf_op jit(solution)/shard_map/ppermute | solution.py:84
  65.3 2.0 %copy-start.2 = (bf16[4,256,512]{2,1,0:T(8,128)(2,1)S(1)}, bf16[4,256,512]{2,1,0:T(8,128)(2,1)}, u32[]{:S(2)}) copy-start(bf16[4,256,512]{2,1,0:T(8,128)(2,1)} %pad_maximum_fusion) | copy-start | bytes 3145732
  69.3 50.4 %all-to-all-start.1 = ((bf16[32,8,1280]{2,1,0:T(8,128)(2,1)}), bf16[32,8,1280]{2,1,0:T(8,128)(2,1)S(1)}, u32[]{:S(2)}, u32[]{:S(2)}) async-start(bf16[32,8,1280]{2,1,0:T(8,128)(2,1)} %bitcast.13), calls=%async_computation.1 | async-start | bytes 1310720 | tf_op jit(solution)/shard_map/all_to_all | solution.py:126
  83.6 36.2 %copy-start.3 = (f32[512,256]{1,0:T(8,128)S(1)}, f32[512,256]{1,0:T(8,128)}, u32[]{:S(2)}) copy-start(f32[512,256]{1,0:T(8,128)} %constant.164) | copy-start | bytes 1572868
  86.2 34.0 %copy-start = (f32[256,128]{1,0:T(8,128)S(1)}, f32[256,128]{1,0:T(8,128)}, u32[]{:S(2)}) copy-start(f32[256,128]{1,0:T(8,128)} %constant.157.clone) | copy-start | bytes 393220
  86.2 34.0 %copy-start.1 = (f32[256,128]{1,0:T(8,128)S(1)}, f32[256,128]{1,0:T(8,128)}, u32[]{:S(2)}) copy-start(f32[256,128]{1,0:T(8,128)} %constant.156.clone) | copy-start | bytes 393220
  86.2 15.3 %collective-permute-start.6 = (bf16[128,2048]{1,0:T(8,128)(2,1)S(1)}, bf16[128,2048]{1,0:T(8,128)(2,1)S(1)}, u32[]{:S(2)}, u32[]{:S(2)}) collective-permute-start(bf16[128,2048]{1,0:T(8,128)(2,1)S(1)} %get-tuple-element.27), channel_id=1, source_target_pairs={{0,4},{4,0},{8,12},{12,8},{1,5},{5,1},{9,13},{13,9},{2,6},{6,2},{1... | collective-permute-start | bytes 1572872 | tf_op jit(solution)/shard_map/ppermute | solution.py:84
  88.6 45.1 %collective-permute-start.8 = (bf16[128,2048]{1,0:T(8,128)(2,1)}, bf16[128,2048]{1,0:T(8,128)(2,1)S(1)}, u32[]{:S(2)}, u32[]{:S(2)}) collective-permute-start(bf16[128,2048]{1,0:T(8,128)(2,1)} %get-tuple-element.25), channel_id=1, source_target_pairs={{0,12},{4,8},{8,4},{12,0},{1,13},{5,9},{9,5},{13,1},{2,14},{6,10},... | collective-permute-start | bytes 1572872 | tf_op jit(solution)/shard_map/ppermute | solution.py:84
  91.3 40.2 %collective-permute-start.9 = (bf16[128,2048]{1,0:T(8,128)(2,1)}, bf16[128,2048]{1,0:T(8,128)(2,1)S(1)}, u32[]{:S(2)}, u32[]{:S(2)}) collective-permute-start(bf16[128,2048]{1,0:T(8,128)(2,1)} %get-tuple-element.26), channel_id=1, source_target_pairs={{0,8},{4,12},{8,0},{12,4},{1,9},{5,13},{9,1},{13,5},{2,10},{6,14},... | collective-permute-start | bytes 1572872 | tf_op jit(solution)/shard_map/ppermute | solution.py:84
  101.5 32.2 %collective-permute-start.7 = (bf16[128,2048]{1,0:T(8,128)(2,1)S(1)}, bf16[128,2048]{1,0:T(8,128)(2,1)S(1)}, u32[]{:S(2)}, u32[]{:S(2)}) collective-permute-start(bf16[128,2048]{1,0:T(8,128)(2,1)S(1)} %collective-permute-done.6), channel_id=1, source_target_pairs={{0,16},{16,0},{1,17},{17,1},{2,18},{18,2},{3,19},{19,3},{4,20},{20... | collective-permute-start | bytes 1572872 | tf_op jit(solution)/shard_map/ppermute | solution.py:84
  119.7 0.9 copy-start.8
  119.8 1.2 copy-start.7
  120.2 1.2 copy-start.5
  120.3 1.5 copy-start.4
  122.9 23.2 %all-to-all-start.2 = ((bf16[32,8,128]{2,1,0:T(8,128)(2,1)}), bf16[32,8,128]{2,1,0:T(8,128)(2,1)S(1)}, u32[]{:S(2)}, u32[]{:S(2)}) async-start(bf16[32,8,128]{2,1,0:T(8,128)(2,1)} %fusion.33), calls=%async_computation.2 | async-start | bytes 131072 | tf_op jit(solution)/shard_map/all_to_all | solution.py:137
  131.5 25.2 %collective-permute-start.11 = (bf16[128,2048]{1,0:T(8,128)(2,1)S(1)}, bf16[128,2048]{1,0:T(8,128)(2,1)S(1)}, u32[]{:S(2)}, u32[]{:S(2)}) collective-permute-start(bf16[128,2048]{1,0:T(8,128)(2,1)S(1)} %collective-permute-done.9), channel_id=1, source_target_pairs={{0,16},{16,0},{1,17},{17,1},{2,18},{18,2},{3,19},{19,3},{4,20},{20... | collective-permute-start | bytes 1572872 | tf_op jit(solution)/shard_map/ppermute | solution.py:84
  146.9 9.5 %all-to-all-start.3 = ((bf16[4,256,128]{2,1,0:T(8,128)(2,1)}), bf16[4,256,128]{2,1,0:T(8,128)(2,1)S(1)}, u32[]{:S(2)}, u32[]{:S(2)}) async-start(bf16[4,256,128]{2,1,0:T(8,128)(2,1)} %broadcast_in_dim.7), calls=%async_computation.3 | async-start | bytes 524288 | tf_op jit(solution)/shard_map/all_to_all | solution.py:69
  150.4 7.0 %collective-permute-start.10 = (bf16[128,2048]{1,0:T(8,128)(2,1)S(1)}, bf16[128,2048]{1,0:T(8,128)(2,1)S(1)}, u32[]{:S(2)}, u32[]{:S(2)}) collective-permute-start(bf16[128,2048]{1,0:T(8,128)(2,1)S(1)} %collective-permute-done.8), channel_id=1, source_target_pairs={{0,16},{16,0},{1,17},{17,1},{2,18},{18,2},{3,19},{19,3},{4,20},{20... | collective-permute-start | bytes 1572872 | tf_op jit(solution)/shard_map/ppermute | solution.py:84

commit v9 on v8

--- a/solution.py
+++ b/solution.py
@@ -13,7 +13,7 @@
 N1, N2 = 32, 128
 TOTAL = N1 * N2
 GROUP = 8
-ARRIVALS = ((0, 3, 1, 2), (0, 1, 2, 3), (0, 1, 2, 3), (1, 2, 0, 3))
+ARRIVALS = ((0, 3, 1, 2), (3, 1, 0, 2), (0, 1, 2, 3), (1, 2, 0, 3))
 
 
 def reverse(count):

time: 178 us -> 177 us (level)
  no operation moved by 1% of the time
where the time goes in v9:
time: 177 us
  starting transfers between devices  69.8 us (39%)
  blocking collectives  41.8 us (24%)
  waiting for transfers between devices  39.3 us (22%)
  local copies, waits for them, and re-layouts  8.43 us (5%)
  other arithmetic  8.21 us (5%)
  matrix products  8.2 us (5%)
    ppermute x11, starting transfers between devices, exchange(): lax.ppermute(block, axis, [(i, i ^ apart) for i in range(lax.axis_size(ax...  38 us
    all_gather x1, blocking collectives, local(): near = lax.all_gather(swapped, 'zl')  25.7 us
    all_to_all x1, blocking collectives, local(): total = lax.all_to_all(total, 'zl', 0, 0)  16.1 us
    all_to_all x1, starting transfers between devices, local(): packet = lax.all_to_all(packet, SPREAD, 0, 0)  14.7 us
    all_to_all x1, waiting for transfers between devices, local(): packet = lax.all_to_all(packet, SPREAD, 0, 0)  14.3 us
    all_to_all x1, waiting for transfers between devices, local(): hidden = lax.all_to_all(hidden, SPREAD, 0, 0).reshape(256, 128)  12.4 us
    ppermute x11, waiting for transfers between devices, exchange(): lax.ppermute(block, axis, [(i, i ^ apart) for i in range(lax.axis_size(ax...  8.86 us
    all_to_all x1, starting transfers between devices, local(): hidden = lax.all_to_all(hidden, SPREAD, 0, 0).reshape(256, 128)  8.2 us
  transfers between devices with their start and end apart: 16, of which 5 were waited for; matrix products, arithmetic and copies ran while one was open for 9% of the time, Pallas kernels for 0%

profile of v9, /device:TPU:1, one launch (start us, length us, event | category | flops | bytes accessed | tf_op | source)
XLA Modules:
  0.0 176.5 jit_solution(762188720591895544)
XLA Ops:
  0.0 1.6 collective-permute-start
  1.6 0.9 constant_dynamic-update-slice_fusion.1
  2.5 0.9 constant_dynamic-update-slice_fusion
  3.4 4.0 %collective-permute-start.1 = (bf16[256,512]{1,0:T(8,128)(2,1)S(1)}, bf16[256,512]{1,0:T(8,128)(2,1)S(1)}, u32[]{:S(2)}, u32[]{:S(2)}) collective-permute-start(bf16[256,512]{1,0:T(8,128)(2,1)S(1)} %constant_dynamic-update-slice_fusion), channel_id=1, source_target_pairs={{0,128},{128,0},{256,384},{384,256},{1,129},{129,1},{257,385},{385... | collective-permute-start | bytes 786440 | tf_op jit(solution)/shard_map/ppermute | solution.py:84
  7.5 0.0 collective-permute-done
  7.5 25.7 %all-gather = bf16[512,512]{1,0:T(8,128)(2,1)S(1)} all-gather(bf16[128,512]{1,0:T(8,128)(2,1)S(1)} %maximum_select_fusion), channel_id=2, replica_groups=mesh['y'=4,'zh'=4,'core'=2,'x'=4,'zl'=4] {'zl'}, dimensions={0}, use_global_device_ids=true | all-gather | bytes 655360 | tf_op jit(solution)/shard_map/all_gather | solution.py:101
  33.3 0.0 collective-permute-done.1
  33.3 1.5 broadcast_in_dim.6
  34.9 4.0 %all-to-all-start = ((bf16[4,512,512]{2,1,0:T(8,128)(2,1)}), bf16[4,512,512]{2,1,0:T(8,128)(2,1)S(1)}, u32[]{:S(2)}, u32[]{:S(2)}) async-start(bf16[4,512,512]{2,1,0:T(8,128)(2,1)} %broadcast_in_dim.6), calls=%async_computation | async-start | bytes 4194304 | tf_op jit(solution)/shard_map/all_to_all | solution.py:69
  38.9 4.8 %collective-permute-start.3 = (bf16[256,512]{1,0:T(8,128)(2,1)S(1)}, bf16[256,512]{1,0:T(8,128)(2,1)S(1)}, u32[]{:S(2)}, u32[]{:S(2)}) collective-permute-start(bf16[256,512]{1,0:T(8,128)(2,1)S(1)} %constant_dynamic-update-slice_fusion), channel_id=1, source_target_pairs={{0,384},{128,256},{256,128},{384,0},{1,385},{129,257},{257,129},{3... | collective-permute-start | bytes 786440 | tf_op jit(solution)/shard_map/ppermute | solution.py:84
  43.6 1.9 %collective-permute-start.2 = (bf16[256,512]{1,0:T(8,128)(2,1)S(1)}, bf16[256,512]{1,0:T(8,128)(2,1)S(1)}, u32[]{:S(2)}, u32[]{:S(2)}) collective-permute-start(bf16[256,512]{1,0:T(8,128)(2,1)S(1)} %collective-permute-done.1), channel_id=1, source_target_pairs={{0,384},{128,256},{256,128},{384,0},{1,385},{129,257},{257,129},{3... | collective-permute-start | bytes 786440 | tf_op jit(solution)/shard_map/ppermute | solution.py:84
  45.6 0.9 pad_maximum_fusion.2
  46.4 5.7 %collective-permute-start.4 = (bf16[2,256,512]{2,1,0:T(8,128)(2,1)}, bf16[2,256,512]{2,1,0:T(8,128)(2,1)}, u32[]{:S(2)}, u32[]{:S(2)}) collective-permute-start(bf16[2,256,512]{2,1,0:T(8,128)(2,1)} %pad_maximum_fusion.2), channel_id=1, source_target_pairs={{0,16},{16,0},{1,17},{17,1},{2,18},{18,2},{3,19},{19,3},{4,20},{20... | collective-permute-start | bytes 1572872 | tf_op jit(solution)/shard_map/ppermute | solution.py:84
  52.1 2.7 %collective-permute-done.2 = bf16[256,512]{1,0:T(8,128)(2,1)S(1)} collective-permute-done((bf16[256,512]{1,0:T(8,128)(2,1)S(1)}, bf16[256,512]{1,0:T(8,128)(2,1)S(1)}, u32[]{:S(2)}, u32[]{:S(2)}) %collective-permute-start.2) | collective-permute-done | bytes 262176 | tf_op jit(solution)/shard_map/ppermute | solution.py:84
  54.8 0.9 pad_maximum_fusion.3
  55.6 4.5 %collective-permute-start.5 = (bf16[2,256,512]{2,1,0:T(8,128)(2,1)}, bf16[2,256,512]{2,1,0:T(8,128)(2,1)}, u32[]{:S(2)}, u32[]{:S(2)}) collective-permute-start(bf16[2,256,512]{2,1,0:T(8,128)(2,1)} %pad_maximum_fusion.3), channel_id=1, source_target_pairs={{0,16},{16,0},{1,17},{17,1},{2,18},{18,2},{3,19},{19,3},{4,20},{20... | collective-permute-start | bytes 1572872 | tf_op jit(solution)/shard_map/ppermute | solution.py:84
  60.3 0.2 fusion.19
  60.5 0.7 fusion.13
  61.2 1.1 pad_maximum_fusion
  62.3 0.0 collective-permute-done.4
  62.3 0.0 collective-permute-done.5
  62.3 1.6 dynamic-slice_select_fusion.3
  63.9 1.1 pad_maximum_fusion.1
  65.0 2.0 %convolution_bitcast_fusion = f32[512,512]{0,1:T(8,128)S(1)} fusion(bf16[4,256,512]{2,1,0:T(8,128)(2,1)} %pad_maximum_fusion.1, bf16[4,512,512]{2,1,0:T(8,128)(2,1)S(1)} %all-to-all-done), kind=kOutput, calls=%fused_computation.7 | convolution fusion | flops 536870912 | bytes 3145728 | tf_op jit(solution)/shard_map/xkc,xtk->ct/dot_general | solution.py:121
  67.0 0.7 fusion.7
  67.8 1.1 copy.21
  68.9 14.7 %all-to-all-start.1 = ((bf16[32,8,1280]{2,1,0:T(8,128)(2,1)}), bf16[32,8,1280]{2,1,0:T(8,128)(2,1)S(1)}, u32[]{:S(2)}, u32[]{:S(2)}) async-start(bf16[32,8,1280]{2,1,0:T(8,128)(2,1)} %bitcast.13), calls=%async_computation.1 | async-start | bytes 1310720 | tf_op jit(solution)/shard_map/all_to_all | solution.py:126
  83.6 0.0 copy-start.3
  83.6 2.6 %fusion.59 = (bf16[128,2048]{1,0:T(8,128)(2,1)}, bf16[128,2048]{1,0:T(8,128)(2,1)}, bf16[128,2048]{1,0:T(8,128)(2,1)S(1)}) fusion(bf16[256,8192]{1,0:T(8,128)(2,1)} %param.14, s32[]{:T(128)S(6)} %select_n.233, s32[]{:T(128)S(6)} %select_n.235, s32[]{:T(128)S(6)} %select_n.236, s32[]{:T(128)S(6)} %select_n.234), kind=kLoop, calls=%fused_computation.121 | loop fusion | bytes 3145744 | tf_op jit(solution)/shard_map/dynamic_slice | solution.py:130
  86.3 2.3 %collective-permute-start.6 = (bf16[128,2048]{1,0:T(8,128)(2,1)S(1)}, bf16[128,2048]{1,0:T(8,128)(2,1)S(1)}, u32[]{:S(2)}, u32[]{:S(2)}) collective-permute-start(bf16[128,2048]{1,0:T(8,128)(2,1)S(1)} %get-tuple-element.27), channel_id=1, source_target_pairs={{0,4},{4,0},{8,12},{12,8},{1,5},{5,1},{9,13},{13,9},{2,6},{6,2},{1... | collective-permute-start | bytes 1572872 | tf_op jit(solution)/shard_map/ppermute | solution.py:84
  88.6 3.3 %collective-permute-start.8 = (bf16[128,2048]{1,0:T(8,128)(2,1)}, bf16[128,2048]{1,0:T(8,128)(2,1)S(1)}, u32[]{:S(2)}, u32[]{:S(2)}) collective-permute-start(bf16[128,2048]{1,0:T(8,128)(2,1)} %get-tuple-element.25), channel_id=1, source_target_pairs={{0,12},{4,8},{8,4},{12,0},{1,13},{5,9},{9,5},{13,1},{2,14},{6,10},... | collective-permute-start | bytes 1572872 | tf_op jit(solution)/shard_map/ppermute | solution.py:84
  91.9 3.5 %collective-permute-start.9 = (bf16[128,2048]{1,0:T(8,128)(2,1)}, bf16[128,2048]{1,0:T(8,128)(2,1)S(1)}, u32[]{:S(2)}, u32[]{:S(2)}) collective-permute-start(bf16[128,2048]{1,0:T(8,128)(2,1)} %get-tuple-element.26), channel_id=1, source_target_pairs={{0,8},{4,12},{8,0},{12,4},{1,9},{5,13},{9,1},{13,5},{2,10},{6,14},... | collective-permute-start | bytes 1572872 | tf_op jit(solution)/shard_map/ppermute | solution.py:84
  95.4 6.2 %collective-permute-done.6 = bf16[128,2048]{1,0:T(8,128)(2,1)S(1)} collective-permute-done((bf16[128,2048]{1,0:T(8,128)(2,1)S(1)}, bf16[128,2048]{1,0:T(8,128)(2,1)S(1)}, u32[]{:S(2)}, u32[]{:S(2)}) %collective-permute-start.6) | collective-permute-done | bytes 524320 | tf_op jit(solution)/shard_map/ppermute | solution.py:84
  101.6 3.6 %collective-permute-start.7 = (bf16[128,2048]{1,0:T(8,128)(2,1)S(1)}, bf16[128,2048]{1,0:T(8,128)(2,1)S(1)}, u32[]{:S(2)}, u32[]{:S(2)}) collective-permute-start(bf16[128,2048]{1,0:T(8,128)(2,1)S(1)} %collective-permute-done.6), channel_id=1, source_target_pairs={{0,16},{16,0},{1,17},{17,1},{2,18},{18,2},{3,19},{19,3},{4,20},{20... | collective-permute-start | bytes 1572872 | tf_op jit(solution)/shard_map/ppermute | solution.py:84
  105.2 14.3 %all-to-all-done.1 = bf16[32,8,1280]{2,1,0:T(8,128)(2,1)S(1)} async-done(((bf16[32,8,1280]{2,1,0:T(8,128)(2,1)}), bf16[32,8,1280]{2,1,0:T(8,128)(2,1)S(1)}, u32[]{:S(2)}, u32[]{:S(2)}) %all-to-all-start.1) | async-done | bytes 655392 | tf_op jit(solution)/shard_map/all_to_all | solution.py:126
  119.6 0.0 copy-start.7
  119.6 0.4 fusion.64
  120.0 0.0 copy-start.5
  120.1 0.0 copy-start.4
  120.1 0.3 copy-done.8
  120.4 0.4 fusion.24
  120.8 0.4 fusion.28
  121.2 0.3 fusion.40
  121.5 0.3 fusion.8
  121.9 0.1 copy.25
  122.0 0.7 fusion.33
  122.7 8.2 %all-to-all-start.2 = ((bf16[32,8,128]{2,1,0:T(8,128)(2,1)}), bf16[32,8,128]{2,1,0:T(8,128)(2,1)S(1)}, u32[]{:S(2)}, u32[]{:S(2)}) async-start(bf16[32,8,128]{2,1,0:T(8,128)(2,1)} %fusion.33), calls=%async_computation.2 | async-start | bytes 131072 | tf_op jit(solution)/shard_map/all_to_all | solution.py:137
  130.9 0.0 collective-permute-done.9
  130.9 2.1 %collective-permute-start.11 = (bf16[128,2048]{1,0:T(8,128)(2,1)S(1)}, bf16[128,2048]{1,0:T(8,128)(2,1)S(1)}, u32[]{:S(2)}, u32[]{:S(2)}) collective-permute-start(bf16[128,2048]{1,0:T(8,128)(2,1)S(1)} %collective-permute-done.9), channel_id=1, source_target_pairs={{0,16},{16,0},{1,17},{17,1},{2,18},{18,2},{3,19},{19,3},{4,20},{20... | collective-permute-start | bytes 1572872 | tf_op jit(solution)/shard_map/ppermute | solution.py:84
  133.1 0.0 collective-permute-done.8
  133.1 12.4 %all-to-all-done.2 = bf16[32,8,128]{2,1,0:T(8,128)(2,1)S(1)} async-done(((bf16[32,8,128]{2,1,0:T(8,128)(2,1)}), bf16[32,8,128]{2,1,0:T(8,128)(2,1)S(1)}, u32[]{:S(2)}, u32[]{:S(2)}) %all-to-all-start.2) | async-done | bytes 65568 | tf_op jit(solution)/shard_map/all_to_all | solution.py:137
  145.6 0.7 broadcast_in_dim.7
  146.3 3.4 %all-to-all-start.3 = ((bf16[4,256,128]{2,1,0:T(8,128)(2,1)}), bf16[4,256,128]{2,1,0:T(8,128)(2,1)S(1)}, u32[]{:S(2)}, u32[]{:S(2)}) async-start(bf16[4,256,128]{2,1,0:T(8,128)(2,1)} %broadcast_in_dim.7), calls=%async_computation.3 | async-start | bytes 524288 | tf_op jit(solution)/shard_map/all_to_all | solution.py:69
  149.8 2.3 %collective-permute-start.10 = (bf16[128,2048]{1,0:T(8,128)(2,1)S(1)}, bf16[128,2048]{1,0:T(8,128)(2,1)S(1)}, u32[]{:S(2)}, u32[]{:S(2)}) collective-permute-start(bf16[128,2048]{1,0:T(8,128)(2,1)S(1)} %collective-permute-done.8), channel_id=1, source_target_pairs={{0,16},{16,0},{1,17},{17,1},{2,18},{18,2},{3,19},{19,3},{4,20},{20... | collective-permute-start | bytes 1572872 | tf_op jit(solution)/shard_map/ppermute | solution.py:84
  152.1 3.7 %all-to-all-done.3 = bf16[4,256,128]{2,1,0:T(8,128)(2,1)S(1)} async-done(((bf16[4,256,128]{2,1,0:T(8,128)(2,1)}), bf16[4,256,128]{2,1,0:T(8,128)(2,1)S(1)}, u32[]{:S(2)}, u32[]{:S(2)}) %all-to-all-start.3) | async-done | bytes 262176 | tf_op jit(solution)/shard_map/all_to_all | solution.py:69
  155.8 0.3 fusion.45
  156.1 0.3 fusion.44
  156.5 0.3 fusion.47
  156.8 0.3 fusion.46
  157.2 0.3 fusion.49
  157.5 0.3 fusion.48
  157.8 1.7 fusion.5
  159.6 16.1 %all_to_all.25 = bf16[4,128,512]{2,1,0:T(8,128)(2,1)S(1)} all-to-all(bf16[4,128,512]{2,1,0:T(8,128)(2,1)S(1)} %bitcast.125), channel_id=1, replica_groups=mesh['y'=4,'zh'=4,'core'=2,'x'=4,'zl'=4] {'zl'}, dimensions={0} | all-to-all | bytes 1048576 | tf_op jit(solution)/shard_map/all_to_all | solution.py:148
  175.8 0.7 reduce_sum.32
  (36 shorter events, 0.6 us)
Async XLA Ops:
  0.0 7.5 %collective-permute-start = (bf16[128,512]{1,0:T(8,128)(2,1)}, bf16[128,512]{1,0:T(8,128)(2,1)S(1)}, u32[]{:S(2)}, u32[]{:S(2)}) collective-permute-start(bf16[128,512]{1,0:T(8,128)(2,1)} %param.11), channel_id=1, source_target_pairs={{0,0},{1,34},{2,64},{3,98},{32,2},{33,33},{34,65},{35,96},{64,3},{... | collective-permute-start | bytes 393224 | tf_op jit(solution)/shard_map/ppermute | solution.py:99
  3.4 29.9 %collective-permute-start.1 = (bf16[256,512]{1,0:T(8,128)(2,1)S(1)}, bf16[256,512]{1,0:T(8,128)(2,1)S(1)}, u32[]{:S(2)}, u32[]{:S(2)}) collective-permute-start(bf16[256,512]{1,0:T(8,128)(2,1)S(1)} %constant_dynamic-update-slice_fusion), channel_id=1, source_target_pairs={{0,128},{128,0},{256,384},{384,256},{1,129},{129,1},{257,385},{385... | collective-permute-start | bytes 786440 | tf_op jit(solution)/shard_map/ppermute | solution.py:84
  34.9 30.1 %all-to-all-start = ((bf16[4,512,512]{2,1,0:T(8,128)(2,1)}), bf16[4,512,512]{2,1,0:T(8,128)(2,1)S(1)}, u32[]{:S(2)}, u32[]{:S(2)}) async-start(bf16[4,512,512]{2,1,0:T(8,128)(2,1)} %broadcast_in_dim.6), calls=%async_computation | async-start | bytes 4194304 | tf_op jit(solution)/shard_map/all_to_all | solution.py:69
  38.9 21.3 %copy-start.6 = (f32[2,128,256]{2,1,0:T(8,128)S(1)}, f32[2,128,256]{2,1,0:T(8,128)}, u32[]{:S(2)}) copy-start(f32[2,128,256]{2,1,0:T(8,128)} %param.15) | copy-start | bytes 786436
  38.9 13.2 %collective-permute-start.3 = (bf16[256,512]{1,0:T(8,128)(2,1)S(1)}, bf16[256,512]{1,0:T(8,128)(2,1)S(1)}, u32[]{:S(2)}, u32[]{:S(2)}) collective-permute-start(bf16[256,512]{1,0:T(8,128)(2,1)S(1)} %constant_dynamic-update-slice_fusion), channel_id=1, source_target_pairs={{0,384},{128,256},{256,128},{384,0},{1,385},{129,257},{257,129},{3... | collective-permute-start | bytes 786440 | tf_op jit(solution)/shard_map/ppermute | solution.py:84
  43.6 11.1 %collective-permute-start.2 = (bf16[256,512]{1,0:T(8,128)(2,1)S(1)}, bf16[256,512]{1,0:T(8,128)(2,1)S(1)}, u32[]{:S(2)}, u32[]{:S(2)}) collective-permute-start(bf16[256,512]{1,0:T(8,128)(2,1)S(1)} %collective-permute-done.1), channel_id=1, source_target_pairs={{0,384},{128,256},{256,128},{384,0},{1,385},{129,257},{257,129},{3... | collective-permute-start | bytes 786440 | tf_op jit(solution)/shard_map/ppermute | solution.py:84
  46.4 15.8 %collective-permute-start.4 = (bf16[2,256,512]{2,1,0:T(8,128)(2,1)}, bf16[2,256,512]{2,1,0:T(8,128)(2,1)}, u32[]{:S(2)}, u32[]{:S(2)}) collective-permute-start(bf16[2,256,512]{2,1,0:T(8,128)(2,1)} %pad_maximum_fusion.2), channel_id=1, source_target_pairs={{0,16},{16,0},{1,17},{17,1},{2,18},{18,2},{3,19},{19,3},{4,20},{20... | collective-permute-start | bytes 1572872 | tf_op jit(solution)/shard_map/ppermute | solution.py:84
  55.6 6.6 %collective-permute-start.5 = (bf16[2,256,512]{2,1,0:T(8,128)(2,1)}, bf16[2,256,512]{2,1,0:T(8,128)(2,1)}, u32[]{:S(2)}, u32[]{:S(2)}) collective-permute-start(bf16[2,256,512]{2,1,0:T(8,128)(2,1)} %pad_maximum_fusion.3), channel_id=1, source_target_pairs={{0,16},{16,0},{1,17},{17,1},{2,18},{18,2},{3,19},{19,3},{4,20},{20... | collective-permute-start | bytes 1572872 | tf_op jit(solution)/shard_map/ppermute | solution.py:84
  65.0 2.0 %copy-start.2 = (bf16[4,256,512]{2,1,0:T(8,128)(2,1)S(1)}, bf16[4,256,512]{2,1,0:T(8,128)(2,1)}, u32[]{:S(2)}) copy-start(bf16[4,256,512]{2,1,0:T(8,128)(2,1)} %pad_maximum_fusion) | copy-start | bytes 3145732
  68.9 50.6 %all-to-all-start.1 = ((bf16[32,8,1280]{2,1,0:T(8,128)(2,1)}), bf16[32,8,1280]{2,1,0:T(8,128)(2,1)S(1)}, u32[]{:S(2)}, u32[]{:S(2)}) async-start(bf16[32,8,1280]{2,1,0:T(8,128)(2,1)} %bitcast.13), calls=%async_computation.1 | async-start | bytes 1310720 | tf_op jit(solution)/shard_map/all_to_all | solution.py:126
  83.6 36.0 %copy-start.3 = (f32[512,256]{1,0:T(8,128)S(1)}, f32[512,256]{1,0:T(8,128)}, u32[]{:S(2)}) copy-start(f32[512,256]{1,0:T(8,128)} %constant.164) | copy-start | bytes 1572868
  86.3 33.7 %copy-start = (f32[256,128]{1,0:T(8,128)S(1)}, f32[256,128]{1,0:T(8,128)}, u32[]{:S(2)}) copy-start(f32[256,128]{1,0:T(8,128)} %constant.157.clone) | copy-start | bytes 393220
  86.3 33.7 %copy-start.1 = (f32[256,128]{1,0:T(8,128)S(1)}, f32[256,128]{1,0:T(8,128)}, u32[]{:S(2)}) copy-start(f32[256,128]{1,0:T(8,128)} %constant.156.clone) | copy-start | bytes 393220
  86.3 15.3 %collective-permute-start.6 = (bf16[128,2048]{1,0:T(8,128)(2,1)S(1)}, bf16[128,2048]{1,0:T(8,128)(2,1)S(1)}, u32[]{:S(2)}, u32[]{:S(2)}) collective-permute-start(bf16[128,2048]{1,0:T(8,128)(2,1)S(1)} %get-tuple-element.27), channel_id=1, source_target_pairs={{0,4},{4,0},{8,12},{12,8},{1,5},{5,1},{9,13},{13,9},{2,6},{6,2},{1... | collective-permute-start | bytes 1572872 | tf_op jit(solution)/shard_map/ppermute | solution.py:84
  88.6 44.5 %collective-permute-start.8 = (bf16[128,2048]{1,0:T(8,128)(2,1)}, bf16[128,2048]{1,0:T(8,128)(2,1)S(1)}, u32[]{:S(2)}, u32[]{:S(2)}) collective-permute-start(bf16[128,2048]{1,0:T(8,128)(2,1)} %get-tuple-element.25), channel_id=1, source_target_pairs={{0,12},{4,8},{8,4},{12,0},{1,13},{5,9},{9,5},{13,1},{2,14},{6,10},... | collective-permute-start | bytes 1572872 | tf_op jit(solution)/shard_map/ppermute | solution.py:84
  91.9 39.0 %collective-permute-start.9 = (bf16[128,2048]{1,0:T(8,128)(2,1)}, bf16[128,2048]{1,0:T(8,128)(2,1)S(1)}, u32[]{:S(2)}, u32[]{:S(2)}) collective-permute-start(bf16[128,2048]{1,0:T(8,128)(2,1)} %get-tuple-element.26), channel_id=1, source_target_pairs={{0,8},{4,12},{8,0},{12,4},{1,9},{5,13},{9,1},{13,5},{2,10},{6,14},... | collective-permute-start | bytes 1572872 | tf_op jit(solution)/shard_map/ppermute | solution.py:84
  101.6 31.5 %collective-permute-start.7 = (bf16[128,2048]{1,0:T(8,128)(2,1)S(1)}, bf16[128,2048]{1,0:T(8,128)(2,1)S(1)}, u32[]{:S(2)}, u32[]{:S(2)}) collective-permute-start(bf16[128,2048]{1,0:T(8,128)(2,1)S(1)} %collective-permute-done.6), channel_id=1, source_target_pairs={{0,16},{16,0},{1,17},{17,1},{2,18},{18,2},{3,19},{19,3},{4,20},{20... | collective-permute-start | bytes 1572872 | tf_op jit(solution)/shard_map/ppermute | solution.py:84
  119.5 0.9 copy-start.8
  119.6 1.2 copy-start.7
  120.0 1.2 copy-start.5
  120.1 1.5 copy-start.4
  122.7 22.8 %all-to-all-start.2 = ((bf16[32,8,128]{2,1,0:T(8,128)(2,1)}), bf16[32,8,128]{2,1,0:T(8,128)(2,1)S(1)}, u32[]{:S(2)}, u32[]{:S(2)}) async-start(bf16[32,8,128]{2,1,0:T(8,128)(2,1)} %fusion.33), calls=%async_computation.2 | async-start | bytes 131072 | tf_op jit(solution)/shard_map/all_to_all | solution.py:137
  130.9 25.2 %collective-permute-start.11 = (bf16[128,2048]{1,0:T(8,128)(2,1)S(1)}, bf16[128,2048]{1,0:T(8,128)(2,1)S(1)}, u32[]{:S(2)}, u32[]{:S(2)}) collective-permute-start(bf16[128,2048]{1,0:T(8,128)(2,1)S(1)} %collective-permute-done.9), channel_id=1, source_target_pairs={{0,16},{16,0},{1,17},{17,1},{2,18},{18,2},{3,19},{19,3},{4,20},{20... | collective-permute-start | bytes 1572872 | tf_op jit(solution)/shard_map/ppermute | solution.py:84
  146.3 9.5 %all-to-all-start.3 = ((bf16[4,256,128]{2,1,0:T(8,128)(2,1)}), bf16[4,256,128]{2,1,0:T(8,128)(2,1)S(1)}, u32[]{:S(2)}, u32[]{:S(2)}) async-start(bf16[4,256,128]{2,1,0:T(8,128)(2,1)} %broadcast_in_dim.7), calls=%async_computation.3 | async-start | bytes 524288 | tf_op jit(solution)/shard_map/all_to_all | solution.py:69
  149.8 7.1 %collective-permute-start.10 = (bf16[128,2048]{1,0:T(8,128)(2,1)S(1)}, bf16[128,2048]{1,0:T(8,128)(2,1)S(1)}, u32[]{:S(2)}, u32[]{:S(2)}) collective-permute-start(bf16[128,2048]{1,0:T(8,128)(2,1)S(1)} %collective-permute-done.8), channel_id=1, source_target_pairs={{0,16},{16,0},{1,17},{17,1},{2,18},{18,2},{3,19},{19,3},{4,20},{20... | collective-permute-start | bytes 1572872 | tf_op jit(solution)/shard_map/ppermute | solution.py:84
